TPU v7x, 32 devices: a whole 2x2x4 slice. The times are simulated.
32 devices in a mesh: dp: 8 (over y, x, core), tensor: 4 (over z).
Axes of the slice: x: 2, y: 2, z: 4, core: 2. Of those that a mesh axis runs over, the one named last changes fastest.
Arguments:
- inputs: bfloat16 [2048, 4096], P('dp', 'tensor'), may hold values from -6 to 6
- first_factor: bfloat16 [256, 16, 1024], P(None, 'tensor'), may hold values from -0.375 to 0.375
- second_factor: bfloat16 [1024, 16, 1024], P(None, 'tensor'), may hold values from -0.1875 to 0.1875
- cotangent: bfloat16 [16384, 2048], P('tensor', 'dp'), may hold values from -6 to 6
Outputs:
- input_grad: bfloat16 [2048, 4096], P('dp', 'tensor')
- first_grad: float32 [256, 16, 1024], P('dp', 'tensor')
All inputs are finite; a program needn't handle non-finite values.
Results may differ from a plain program's by a relative error of at most 0.0063.
Values may be sent and summed in bfloat16 or wider, within the bound.
No kernel may reach another device: no remote copies, remote signals or barrier semaphores. Data moves between devices by JAX's collectives and lax.ppermute only.
A program may use at most 64 MiB of HBM per device.

v0:
```python
import jax
import jax.numpy as jnp
from jax import lax
from jax.sharding import PartitionSpec as P


def gelu_backward(pre_act, upstream):
    value, pullback = jax.vjp(lambda v: jax.nn.gelu(v, approximate=True), pre_act)
    return pullback(upstream)[0]


def body(inputs, first_factor, second_factor, cotangent):
    tokens_here = inputs.shape[0]
    in_width = first_factor.shape[0]
    local = first_factor.shape[1]
    out_width = first_factor.shape[2]
    blocks = local * lax.axis_size("tensor")
    group = out_width // blocks
    block_grouped = inputs.reshape(tokens_here, local, in_width)
    split_first = first_factor.reshape(in_width, local, blocks, group)
    outgoing = jnp.einsum(
        "tlk,kljg->jlgt", block_grouped, split_first, preferred_element_type=jnp.float32
    ).astype(jnp.bfloat16)
    arrived = lax.all_to_all(outgoing, "tensor", split_axis=0, concat_axis=1, tiled=True)
    mixed = arrived.reshape(local, out_width, tokens_here)
    pre_act = jnp.einsum("lmt,mln->lnt", mixed, second_factor, preferred_element_type=jnp.float32)
    upstream = cotangent.reshape(local, out_width, tokens_here).astype(jnp.float32)
    pre_grad = gelu_backward(pre_act, upstream).astype(jnp.bfloat16)
    mixed_grad = jnp.einsum(
        "lnt,mln->lmt", pre_grad, second_factor, preferred_element_type=jnp.float32
    ).astype(jnp.bfloat16)
    returned = lax.all_to_all(
        mixed_grad.reshape(local, blocks, group, tokens_here),
        "tensor",
        split_axis=1,
        concat_axis=0,
        tiled=True,
    )
    input_grad = jnp.einsum(
        "jlgt,kljg->tlk", returned, split_first, preferred_element_type=jnp.float32
    )
    input_grad = input_grad.reshape(tokens_here, local * in_width).astype(jnp.bfloat16)
    factor = (tokens_here * lax.axis_size("dp")) ** (-0.5)
    first_term = jnp.einsum(
        "tlk,jlgt->kljg", block_grouped, returned, preferred_element_type=jnp.float32
    ).reshape(in_width, local, out_width)
    first_sum = lax.psum_scatter(first_term, "dp", scatter_dimension=0, tiled=True)
    return (input_grad, first_sum * factor)


def solution(mesh):
    return jax.shard_map(
        body,
        mesh=mesh,
        in_specs=(
            P("dp", "tensor"),
            P(None, "tensor", None),
            P(None, "tensor", None),
            P("tensor", "dp"),
        ),
        out_specs=(P("dp", "tensor"), P("dp", "tensor", None)),
        check_vma=False,
    )
```

profile of v0, /device:TPU:0, one launch (start us, length us, event | category | flops | bytes accessed | tf_op | source)
XLA Modules:
  0.0 245.3 jit_solution(18341952113642233045)
XLA Ops:
  7.2 1.4 reshape.26
  8.6 3.0 %copy.43 = bf16[256,4,1024]{0,2,1:T(8,128)(2,1)S(1)} copy(bf16[256,4,1024]{2,1,0:T(4,128)(2,1)} %param.5) | data formatting | bytes 4194304 | tf_op args[1]
  11.6 0.7 convert_bitcast_fusion.1
  12.4 1.5 copy.45
  13.8 6.3 %all-to-all-start = ((bf16[16,4,64,256]{3,2,1,0:T(8,128)(2,1)}), bf16[16,4,64,256]{3,2,1,0:T(8,128)(2,1)}, u32[]{:S(2)}, u32[]{:S(2)}) async-start(bf16[16,4,64,256]{3,2,1,0:T(8,128)(2,1)} %copy.45), calls=%async_computation | async-start | bytes 4194304 | tf_op jit(solution)/shard_map/all_to_all | solution.py:24
  20.1 0.0 all-reduce.3.cloned.1.call-start
  20.1 4.2 %copy.49 = f32[4,1024,256]{1,2,0:T(8,128)} copy(bf16[4,1024,256]{2,1,0:T(8,128)(2,1)} %bitcast.59) | data formatting | bytes 6291456 | tf_op jit(solution)/shard_map/convert_element_type | solution.py:27
  24.3 44.1 %all-to-all-done = bf16[16,4,64,256]{3,2,1,0:T(8,128)(2,1)} async-done(((bf16[16,4,64,256]{3,2,1,0:T(8,128)(2,1)}), bf16[16,4,64,256]{3,2,1,0:T(8,128)(2,1)}, u32[]{:S(2)}, u32[]{:S(2)}) %all-to-all-start) | async-done | bytes 2097184 | tf_op jit(solution)/shard_map/all_to_all | solution.py:24
  68.4 3.2 %copy.46 = bf16[4,4,4,64,256]{4,3,2,1,0:T(8,128)(2,1)} copy(bf16[4,4,4,64,256]{4,3,2,0,1:T(8,128)(2,1)} %bitcast.5) | data formatting | bytes 4194304 | tf_op jit(solution)/shard_map/all_to_all | solution.py:24
  71.6 20.2 %convert_bitcast_fusion = bf16[4,1024,256]{1,2,0:T(8,128)(2,1)} fusion(bf16[1024,4,1024]{2,1,0:T(4,128)(2,1)} %param.6, f32[4,1024,256]{1,2,0:T(8,128)} %copy.49, bf16[4,1024,256]{2,1,0:T(8,128)(2,1)} %bitcast.61), kind=kOutput, calls=%fused_computation.16 | convolution fusion | flops 4316987392 | bytes 16777216 | tf_op jit(solution)/shard_map/lnt,mln->lmt/dot_general | solution.py:29
  91.8 3.9 %copy.52 = bf16[4,1024,256]{2,1,0:T(8,128)(2,1)} copy(bf16[4,1024,256]{1,2,0:T(8,128)(2,1)} %convert_bitcast_fusion) | data formatting | bytes 4194304 | tf_op jit(solution)/shard_map/convert_element_type | solution.py:31
  95.8 1.7 copy.53
  97.5 50.2 %all_to_all.33 = bf16[4,16,64,256]{3,2,0,1:T(8,128)(2,1)S(1)} all-to-all(bf16[4,16,64,256]{3,2,0,1:T(8,128)(2,1)S(1)} %copy.53), channel_id=1, replica_groups=mesh['dp'=8,'tensor'=4] {'tensor'}, dimensions={1} | all-to-all | bytes 4194304 | tf_op jit(solution)/shard_map/all_to_all | solution.py:32
  147.7 0.2 copy.54
  147.9 0.0 copy-start
  147.9 2.7 %fusion.31 = f32[4,16,64,256]{3,2,1,0:T(8,128)} fusion(bf16[16,4,64,256]{3,2,0,1:T(8,128)(2,1)S(1)} %bitcast.53, bf16[256,4,256,1]{2,1,0,3:T(4,128)(2,1)S(1)} %bitcast.56), kind=kOutput, calls=%fused_computation.27 | convolution fusion | flops 536870912 | bytes 6815744 | tf_op jit(solution)/shard_map/tlk,jlgt->kljg/dot_general | solution.py:44
  150.6 0.0 copy-done
  150.6 5.6 %copy.56 = f32[256,4,1024]{2,1,0:T(4,128)} copy(f32[256,4,1024]{0,2,1:T(8,128)} %bitcast.50) | data formatting | bytes 8388608 | tf_op jit(solution)/shard_map/reshape | solution.py:46
  156.2 0.0 copy-start.1
  156.2 0.0 all-reduce.3.cloned.1.call-update
  156.2 0.6 copy-done.1
  156.9 0.6 dynamic-slice
  158.1 2.4 fusion.30
  160.5 1.0 copy.57
  161.5 74.9 %all-reduce.3.cloned.1.call-done = f32[256,4,1024]{2,1,0:T(4,128)} async-done(((f32[256,4,1024]{2,1,0:T(4,128)}), f32[256,4,1024]{2,1,0:T(4,128)}) %all-reduce.3.cloned.1.call-update) | async-done | bytes 4194320
  236.5 2.0 dynamic-slice_multiply_fusion
Async XLA Ops:
  13.8 54.6 %all-to-all-start = ((bf16[16,4,64,256]{3,2,1,0:T(8,128)(2,1)}), bf16[16,4,64,256]{3,2,1,0:T(8,128)(2,1)}, u32[]{:S(2)}, u32[]{:S(2)}) async-start(bf16[16,4,64,256]{3,2,1,0:T(8,128)(2,1)} %copy.45), calls=%async_computation | async-start | bytes 4194304 | tf_op jit(solution)/shard_map/all_to_all | solution.py:24
  20.1 216.3 %all-reduce.3.cloned.1.call-start = ((), (), s32[]{:S(2)}) async-start(), calls=%async_computation.2 | async-start | bytes 8388608
  147.9 2.7 %copy-start = (bf16[4,4,4,64,256]{4,3,0,1,2:T(8,128)(2,1)}, bf16[4,4,4,64,256]{4,3,0,1,2:T(8,128)(2,1)S(1)}, u32[]{:S(2)}) copy-start(bf16[4,4,4,64,256]{4,3,0,1,2:T(8,128)(2,1)S(1)} %copy.54) | copy-start | bytes 6291460
  156.2 0.7 copy-start.1
Sparse Core Ops, SparseCore 0:
  156.3 80.0 all-reduce.2
where the time goes:
time: 246 us; the launch traced here: 245 us
  waiting for transfers between devices  119 us (48%)
  blocking collectives  50.2 us (20%)
  local copies, waits for them, and re-layouts  27 us (11%)
  matrix products  26.1 us (11%)
  between operations  14.7 us (6%)
  starting transfers between devices  6.31 us (3%)
    unnamed x2, waiting for transfers between devices  74.9 us
    all_to_all x1, blocking collectives, body(): lax.all_to_all(mixed_grad.reshape(local, blocks, group, tokens_here), 'te...  50.2 us
    all_to_all x1, waiting for transfers between devices, body(): lax.all_to_all(outgoing, 'tensor', split_axis=0, concat_axis=1, tiled=True)  44.1 us
    dot_general x1, matrix products, body(): jnp.einsum('lnt,mln->lmt', pre_grad, second_factor, preferred_element_typ...  20.2 us
    all_to_all x1, starting transfers between devices, body(): lax.all_to_all(outgoing, 'tensor', split_axis=0, concat_axis=1, tiled=True)  6.31 us
    reshape x1, local copies, waits for them, and re-layouts, body(): first_term = jnp.einsum('tlk,jlgt->kljg', block_grouped, returned, prefer...  5.57 us
    unnamed x7, local copies, waits for them, and re-layouts  5.21 us
  transfers between devices with their start and end apart: 2, of which 2 were waited for; matrix products, arithmetic and copies ran while one was open for 3% of the time, Pallas kernels for 0%

commit v1 on v0

v1 whole, which is shorter than its diff:
```python
import functools

import jax
import jax.numpy as jnp
from jax import lax
from jax.experimental import pallas as pl
from jax.experimental.pallas import tpu as pltpu
from jax.sharding import PartitionSpec as P

BF16 = jnp.bfloat16
F32 = jnp.float32


def dot(a, b, dims):
    return lax.dot_general(a, b, (dims, ((), ())), preferred_element_type=F32)


def gelu_slope(v):
    c = 0.7978845608028654
    v2 = v * v
    t = jnp.tanh(v * (c + (c * 0.044715) * v2))
    return 0.5 + 0.5 * t + (0.5 * v) * (1.0 - t * t) * (c + (3.0 * c * 0.044715) * v2)


VMEM = pl.BlockSpec(memory_space=pltpu.VMEM)
SMALL = pltpu.CompilerParams(vmem_limit_bytes=16 << 20)
FREE = pl.CostEstimate(flops=0, bytes_accessed=0, transcendentals=0)
SMEM = pl.BlockSpec(memory_space=pltpu.SMEM)


def on_chip(kernel, name, at, operands, shapes, stored=(), limit=16 << 20, **more):
    held = [pltpu.with_memory_space_constraint(a, pltpu.VMEM) for a in operands]
    out = [pltpu.VMEM(shape, dtype) for shape, dtype in shapes]
    return pl.pallas_call(
        kernel,
        in_specs=[SMEM] + [VMEM] * len(held) + [pl.BlockSpec(memory_space=pl.ANY)] * len(stored),
        out_specs=[VMEM] * len(out),
        out_shape=out,
        compiler_params=pltpu.CompilerParams(vmem_limit_bytes=limit),
        cost_estimate=FREE,
        name=name,
        **more,
    )(at, *held, *stored)


def cut_kernel(nz, local, cols, kd, at_ref, f_ref, *outs):
    for r in range(1, nz):
        col = pl.multiple_of(lax.rem(at_ref[0] + nz - r, nz) * cols, cols)
        for b in range(local):
            outs[r - 1][b] = f_ref[:, b, pl.ds(col, cols)]


def cut(at, first_factor, nz, nd):
    width, local, out_width = first_factor.shape
    kd, cols = width // nd, out_width // nz
    return pl.pallas_call(
        functools.partial(cut_kernel, nz, local, cols, kd),
        grid_spec=pltpu.PrefetchScalarGridSpec(
            num_scalar_prefetch=1,
            grid=(1,),
            in_specs=[pl.BlockSpec((kd, local, out_width), lambda i, at_ref: (at_ref[1], 0, 0))],
            out_specs=[pl.BlockSpec((local, kd, cols), lambda i, at_ref: (0, 0, 0))] * (nz - 1),
        ),
        out_shape=[pltpu.VMEM((local, kd, cols), BF16)] * (nz - 1),
        compiler_params=SMALL,
        cost_estimate=FREE,
        name="cut",
    )(at, first_factor)


def own_kernel(local, at_ref, f_ref, later_ref, out):
    for b in range(local):
        out[b] = f_ref[:, b, :]


def own_columns(at, first_factor, earlier, nz):
    width, local, out_width = first_factor.shape
    cols = out_width // nz
    return pl.pallas_call(
        functools.partial(own_kernel, local),
        grid_spec=pltpu.PrefetchScalarGridSpec(
            num_scalar_prefetch=1,
            grid=(1,),
            in_specs=[pl.BlockSpec((width, local, cols), lambda i, at_ref: (0, 0, at_ref[0])), VMEM],
            out_specs=pl.BlockSpec((local, width, cols), lambda i, at_ref: (0, 0, 0)),
        ),
        out_shape=pltpu.VMEM((local, width, cols), BF16),
        compiler_params=SMALL,
        cost_estimate=FREE,
        name="own_columns",
    )(at, first_factor, pltpu.with_memory_space_constraint(earlier, pltpu.VMEM))


def turn_kernel(x_ref, later_ref, out):
    out[...] = x_ref[...].T


def turned(cotangent, earlier, tile=512):
    units, tokens = cotangent.shape
    return pl.pallas_call(
        turn_kernel,
        grid=(units // tile,),
        in_specs=[pl.BlockSpec((tile, tokens), lambda i: (i, 0)), VMEM],
        out_specs=pl.BlockSpec((tokens, tile), lambda i: (0, i)),
        out_shape=pltpu.VMEM((tokens, units), BF16),
        compiler_params=SMALL,
        cost_estimate=FREE,
        name="turned",
    )(cotangent, pltpu.with_memory_space_constraint(earlier, pltpu.VMEM))


def assemble_kernel(local, kd, orders, at_ref, own_ref, *refs):
    out = refs[-1]
    out[:local] = own_ref[...]
    core = jnp.bitwise_and(at_ref[1], 1)
    at = local
    for i, order in enumerate(orders):
        mine, other = refs[2 * i], refs[2 * i + 1]
        bits = len(order) + 1
        blocks = mine.shape[bits - 1]
        for d in range(1 << bits):
            place = tuple((d >> bit) & 1 for bit in reversed(order))
            for b in range(blocks):
                rows = jnp.where(core == (d & 1), mine[place + (b,)], other[place + (b,)])
                out[at + b, d * kd : (d + 1) * kd, :] = rows
        at += blocks


def layer_kernel(nz, local, width, cols, chunk, at_ref, *refs):
    x_refs = refs[:nz]
    f_ref, cot_ref = refs[nz : nz + 2]
    s_hbm, *dx_refs, og_ref, mixed, back, s_ref, arrived = refs[-(nz + 6) :]
    fetch = [pltpu.make_async_copy(s_hbm.at[j], s_ref.at[j], arrived.at[j]) for j in range(local)]
    for copy in fetch:
        copy.start()
    z = at_ref[0]
    group = cols // local
    rows, out_width = dx_refs[0].shape[0], mixed.shape[2]
    here = slice(chunk * rows, (chunk + 1) * rows)
    low = lax.broadcasted_iota(jnp.int32, (rows, 2 * group), 1) < group

    for r in range(nz):
        for b in range(0, local, 2):
            one = dot(x_refs[r][:, b * width : (b + 1) * width], f_ref[r * local + b], ((1,), (0,)))
            two = dot(x_refs[r][:, (b + 1) * width : (b + 2) * width], f_ref[r * local + b + 1], ((1,), (0,)))
            at = (r * local + b) * group
            for h in range(local // 2):
                p = one[:, 2 * h * group : (2 * h + 2) * group]
                q = two[:, 2 * h * group : (2 * h + 2) * group]
                mixed[2 * h, :, at : at + 2 * group] = jnp.where(low, p, pltpu.roll(q, group, 1)).astype(BF16)
                mixed[2 * h + 1, :, at : at + 2 * group] = jnp.where(low, pltpu.roll(p, group, 1), q).astype(BF16)

    planes = [lax.rem(z + r, nz) for r in range(nz)]

    for j in range(local):
        fetch[j].wait()
        weight = jnp.concatenate(
            [s_ref[j, pl.ds(pl.multiple_of(p * cols, cols), cols), :] for p in planes], axis=0
        )
        pre_act = dot(mixed[j], weight, ((1,), (0,)))
        upstream = cot_ref[here, j * out_width : (j + 1) * out_width]
        pre_grad = (upstream.astype(F32) * gelu_slope(pre_act)).astype(BF16)
        back[j] = dot(pre_grad, weight, ((1,), (1,)))

    for r in range(nz):
        for b in range(0, local, 2):
            at = (r * local + b) * group
            one, two = [], []
            for h in range(local // 2):
                p = back[2 * h, :, at : at + 2 * group]
                q = back[2 * h + 1, :, at : at + 2 * group]
                one.append(jnp.where(low, p, pltpu.roll(q, group, 1)).astype(BF16))
                two.append(jnp.where(low, pltpu.roll(p, group, 1), q).astype(BF16))
            for i, part in ((b, one), (b + 1, two)):
                og = jnp.concatenate(part, axis=1)
                og_ref[r, :, i * cols : (i + 1) * cols] = og
                dx_refs[r][:, i * width : (i + 1) * width] = dot(
                    og, f_ref[r * local + i], ((1,), (1,))
                ).astype(dx_refs[r].dtype)


def layer(at, xs, first, second, cot, later, chunk, rows, nz, local, width, cols):
    out_width = second.shape[2]
    piece = (rows, local * width)
    return on_chip(
        functools.partial(layer_kernel, nz, local, width, cols, chunk),
        "layer",
        at,
        list(xs) + [first, cot, *later],
        [(piece, F32)] + [(piece, BF16)] * (nz - 1) + [((nz, rows, local * cols), BF16)],
        scratch_shapes=[
            pltpu.VMEM((local, rows, out_width), BF16),
            pltpu.VMEM((local, rows, out_width), F32),
            pltpu.VMEM(second.shape, BF16),
            pltpu.SemaphoreType.DMA((local,)),
        ],
        stored=[second],
        limit=28 << 20,
    )


def grad_kernel(nz, parts, local, width, cols, nd, at_ref, *refs):
    x_refs, og_refs = refs[: parts * nz], refs[parts * nz : parts * (nz + 1)]
    give, keep = refs[-2:]
    me = at_ref[1]
    kd = width // nd
    for r in range(nz):
        for b in range(local):
            x = jnp.concatenate(
                [x_refs[c * nz + r][:, b * width : (b + 1) * width] for c in range(parts)], axis=0
            )
            og = jnp.concatenate([og_refs[c][r, :, b * cols : (b + 1) * cols] for c in range(parts)], axis=0)
            term = dot(x, og, ((0,), (0,))).astype(BF16)
            for d in range(0, nd, 2):
                to = lax.div(jnp.bitwise_xor(me, d), 2)
                low, high = term[d * kd : (d + 1) * kd], term[(d + 1) * kd : (d + 2) * kd]
                odd = jnp.bitwise_and(me, 1) == 1
                keep[to, r * local + b] = jnp.where(odd, high, low)
                give[to, r * local + b] = jnp.where(odd, low, high)


def first_grad_terms(at, xs, ogs, later, nz, local, width, cols, nd):
    shape = (nd // 2, nz * local, width // nd, cols)
    return on_chip(
        functools.partial(grad_kernel, nz, len(ogs), local, width, cols, nd),
        "first_grad_terms",
        at,
        [a for x in xs for a in x] + list(ogs) + list(later),
        [(shape, BF16)] * 2,
    )


def sums_kernel(plan, at_ref, *refs):
    used = 0
    for i, has_got in enumerate(plan):
        total = refs[used][...]
        if has_got:
            total = (total.astype(F32) + refs[used + 1][...].astype(F32)).astype(BF16)
        used += 1 + has_got
        refs[i - len(plan)][...] = total


def sums(at, pairs, *earlier):
    return on_chip(
        functools.partial(sums_kernel, [got is not None for _, got in pairs]),
        "sums",
        at,
        [a for pair in pairs for a in pair if a is not None] + list(earlier),
        [(part.shape, BF16) for part, _ in pairs],
    )


def after(at, values, *earlier):
    return on_chip(
        functools.partial(sums_kernel, [False] * len(values)),
        "after",
        at,
        list(values) + list(earlier),
        [(v.shape, v.dtype) for v in values],
    )


def halved_kernel(count, at_ref, *refs):
    low, high = refs[-2:]
    half, size = low.shape[0], refs[0].shape[0]
    for i in range(count):
        for b in range(size):
            at = i * size + b
            (low if at < half else high)[at % half] = refs[i][b]


def halved(at, blocks, *earlier):
    size, kd, cols = blocks[0].shape
    shape = (len(blocks) * size // 2, kd, cols)
    return on_chip(
        functools.partial(halved_kernel, len(blocks)), "halved", at, list(blocks) + list(earlier), [(shape, BF16)] * 2
    )


def join_kernel(count, at_ref, *refs):
    out = refs[-1]
    rows = refs[0].shape[0]
    for c in range(count):
        out[c * rows : (c + 1) * rows] = (refs[2 * c][...] + refs[2 * c + 1][...].astype(F32)).astype(BF16)


def join(at, pairs):
    held = [pltpu.with_memory_space_constraint(a, pltpu.VMEM) for pair in pairs for a in pair]
    rows, width = held[0].shape
    return pl.pallas_call(
        functools.partial(join_kernel, len(pairs)),
        in_specs=[SMEM] + [VMEM] * len(held),
        out_specs=VMEM,
        out_shape=jax.ShapeDtypeStruct((rows * len(pairs), width), BF16),
        compiler_params=SMALL,
        cost_estimate=FREE,
        name="join",
    )(at, *held)


def place_kernel(nz, local, cols, factor, at_ref, *refs):
    out = refs[-1]
    for r in range(nz):
        at = pl.multiple_of(lax.rem(at_ref[0] + nz - r, nz) * cols, cols)
        for b in range(local):
            out[:, b, pl.ds(at, cols)] = refs[r][b].astype(F32) * factor


def place(at, pieces, factor):
    nz = len(pieces)
    local, kd, cols = pieces[0].shape
    held = [pltpu.with_memory_space_constraint(a, pltpu.VMEM) for a in pieces]
    return pl.pallas_call(
        functools.partial(place_kernel, nz, local, cols, factor),
        in_specs=[SMEM] + [VMEM] * nz,
        out_specs=VMEM,
        out_shape=jax.ShapeDtypeStruct((kd, local, nz * cols), F32),
        compiler_params=SMALL,
        cost_estimate=FREE,
        name="place",
    )(at, *held)


def swap(bit, nd):
    return [(i, i ^ (1 << bit)) for i in range(nd)]


def ring_step(value, step, nz):
    return lax.ppermute(value, "tensor", [(i, (i + step) % nz) for i in range(nz)])


def double_over_dp(part, bit, d, nd):
    got = lax.ppermute(part, "dp", swap(bit, nd))
    upper = (d >> bit) & 1 == 1
    return jnp.stack([jnp.where(upper, got, part), jnp.where(upper, part, got)])


def body(inputs, first_factor, second_factor, cotangent):
    nz, nd = lax.axis_size("tensor"), lax.axis_size("dp")
    z, d = lax.axis_index("tensor"), lax.axis_index("dp")
    at = jnp.stack([z, d]).astype(jnp.int32)
    tokens_here = inputs.shape[0]
    width, local, out_width = first_factor.shape
    cols = out_width // nz
    kd = width // nd
    steps = (1, -1)
    rows = tokens_here // len(steps)
    bits = nd.bit_length() - 1
    orders = [list(range(1, bits)), list(range(bits - 1, 0, -1))]

    turn = lambda c, n: (-n * steps[c]) % nz
    xs = [[inputs[c * rows : (c + 1) * rows]] + [None] * (nz - 1) for c in range(len(steps))]
    for c in range(len(steps)):
        xs[c][turn(c, 1)] = ring_step(xs[c][0], steps[c], nz)

    def pass_on(n, *earlier, also=()):
        came = after(at, [xs[c][turn(c, n - 1)] for c in range(len(steps))] + list(also), *earlier)
        for c in range(len(steps)):
            xs[c][turn(c, n - 1)] = came[c]
            xs[c][turn(c, n)] = ring_step(came[c], steps[c], nz)
        return came[len(steps) :]

    second = second_factor.transpose(1, 0, 2)
    sends = cut(at, first_factor, nz, nd)
    got = [ring_step(sends[r - 1], -r, nz) for r in range(1, nz)]
    if nz > 2:
        pass_on(2, *got)
    others = halved(at, got, *[xs[c][turn(c, 1)] for c in range(len(steps))])
    for k in range(max(bits - 1, 1)):
        if bits > 1:
            others = [double_over_dp(o, order[k], d, nd) for o, order in zip(others, orders)]
        if k == 0:
            cot = turned(cotangent, others[0])
            own = own_columns(at, first_factor, others[1], nz)
    if nz > 3:
        others = pass_on(3, own, cot, also=others)
    for n in range(4, nz):
        pass_on(n)
    pieces = []
    for o in others:
        pieces += [o, lax.ppermute(o, "dp", swap(0, nd))]
    first = on_chip(
        functools.partial(assemble_kernel, local, kd, orders),
        "assemble",
        at,
        [own] + pieces,
        [((nz * local, width, cols), BF16)],
    )[0]

    parts, ogs = [], []
    for c in range(len(steps)):
        later = [xs[1][turn(1, nz - 1)]] if c == 0 else []
        res = layer(at, xs[c], first, second, cot, later, c, rows, nz, local, width, cols)
        parts.append(res[:nz])
        ogs.append(res[nz])
    ring = [ring_step(parts[0][turn(0, 1)], steps[0], nz), None]

    def ring_next(n, *earlier):
        pairs, whose = [], []
        if n < nz:
            pairs.append((parts[0][turn(0, n)], ring[0]))
            whose.append(0)
        pairs.append((parts[1][turn(1, n - 1)], ring[1]))
        whose.append(1)
        sent = sums(at, pairs, *earlier)
        for c, send in zip(whose, sent):
            ring[c] = ring_step(send, steps[c], nz)
        return sent

    sent = ring_next(2)
    give, keep = first_grad_terms(at, xs, ogs, sent, nz, local, width, cols, nd)
    got = lax.ppermute(give, "dp", swap(0, nd))
    keep = keep.reshape([2] * (bits - 1) + list(keep.shape[1:]))
    got = got.reshape(keep.shape)
    half = nz * local // 2
    totals = []
    for i in range(2):
        cut_half = lambda a: a[(slice(None),) * (bits - 1) + (slice(i * half, (i + 1) * half),)]
        totals.append(cut_half(keep).astype(F32) + cut_half(got).astype(F32))
    left = [list(range(bits - 1, 0, -1)) for _ in range(2)]
    for k in range(bits - 1):
        give = []
        for i in range(2):
            axis = left[i].index(orders[i][k])
            left[i].remove(orders[i][k])
            pick = lambda n: lax.index_in_dim(totals[i], n, axis, keepdims=False)
            give.append(pick(1).astype(BF16))
            totals[i] = pick(0)
        if k == 0 and nz > 2:
            ring_next(3, *give)
        for i in range(2):
            totals[i] = totals[i] + lax.ppermute(give[i], "dp", swap(orders[i][k], nd)).astype(F32)
    blocks = jnp.concatenate(totals, axis=0).reshape(nz, local, kd, cols)
    give = [blocks[r].astype(BF16) for r in range(1, nz)]
    pieces = [blocks[0]] + [ring_step(give[r - 1], r, nz) for r in range(1, nz)]
    for n in range(4, nz + 1):
        ring_next(n, *pieces[1:], ring[0])
    first_sum = place(at, pieces, (tokens_here * nd) ** (-0.5))
    return join(at, [(parts[c][0], ring[c]) for c in range(len(steps))]), first_sum


def plain_body(inputs, first_factor, second_factor, cotangent):
    tokens_here = inputs.shape[0]
    in_width, local, out_width = first_factor.shape
    blocks = local * lax.axis_size("tensor")
    group = out_width // blocks
    block_grouped = inputs.reshape(tokens_here, local, in_width)
    split_first = first_factor.reshape(in_width, local, blocks, group)
    outgoing = jnp.einsum("tlk,kljg->jlgt", block_grouped, split_first, preferred_element_type=F32).astype(BF16)
    arrived = lax.all_to_all(outgoing, "tensor", split_axis=0, concat_axis=1, tiled=True)
    mixed = arrived.reshape(local, out_width, tokens_here)
    pre_act = jnp.einsum("lmt,mln->lnt", mixed, second_factor, preferred_element_type=F32)
    upstream = cotangent.reshape(local, out_width, tokens_here).astype(F32)
    pre_grad = (upstream * gelu_slope(pre_act)).astype(BF16)
    mixed_grad = jnp.einsum("lnt,mln->lmt", pre_grad, second_factor, preferred_element_type=F32).astype(BF16)
    returned = lax.all_to_all(
        mixed_grad.reshape(local, blocks, group, tokens_here), "tensor", split_axis=1, concat_axis=0, tiled=True
    )
    input_grad = jnp.einsum("jlgt,kljg->tlk", returned, split_first, preferred_element_type=F32)
    input_grad = input_grad.reshape(tokens_here, local * in_width).astype(BF16)
    factor = (tokens_here * lax.axis_size("dp")) ** (-0.5)
    first_term = jnp.einsum("tlk,jlgt->kljg", block_grouped, returned, preferred_element_type=F32)
    first_term = first_term.reshape(in_width, local, out_width)
    first_sum = lax.psum_scatter(first_term, "dp", scatter_dimension=0, tiled=True)
    return input_grad, first_sum * factor


def solution(mesh):
    nz, nd = mesh.shape["tensor"], mesh.shape["dp"]

    def run(inputs, first_factor, second_factor, cotangent):
        width, local, _ = first_factor.shape
        fits = local % 2 == 0 and width % (16 * nd) == 0 and nd & (nd - 1) == 0
        return (body if fits else plain_body)(inputs, first_factor, second_factor, cotangent)

    return jax.shard_map(
        run,
        mesh=mesh,
        in_specs=(
            P("dp", "tensor"),
            P(None, "tensor", None),
            P(None, "tensor", None),
            P("tensor", "dp"),
        ),
        out_specs=(P("dp", "tensor"), P("dp", "tensor", None)),
        check_vma=False,
    )
```

time: 246 us -> 128 us (0.52)
  waiting for transfers between devices: 119 us -> 41.9 us
  blocking collectives: 50.2 us -> 0 us
  starting transfers between devices: 6.31 us -> 39 us
  Pallas kernels: 0 us -> 27.8 us
  matrix products: 26.1 us -> 0 us
  between operations: 14.7 us -> 0.97 us
  local copies, waits for them, and re-layouts: 27 us -> 17.3 us
    unnamed x2 -> x0, waiting for transfers between devices: 74.9 us -> none
    all_to_all x1 -> x0, blocking collectives: 50.2 us -> none  [body(): lax.all_to_all(mixed_grad.reshape(local, blocks, group, tokens_here), 'te...]
    all_to_all x1 -> x0, waiting for transfers between devices: 44.1 us -> none  [body(): lax.all_to_all(outgoing, 'tensor', split_axis=0, concat_axis=1, tiled=True)]
    ppermute x0 -> x29, waiting for transfers between devices: none -> 41.9 us  [the longest x18 32.3 us: ring_step(): lax.ppermute(value, 'tensor', [(i, (i + step) % nz) for i in range(nz)])]
    ppermute x0 -> x29, starting transfers between devices: none -> 39 us  [the longest x18 29.4 us: ring_step(): lax.ppermute(value, 'tensor', [(i, (i + step) % nz) for i in range(nz)])]
    pallas_call x0 -> x15, Pallas kernels: none -> 27.8 us  [the longest x10 20.8 us: on_chip(): pl.pallas_call(kernel, in_specs=[SMEM] + [VMEM] * len(held) + [pl.BlockSp...]
    dot_general x4 -> x0, matrix products: 26.1 us -> none  [the longest x1 20.2 us: body(): jnp.einsum('lnt,mln->lmt', pre_grad, second_factor, preferred_element_typ...]
    unnamed x7 -> x15, local copies, waits for them, and re-layouts: 5.21 us -> 16.2 us
  transfers between devices with their start and end apart: 2 -> 29, of which waited for: 2 -> 13; matrix products, arithmetic and copies ran while one was open for 3% -> 8% of each run, Pallas kernels for 0% -> 11%
where the time goes in v1:
time: 128 us
  waiting for transfers between devices  41.9 us (33%)
  starting transfers between devices  39 us (30%)
  Pallas kernels  27.8 us (22%)
  local copies, waits for them, and re-layouts  17.3 us (14%)
    ppermute x18, waiting for transfers between devices, ring_step(): lax.ppermute(value, 'tensor', [(i, (i + step) % nz) for i in range(nz)])  32.3 us
    ppermute x18, starting transfers between devices, ring_step(): lax.ppermute(value, 'tensor', [(i, (i + step) % nz) for i in range(nz)])  29.4 us
    pallas_call x10, Pallas kernels, on_chip(): pl.pallas_call(kernel, in_specs=[SMEM] + [VMEM] * len(held) + [pl.BlockSp...  20.8 us
    unnamed x15, local copies, waits for them, and re-layouts  16.2 us
    ppermute x4, waiting for transfers between devices, double_over_dp(): got = lax.ppermute(part, 'dp', swap(bit, nd))  5.3 us
    ppermute x4, starting transfers between devices, body(): lax.ppermute(give[i], 'dp', swap(orders[i][k], nd)).astype(F32)  4.63 us
    ppermute x4, waiting for transfers between devices, body(): lax.ppermute(give[i], 'dp', swap(orders[i][k], nd)).astype(F32)  4.31 us
    ppermute x4, starting transfers between devices, double_over_dp(): got = lax.ppermute(part, 'dp', swap(bit, nd))  4.25 us
  transfers between devices with their start and end apart: 29, of which 13 were waited for; matrix products, arithmetic and copies ran while one was open for 8% of the time, Pallas kernels for 11%

profile of v1, /device:TPU:0, one launch (start us, length us, event | category | flops | bytes accessed | tf_op | source)
XLA Modules:
  0.0 127.8 jit_solution(11581960014559742029)
XLA Ops:
  0.6 1.1 fusion.9
  1.7 5.1 %collective-permute-start.1 = (bf16[128,1024]{1,0:T(8,128)(2,1)S(1)}, bf16[128,1024]{1,0:T(8,128)(2,1)S(1)}, u32[]{:S(2)}, u32[]{:S(2)}) collective-permute-start(bf16[128,1024]{1,0:T(8,128)(2,1)S(1)} %get-tuple-element.58.refs_0_.refs_4_), channel_id=1, source_target_pairs={{0,3},{1,0},{2,1},{3,2},{4,7},{5,4},{6,5},{7,6},{8,11},{9,8},{10,9... | collective-permute-start | bytes 786440 | tf_op jit(solution)/shard_map/ppermute | solution.py:329
  6.8 0.1 pad_add_fusion.at_ref
  6.9 1.6 %copy-done.2 = bf16[256,4,1024]{2,1,0:T(4,128)(2,1)S(1)} copy-done((bf16[256,4,1024]{2,1,0:T(4,128)(2,1)S(1)}, bf16[256,4,1024]{2,1,0:T(4,128)(2,1)}, u32[]{:S(2)}) %copy-start.2) | copy-done | bytes 2097176
  8.5 0.8 cut.1
  9.3 3.9 %collective-permute-start.2 = (bf16[4,32,256]{2,1,0:T(8,128)(2,1)S(1)}, bf16[4,32,256]{2,1,0:T(8,128)(2,1)S(1)}, u32[]{:S(2)}, u32[]{:S(2)}) collective-permute-start(bf16[4,32,256]{2,1,0:T(8,128)(2,1)S(1)} %get-tuple-element.29), channel_id=1, source_target_pairs={{0,3},{1,0},{2,1},{3,2},{4,7},{5,4},{6,5},{7,6},{8,11},{9,8},{10,9... | collective-permute-start | bytes 196616 | tf_op jit(solution)/shard_map/ppermute | solution.py:329
  13.2 0.6 collective-permute-start.4
  13.8 6.7 %collective-permute-done.2.refs_2_.refs_0_ = bf16[4,32,256]{2,1,0:T(8,128)(2,1)S(1)} collective-permute-done((bf16[4,32,256]{2,1,0:T(8,128)(2,1)S(1)}, bf16[4,32,256]{2,1,0:T(8,128)(2,1)S(1)}, u32[]{:S(2)}, u32[]{:S(2)}) %collective-permute-start.2) | collective-permute-done | bytes 65568 | tf_op jit(solution)/shard_map/ppermute | solution.py:329
  20.5 3.0 %collective-permute-done.3.refs_3_.refs_1_ = bf16[4,32,256]{2,1,0:T(8,128)(2,1)S(1)} collective-permute-done((bf16[4,32,256]{2,1,0:T(8,128)(2,1)S(1)}, bf16[4,32,256]{2,1,0:T(8,128)(2,1)S(1)}, u32[]{:S(2)}, u32[]{:S(2)}) %collective-permute-start.3) | collective-permute-done | bytes 65568 | tf_op jit(solution)/shard_map/ppermute | solution.py:329
  23.5 0.7 copy-done.5
  24.2 0.9 copy-done.6
  25.2 0.6 after.2
  25.7 0.6 halved.1
  26.3 1.6 %collective-permute-start.7 = (bf16[6,32,256]{2,1,0:T(8,128)(2,1)S(1)}, bf16[6,32,256]{2,1,0:T(8,128)(2,1)S(1)}, u32[]{:S(2)}, u32[]{:S(2)}) collective-permute-start(bf16[6,32,256]{2,1,0:T(8,128)(2,1)S(1)} %get-tuple-element.34), channel_id=1, source_target_pairs={{0,8},{4,12},{8,0},{12,4},{16,24},{20,28},{24,16},{28,20},{1,9},{5... | collective-permute-start | bytes 294920 | tf_op jit(solution)/shard_map/ppermute | solution.py:333
  27.9 1.2 collective-permute-start.5
  29.1 2.6 %collective-permute-start.6 = (bf16[128,1024]{1,0:T(8,128)(2,1)S(1)}, bf16[128,1024]{1,0:T(8,128)(2,1)S(1)}, u32[]{:S(2)}, u32[]{:S(2)}) collective-permute-start(bf16[128,1024]{1,0:T(8,128)(2,1)S(1)} %get-tuple-element.33.refs_4_.refs_1_.refs_5_), channel_id=1, source_target_pairs={{0,3},{1,0},{2,1},{3,2},{4,7},{5,4},{6,5},{7,6},{8,11},{9,8},{10,9... | collective-permute-start | bytes 786440 | tf_op jit(solution)/shard_map/ppermute | solution.py:329
  31.7 1.5 %collective-permute-start.9 = (bf16[6,32,256]{2,1,0:T(8,128)(2,1)S(1)}, bf16[6,32,256]{2,1,0:T(8,128)(2,1)S(1)}, u32[]{:S(2)}, u32[]{:S(2)}) collective-permute-start(bf16[6,32,256]{2,1,0:T(8,128)(2,1)S(1)} %get-tuple-element.35), channel_id=1, source_target_pairs={{0,16},{4,20},{8,24},{12,28},{16,0},{20,4},{24,8},{28,12},{1,17},{... | collective-permute-start | bytes 294920 | tf_op jit(solution)/shard_map/ppermute | solution.py:333
  33.3 0.6 collective-permute-start.8
  33.8 3.4 %collective-permute-done.9 = bf16[6,32,256]{2,1,0:T(8,128)(2,1)S(1)} collective-permute-done((bf16[6,32,256]{2,1,0:T(8,128)(2,1)S(1)}, bf16[6,32,256]{2,1,0:T(8,128)(2,1)S(1)}, u32[]{:S(2)}, u32[]{:S(2)}) %collective-permute-start.9) | collective-permute-done | bytes 98336 | tf_op jit(solution)/shard_map/ppermute | solution.py:333
  37.3 0.6 collective-permute-start.10
  37.9 2.0 %own_columns.1.refs_4_.own_ref = bf16[4,256,256]{2,1,0:T(8,128)(2,1)S(1)} custom-call(s32[2]{0:T(128)S(1)} %pad_add_fusion.at_ref, bf16[256,4,1024]{2,1,0:T(4,128)(2,1)S(1)} %copy-done.3, bf16[2,6,32,256]{3,2,1,0:T(8,128)(2,1)S(1)} %pad_maximum_fusion.3.later_ref), custom_call_target="tpu_custom_call" | custom-call | tf_op jit(solution)/shard_map/own_columns/pallas_call | solution.py:79
  39.9 1.2 turned.1.refs_5_
  41.2 1.9 %collective-permute-done.10 = bf16[2,6,32,256]{3,2,1,0:T(8,128)(2,1)S(1)} collective-permute-done((bf16[2,6,32,256]{3,2,1,0:T(8,128)(2,1)S(1)}, bf16[2,6,32,256]{3,2,1,0:T(8,128)(2,1)S(1)}, u32[]{:S(2)}, u32[]{:S(2)}) %collective-permute-start.10) | collective-permute-done | bytes 196640 | tf_op jit(solution)/shard_map/ppermute | solution.py:333
  43.1 0.1 pad_maximum_fusion
  43.2 0.6 after.3
  43.9 0.1 collective-permute-start.12
  43.9 0.5 collective-permute-start.13
  44.4 3.8 %collective-permute-start.14 = (bf16[128,1024]{1,0:T(8,128)(2,1)S(1)}, bf16[128,1024]{1,0:T(8,128)(2,1)S(1)}, u32[]{:S(2)}, u32[]{:S(2)}) collective-permute-start(bf16[128,1024]{1,0:T(8,128)(2,1)S(1)} %get-tuple-element.39.refs_2_.refs_6_), channel_id=1, source_target_pairs={{0,3},{1,0},{2,1},{3,2},{4,7},{5,4},{6,5},{7,6},{8,11},{9,8},{10,9... | collective-permute-start | bytes 786440 | tf_op jit(solution)/shard_map/ppermute | solution.py:329
  48.3 9.5 %copy.13 = bf16[1024,4,1024]{2,0,1:T(8,128)(2,1)} copy(bf16[1024,4,1024]{2,1,0:T(4,128)(2,1)} %param.6) | data formatting | bytes 16777216 | tf_op args[2]
  57.8 0.7 assemble.1.refs_4_
  58.5 3.4 %copy-done = bf16[1024,4,1024]{2,0,1:T(8,128)(2,1)S(1)} copy-done((bf16[1024,4,1024]{2,0,1:T(8,128)(2,1)S(1)}, bf16[1024,4,1024]{2,0,1:T(8,128)(2,1)}, u32[]{:S(2)}) %copy-start) | copy-done | bytes 8388632
  61.9 7.5 %layer.2 = (f32[128,1024]{1,0:T(8,128)S(1)}, bf16[128,1024]{1,0:T(8,128)(2,1)S(1)}, bf16[128,1024]{1,0:T(8,128)(2,1)S(1)}, bf16[128,1024]{1,0:T(8,128)(2,1)S(1)}, bf16[4,128,1024]{2,1,0:T(8,128)(2,1)S(1)}) custom-call(s32[2]{0:T(128)S(1)} %pad_add_fusion.at_ref, bf16[128,1024]{1,0:T(8,128)(2,1)S(1)} %get-tuple-element.59.refs_0_, ...), custom_call_target="tpu_custom_call" | custom-call | tf_op jit(solution)/shard_map/layer/pallas_call | solution.py:34
  69.4 0.8 collective-permute-start.15
  70.3 7.5 %layer.3 = (f32[128,1024]{1,0:T(8,128)S(1)}, bf16[128,1024]{1,0:T(8,128)(2,1)S(1)}, bf16[128,1024]{1,0:T(8,128)(2,1)S(1)}, bf16[128,1024]{1,0:T(8,128)(2,1)S(1)}, bf16[4,128,1024]{2,1,0:T(8,128)(2,1)S(1)}) custom-call(s32[2]{0:T(128)S(1)} %pad_add_fusion.at_ref, bf16[128,1024]{1,0:T(8,128)(2,1)S(1)} %get-tuple-element.58.refs_0_.refs_4_, ...), custom_call_target="tpu_custom_call" | custom-call | tf_op jit(solution)/shard_map/layer/pallas_call | solution.py:34
  77.8 1.4 %collective-permute-done.15.refs_1_ = bf16[128,1024]{1,0:T(8,128)(2,1)S(1)} collective-permute-done((bf16[128,1024]{1,0:T(8,128)(2,1)S(1)}, bf16[128,1024]{1,0:T(8,128)(2,1)S(1)}, u32[]{:S(2)}, u32[]{:S(2)}) %collective-permute-start.15) | collective-permute-done | bytes 262176 | tf_op jit(solution)/shard_map/ppermute | solution.py:329
  79.2 0.6 sums.3
  79.8 1.4 %first_grad_terms.1 = (bf16[4,16,32,256]{3,2,1,0:T(8,128)(2,1)S(1)}, bf16[4,16,32,256]{3,2,1,0:T(8,128)(2,1)S(1)}) custom-call(s32[2]{0:T(128)S(1)} %pad_add_fusion.at_ref, bf16[128,1024]{1,0:T(8,128)(2,1)S(1)} %get-tuple-element.59.refs_0_, bf16[128,1024]{1,0:T(8,128)(2,1)S(1)} %collective-permute-done.11.refs_1_, ...), custom_call_target="tpu_custom_call" | custom-call | tf_op jit(solution)/shard_map/first_grad_terms/pallas_call | solution.py:34
  81.2 0.1 collective-permute-start.18
  81.3 0.9 collective-permute-start.16
  82.2 3.0 %collective-permute-start.17 = (bf16[128,1024]{1,0:T(8,128)(2,1)S(1)}, bf16[128,1024]{1,0:T(8,128)(2,1)S(1)}, u32[]{:S(2)}, u32[]{:S(2)}) collective-permute-start(bf16[128,1024]{1,0:T(8,128)(2,1)S(1)} %get-tuple-element.47.refs_11_), channel_id=1, source_target_pairs={{0,3},{1,0},{2,1},{3,2},{4,7},{5,4},{6,5},{7,6},{8,11},{9,8},{10,9... | collective-permute-start | bytes 786440 | tf_op jit(solution)/shard_map/ppermute | solution.py:329
  85.2 0.3 convert_add_fusion
  85.5 0.6 collective-permute-start.21
  86.2 1.7 %collective-permute-start.24 = (bf16[2,8,32,256]{3,2,1,0:T(8,128)(2,1)S(1)}, bf16[2,8,32,256]{3,2,1,0:T(8,128)(2,1)S(1)}, u32[]{:S(2)}, u32[]{:S(2)}) collective-permute-start(bf16[2,8,32,256]{3,2,1,0:T(8,128)(2,1)S(1)} %fusion.2.refs_5_), channel_id=1, source_target_pairs={{0,16},{4,20},{8,24},{12,28},{16,0},{20,4},{24,8},{28,12},{1,17},{... | collective-permute-start | bytes 786440 | tf_op jit(solution)/shard_map/ppermute | solution.py:432
  87.9 4.4 %collective-permute-done.16.refs_1_ = bf16[128,1024]{1,0:T(8,128)(2,1)S(1)} collective-permute-done((bf16[128,1024]{1,0:T(8,128)(2,1)S(1)}, bf16[128,1024]{1,0:T(8,128)(2,1)S(1)}, u32[]{:S(2)}, u32[]{:S(2)}) %collective-permute-start.16) | collective-permute-done | bytes 262176 | tf_op jit(solution)/shard_map/ppermute | solution.py:329
  92.3 3.9 %collective-permute-done.17.refs_3_ = bf16[128,1024]{1,0:T(8,128)(2,1)S(1)} collective-permute-done((bf16[128,1024]{1,0:T(8,128)(2,1)S(1)}, bf16[128,1024]{1,0:T(8,128)(2,1)S(1)}, u32[]{:S(2)}, u32[]{:S(2)}) %collective-permute-start.17) | collective-permute-done | bytes 262176 | tf_op jit(solution)/shard_map/ppermute | solution.py:329
  96.2 0.7 sums.4
  96.8 0.5 collective-permute-start.19
  97.3 3.4 %collective-permute-start.20 = (bf16[128,1024]{1,0:T(8,128)(2,1)S(1)}, bf16[128,1024]{1,0:T(8,128)(2,1)S(1)}, u32[]{:S(2)}, u32[]{:S(2)}) collective-permute-start(bf16[128,1024]{1,0:T(8,128)(2,1)S(1)} %get-tuple-element.55), channel_id=1, source_target_pairs={{0,3},{1,0},{2,1},{3,2},{4,7},{5,4},{6,5},{7,6},{8,11},{9,8},{10,9... | collective-permute-start | bytes 786440 | tf_op jit(solution)/shard_map/ppermute | solution.py:329
  100.7 0.1 fusion.1
  100.8 1.7 %collective-permute-start.22 = (bf16[8,32,256]{2,1,0:T(8,128)(2,1)S(1)}, bf16[8,32,256]{2,1,0:T(8,128)(2,1)S(1)}, u32[]{:S(2)}, u32[]{:S(2)}) collective-permute-start(bf16[8,32,256]{2,1,0:T(8,128)(2,1)S(1)} %fusion.7), channel_id=1, source_target_pairs={{0,16},{4,20},{8,24},{12,28},{16,0},{20,4},{24,8},{28,12},{1,17},{... | collective-permute-start | bytes 393224 | tf_op jit(solution)/shard_map/ppermute | solution.py:432
  102.5 0.1 fusion
  102.6 0.6 collective-permute-start.25
  103.2 2.6 %collective-permute-done.22 = bf16[8,32,256]{2,1,0:T(8,128)(2,1)S(1)} collective-permute-done((bf16[8,32,256]{2,1,0:T(8,128)(2,1)S(1)}, bf16[8,32,256]{2,1,0:T(8,128)(2,1)S(1)}, u32[]{:S(2)}, u32[]{:S(2)}) %collective-permute-start.22) | collective-permute-done | bytes 131104 | tf_op jit(solution)/shard_map/ppermute | solution.py:432
  105.9 0.1 collective-permute-start.23
  106.0 1.7 %collective-permute-done.25 = bf16[8,32,256]{2,1,0:T(8,128)(2,1)S(1)} collective-permute-done((bf16[8,32,256]{2,1,0:T(8,128)(2,1)S(1)}, bf16[8,32,256]{2,1,0:T(8,128)(2,1)S(1)}, u32[]{:S(2)}, u32[]{:S(2)}) %collective-permute-start.25) | collective-permute-done | bytes 131104 | tf_op jit(solution)/shard_map/ppermute | solution.py:432
  107.7 2.2 %collective-permute-start.27 = (bf16[4,32,256]{2,1,0:T(8,128)(2,1)S(1)}, bf16[4,32,256]{2,1,0:T(8,128)(2,1)S(1)}, u32[]{:S(2)}, u32[]{:S(2)}) collective-permute-start(bf16[4,32,256]{2,1,0:T(8,128)(2,1)S(1)} %get-tuple-element.68), channel_id=1, source_target_pairs={{0,3},{1,0},{2,1},{3,2},{4,7},{5,4},{6,5},{7,6},{8,11},{9,8},{10,9... | collective-permute-start | bytes 196616 | tf_op jit(solution)/shard_map/ppermute | solution.py:329
  109.9 2.3 %collective-permute-done.20.refs_1_ = bf16[128,1024]{1,0:T(8,128)(2,1)S(1)} collective-permute-done((bf16[128,1024]{1,0:T(8,128)(2,1)S(1)}, bf16[128,1024]{1,0:T(8,128)(2,1)S(1)}, u32[]{:S(2)}, u32[]{:S(2)}) %collective-permute-start.20) | collective-permute-done | bytes 262176 | tf_op jit(solution)/shard_map/ppermute | solution.py:329
  112.2 2.6 %collective-permute-done.23.refs_2_.refs_1_ = bf16[4,32,256]{2,1,0:T(8,128)(2,1)S(1)} collective-permute-done((bf16[4,32,256]{2,1,0:T(8,128)(2,1)S(1)}, bf16[4,32,256]{2,1,0:T(8,128)(2,1)S(1)}, u32[]{:S(2)}, u32[]{:S(2)}) %collective-permute-start.23) | collective-permute-done | bytes 65568 | tf_op jit(solution)/shard_map/ppermute | solution.py:329
  114.8 2.7 %collective-permute-done.26.refs_3_.refs_2_ = bf16[4,32,256]{2,1,0:T(8,128)(2,1)S(1)} collective-permute-done((bf16[4,32,256]{2,1,0:T(8,128)(2,1)S(1)}, bf16[4,32,256]{2,1,0:T(8,128)(2,1)S(1)}, u32[]{:S(2)}, u32[]{:S(2)}) %collective-permute-start.26) | collective-permute-done | bytes 65568 | tf_op jit(solution)/shard_map/ppermute | solution.py:329
  117.5 0.6 sums.5
  118.1 1.3 %collective-permute-start.28 = (bf16[128,1024]{1,0:T(8,128)(2,1)S(1)}, bf16[128,1024]{1,0:T(8,128)(2,1)S(1)}, u32[]{:S(2)}, u32[]{:S(2)}) collective-permute-start(bf16[128,1024]{1,0:T(8,128)(2,1)S(1)} %sums.5), channel_id=1, source_target_pairs={{0,3},{1,0},{2,1},{3,2},{4,7},{5,4},{6,5},{7,6},{8,11},{9,8},{10,9... | collective-permute-start | bytes 786440 | tf_op jit(solution)/shard_map/ppermute | solution.py:329
  119.4 1.5 %place.1 = f32[32,4,1024]{2,1,0:T(4,128)} custom-call(s32[2]{0:T(128)S(1)} %pad_add_fusion.at_ref, f32[4,32,256]{2,1,0:T(8,128)S(1)} %slice.102.refs_0_, bf16[4,32,256]{2,1,0:T(8,128)(2,1)S(1)} %collective-permute-done.23.refs_2_.refs_1_, bf16[4,32,256]{2,1,0:T(8,128)(2,1)S(1)} %collective-permute-done.26.refs_3_.refs_2_, ...), custom_call_target="tpu_custom_call" | custom-call | tf_op jit(solution)/shard_map/place/pallas_call | solution.py:313
  121.0 5.4 %collective-permute-done.28.refs_3_ = bf16[128,1024]{1,0:T(8,128)(2,1)S(1)} collective-permute-done((bf16[128,1024]{1,0:T(8,128)(2,1)S(1)}, bf16[128,1024]{1,0:T(8,128)(2,1)S(1)}, u32[]{:S(2)}, u32[]{:S(2)}) %collective-permute-start.28) | collective-permute-done | bytes 262176 | tf_op jit(solution)/shard_map/ppermute | solution.py:329
  126.4 1.4 %join.1 = bf16[256,1024]{1,0:T(8,128)(2,1)} custom-call(s32[2]{0:T(128)S(1)} %pad_add_fusion.at_ref, f32[128,1024]{1,0:T(8,128)S(1)} %get-tuple-element.40.refs_0_, bf16[128,1024]{1,0:T(8,128)(2,1)S(1)} %collective-permute-done.19.refs_5_.refs_1_, f32[128,1024]{1,0:T(8,128)S(1)} %get-tuple-element.53.refs_2_, ...), custom_call_target="tpu_custom_call" | custom-call | tf_op jit(solution)/shard_map/join/pallas_call | solution.py:290
  (45 shorter events, 0.4 us)
Async XLA Ops:
  1.7 21.8 %collective-permute-start.1 = (bf16[128,1024]{1,0:T(8,128)(2,1)S(1)}, bf16[128,1024]{1,0:T(8,128)(2,1)S(1)}, u32[]{:S(2)}, u32[]{:S(2)}) collective-permute-start(bf16[128,1024]{1,0:T(8,128)(2,1)S(1)} %get-tuple-element.58.refs_0_.refs_4_), channel_id=1, source_target_pairs={{0,3},{1,0},{2,1},{3,2},{4,7},{5,4},{6,5},{7,6},{8,11},{9,8},{10,9... | collective-permute-start | bytes 786440 | tf_op jit(solution)/shard_map/ppermute | solution.py:329
  6.8 16.7 %collective-permute-start = (bf16[128,1024]{1,0:T(8,128)(2,1)S(1)}, bf16[128,1024]{1,0:T(8,128)(2,1)S(1)}, u32[]{:S(2)}, u32[]{:S(2)}) collective-permute-start(bf16[128,1024]{1,0:T(8,128)(2,1)S(1)} %get-tuple-element.59.refs_0_), channel_id=1, source_target_pairs={{0,1},{1,2},{2,3},{3,0},{4,5},{5,6},{6,7},{7,4},{8,9},{9,10},{10,1... | collective-permute-start | bytes 786440 | tf_op jit(solution)/shard_map/ppermute | solution.py:329
  6.9 1.6 %copy-start.2 = (bf16[256,4,1024]{2,1,0:T(4,128)(2,1)S(1)}, bf16[256,4,1024]{2,1,0:T(4,128)(2,1)}, u32[]{:S(2)}) copy-start(bf16[256,4,1024]{2,1,0:T(4,128)(2,1)} %f_ref.3) | copy-start | bytes 6291460
  8.5 29.5 %copy-start.3 = (bf16[256,4,1024]{2,1,0:T(4,128)(2,1)S(1)}, bf16[256,4,1024]{2,1,0:T(4,128)(2,1)}, u32[]{:S(2)}) copy-start(bf16[256,4,1024]{2,1,0:T(4,128)(2,1)} %f_ref.3) | copy-start | bytes 6291460
  9.3 11.2 %collective-permute-start.2 = (bf16[4,32,256]{2,1,0:T(8,128)(2,1)S(1)}, bf16[4,32,256]{2,1,0:T(8,128)(2,1)S(1)}, u32[]{:S(2)}, u32[]{:S(2)}) collective-permute-start(bf16[4,32,256]{2,1,0:T(8,128)(2,1)S(1)} %get-tuple-element.29), channel_id=1, source_target_pairs={{0,3},{1,0},{2,1},{3,2},{4,7},{5,4},{6,5},{7,6},{8,11},{9,8},{10,9... | collective-permute-start | bytes 196616 | tf_op jit(solution)/shard_map/ppermute | solution.py:329
  13.2 10.3 %collective-permute-start.3 = (bf16[4,32,256]{2,1,0:T(8,128)(2,1)S(1)}, bf16[4,32,256]{2,1,0:T(8,128)(2,1)S(1)}, u32[]{:S(2)}, u32[]{:S(2)}) collective-permute-start(bf16[4,32,256]{2,1,0:T(8,128)(2,1)S(1)} %get-tuple-element.30), channel_id=1, source_target_pairs={{0,2},{1,3},{2,0},{3,1},{4,6},{5,7},{6,4},{7,5},{8,10},{9,11},{10,... | collective-permute-start | bytes 196616 | tf_op jit(solution)/shard_map/ppermute | solution.py:329
  13.2 10.3 %collective-permute-start.4 = (bf16[4,32,256]{2,1,0:T(8,128)(2,1)S(1)}, bf16[4,32,256]{2,1,0:T(8,128)(2,1)S(1)}, u32[]{:S(2)}, u32[]{:S(2)}) collective-permute-start(bf16[4,32,256]{2,1,0:T(8,128)(2,1)S(1)} %get-tuple-element.31), channel_id=1, source_target_pairs={{0,1},{1,2},{2,3},{3,0},{4,5},{5,6},{6,7},{7,4},{8,9},{9,10},{10,1... | collective-permute-start | bytes 196616 | tf_op jit(solution)/shard_map/ppermute | solution.py:329
  23.5 0.7 copy-start.5
  24.2 0.9 copy-start.6
  26.3 6.9 %collective-permute-start.7 = (bf16[6,32,256]{2,1,0:T(8,128)(2,1)S(1)}, bf16[6,32,256]{2,1,0:T(8,128)(2,1)S(1)}, u32[]{:S(2)}, u32[]{:S(2)}) collective-permute-start(bf16[6,32,256]{2,1,0:T(8,128)(2,1)S(1)} %get-tuple-element.34), channel_id=1, source_target_pairs={{0,8},{4,12},{8,0},{12,4},{16,24},{20,28},{24,16},{28,20},{1,9},{5... | collective-permute-start | bytes 294920 | tf_op jit(solution)/shard_map/ppermute | solution.py:333
  27.9 15.3 %collective-permute-start.5 = (bf16[128,1024]{1,0:T(8,128)(2,1)S(1)}, bf16[128,1024]{1,0:T(8,128)(2,1)S(1)}, u32[]{:S(2)}, u32[]{:S(2)}) collective-permute-start(bf16[128,1024]{1,0:T(8,128)(2,1)S(1)} %get-tuple-element.32.refs_3_), channel_id=1, source_target_pairs={{0,1},{1,2},{2,3},{3,0},{4,5},{5,6},{6,7},{7,4},{8,9},{9,10},{10,1... | collective-permute-start | bytes 786440 | tf_op jit(solution)/shard_map/ppermute | solution.py:329
  29.1 14.1 %collective-permute-start.6 = (bf16[128,1024]{1,0:T(8,128)(2,1)S(1)}, bf16[128,1024]{1,0:T(8,128)(2,1)S(1)}, u32[]{:S(2)}, u32[]{:S(2)}) collective-permute-start(bf16[128,1024]{1,0:T(8,128)(2,1)S(1)} %get-tuple-element.33.refs_4_.refs_1_.refs_5_), channel_id=1, source_target_pairs={{0,3},{1,0},{2,1},{3,2},{4,7},{5,4},{6,5},{7,6},{8,11},{9,8},{10,9... | collective-permute-start | bytes 786440 | tf_op jit(solution)/shard_map/ppermute | solution.py:329
  31.7 5.6 %collective-permute-start.9 = (bf16[6,32,256]{2,1,0:T(8,128)(2,1)S(1)}, bf16[6,32,256]{2,1,0:T(8,128)(2,1)S(1)}, u32[]{:S(2)}, u32[]{:S(2)}) collective-permute-start(bf16[6,32,256]{2,1,0:T(8,128)(2,1)S(1)} %get-tuple-element.35), channel_id=1, source_target_pairs={{0,16},{4,20},{8,24},{12,28},{16,0},{20,4},{24,8},{28,12},{1,17},{... | collective-permute-start | bytes 294920 | tf_op jit(solution)/shard_map/ppermute | solution.py:333
  33.2 6.7 %copy-start.4 = (bf16[4096,256]{1,0:T(8,128)(2,1)S(1)}, bf16[4096,256]{1,0:T(8,128)(2,1)}, u32[]{:S(2)}) copy-start(bf16[4096,256]{1,0:T(8,128)(2,1)} %x_ref.1) | copy-start | bytes 6291460
  33.3 7.9 %collective-permute-start.8 = (bf16[2,6,32,256]{3,2,1,0:T(8,128)(2,1)S(1)}, bf16[2,6,32,256]{3,2,1,0:T(8,128)(2,1)S(1)}, u32[]{:S(2)}, u32[]{:S(2)}) collective-permute-start(bf16[2,6,32,256]{3,2,1,0:T(8,128)(2,1)S(1)} %pad_maximum_fusion.2.later_ref), channel_id=1, source_target_pairs={{0,16},{4,20},{8,24},{12,28},{16,0},{20,4},{24,8},{28,12},{1,17},{... | collective-permute-start | bytes 589832 | tf_op jit(solution)/shard_map/ppermute | solution.py:333
  37.3 5.7 %collective-permute-start.10 = (bf16[2,6,32,256]{3,2,1,0:T(8,128)(2,1)S(1)}, bf16[2,6,32,256]{3,2,1,0:T(8,128)(2,1)S(1)}, u32[]{:S(2)}, u32[]{:S(2)}) collective-permute-start(bf16[2,6,32,256]{3,2,1,0:T(8,128)(2,1)S(1)} %pad_maximum_fusion.3.later_ref), channel_id=1, source_target_pairs={{0,8},{4,12},{8,0},{12,4},{16,24},{20,28},{24,16},{28,20},{1,9},{5... | collective-permute-start | bytes 589832 | tf_op jit(solution)/shard_map/ppermute | solution.py:333
  43.9 13.9 %collective-permute-start.12 = (bf16[2,2,6,32,256]{4,3,2,1,0:T(8,128)(2,1)S(1)}, bf16[2,2,6,32,256]{4,3,2,1,0:T(8,128)(2,1)S(1)}, u32[]{:S(2)}, u32[]{:S(2)}) collective-permute-start(bf16[2,2,6,32,256]{4,3,2,1,0:T(8,128)(2,1)S(1)} %get-tuple-element.37.refs_0_), channel_id=1, source_target_pairs={{0,4},{4,0},{8,12},{12,8},{16,20},{20,16},{24,28},{28,24},{1,5},{5... | collective-permute-start | bytes 1179656 | tf_op jit(solution)/shard_map/ppermute | solution.py:381
  43.9 13.9 %collective-permute-start.13 = (bf16[2,2,6,32,256]{4,3,2,1,0:T(8,128)(2,1)S(1)}, bf16[2,2,6,32,256]{4,3,2,1,0:T(8,128)(2,1)S(1)}, u32[]{:S(2)}, u32[]{:S(2)}) collective-permute-start(bf16[2,2,6,32,256]{4,3,2,1,0:T(8,128)(2,1)S(1)} %get-tuple-element.38.refs_2_), channel_id=1, source_target_pairs={{0,4},{4,0},{8,12},{12,8},{16,20},{20,16},{24,28},{28,24},{1,5},{5... | collective-permute-start | bytes 1179656 | tf_op jit(solution)/shard_map/ppermute | solution.py:381
  44.4 14.1 %collective-permute-start.11 = (bf16[128,1024]{1,0:T(8,128)(2,1)S(1)}, bf16[128,1024]{1,0:T(8,128)(2,1)S(1)}, u32[]{:S(2)}, u32[]{:S(2)}) collective-permute-start(bf16[128,1024]{1,0:T(8,128)(2,1)S(1)} %get-tuple-element.36.refs_2_), channel_id=1, source_target_pairs={{0,1},{1,2},{2,3},{3,0},{4,5},{5,6},{6,7},{7,4},{8,9},{9,10},{10,1... | collective-permute-start | bytes 786440 | tf_op jit(solution)/shard_map/ppermute | solution.py:329
  44.4 14.1 %collective-permute-start.14 = (bf16[128,1024]{1,0:T(8,128)(2,1)S(1)}, bf16[128,1024]{1,0:T(8,128)(2,1)S(1)}, u32[]{:S(2)}, u32[]{:S(2)}) collective-permute-start(bf16[128,1024]{1,0:T(8,128)(2,1)S(1)} %get-tuple-element.39.refs_2_.refs_6_), channel_id=1, source_target_pairs={{0,3},{1,0},{2,1},{3,2},{4,7},{5,4},{6,5},{7,6},{8,11},{9,8},{10,9... | collective-permute-start | bytes 786440 | tf_op jit(solution)/shard_map/ppermute | solution.py:329
  58.5 3.4 %copy-start = (bf16[1024,4,1024]{2,0,1:T(8,128)(2,1)S(1)}, bf16[1024,4,1024]{2,0,1:T(8,128)(2,1)}, u32[]{:S(2)}) copy-start(bf16[1024,4,1024]{2,0,1:T(8,128)(2,1)} %copy.13) | copy-start | bytes 25165828
  61.9 8.4 %copy-start.1 = (bf16[1024,4,1024]{2,0,1:T(8,128)(2,1)S(1)}, bf16[1024,4,1024]{2,0,1:T(8,128)(2,1)}, u32[]{:S(2)}) copy-start(bf16[1024,4,1024]{2,0,1:T(8,128)(2,1)} %copy.13) | copy-start | bytes 25165828
  69.4 9.8 %collective-permute-start.15 = (bf16[128,1024]{1,0:T(8,128)(2,1)S(1)}, bf16[128,1024]{1,0:T(8,128)(2,1)S(1)}, u32[]{:S(2)}, u32[]{:S(2)}) collective-permute-start(bf16[128,1024]{1,0:T(8,128)(2,1)S(1)} %get-tuple-element.43), channel_id=1, source_target_pairs={{0,1},{1,2},{2,3},{3,0},{4,5},{5,6},{6,7},{7,4},{8,9},{9,10},{10,1... | collective-permute-start | bytes 786440 | tf_op jit(solution)/shard_map/ppermute | solution.py:329
  81.2 4.0 %collective-permute-start.18 = (bf16[4,16,32,256]{3,2,1,0:T(8,128)(2,1)S(1)}, bf16[4,16,32,256]{3,2,1,0:T(8,128)(2,1)S(1)}, u32[]{:S(2)}, u32[]{:S(2)}) collective-permute-start(bf16[4,16,32,256]{3,2,1,0:T(8,128)(2,1)S(1)} %get-tuple-element.51), channel_id=1, source_target_pairs={{0,4},{4,0},{8,12},{12,8},{16,20},{20,16},{24,28},{28,24},{1,5},{5... | collective-permute-start | bytes 3145736 | tf_op jit(solution)/shard_map/ppermute | solution.py:412
  81.3 11.0 %collective-permute-start.16 = (bf16[128,1024]{1,0:T(8,128)(2,1)S(1)}, bf16[128,1024]{1,0:T(8,128)(2,1)S(1)}, u32[]{:S(2)}, u32[]{:S(2)}) collective-permute-start(bf16[128,1024]{1,0:T(8,128)(2,1)S(1)} %get-tuple-element.45.refs_10_), channel_id=1, source_target_pairs={{0,1},{1,2},{2,3},{3,0},{4,5},{5,6},{6,7},{7,4},{8,9},{9,10},{10,1... | collective-permute-start | bytes 786440 | tf_op jit(solution)/shard_map/ppermute | solution.py:329
  82.2 14.0 %collective-permute-start.17 = (bf16[128,1024]{1,0:T(8,128)(2,1)S(1)}, bf16[128,1024]{1,0:T(8,128)(2,1)S(1)}, u32[]{:S(2)}, u32[]{:S(2)}) collective-permute-start(bf16[128,1024]{1,0:T(8,128)(2,1)S(1)} %get-tuple-element.47.refs_11_), channel_id=1, source_target_pairs={{0,3},{1,0},{2,1},{3,2},{4,7},{5,4},{6,5},{7,6},{8,11},{9,8},{10,9... | collective-permute-start | bytes 786440 | tf_op jit(solution)/shard_map/ppermute | solution.py:329
  85.5 15.2 %collective-permute-start.21 = (bf16[2,8,32,256]{3,2,1,0:T(8,128)(2,1)S(1)}, bf16[2,8,32,256]{3,2,1,0:T(8,128)(2,1)S(1)}, u32[]{:S(2)}, u32[]{:S(2)}) collective-permute-start(bf16[2,8,32,256]{3,2,1,0:T(8,128)(2,1)S(1)} %fusion.3.refs_4_), channel_id=1, source_target_pairs={{0,8},{4,12},{8,0},{12,4},{16,24},{20,28},{24,16},{28,20},{1,9},{5... | collective-permute-start | bytes 786440 | tf_op jit(solution)/shard_map/ppermute | solution.py:432
  86.2 16.3 %collective-permute-start.24 = (bf16[2,8,32,256]{3,2,1,0:T(8,128)(2,1)S(1)}, bf16[2,8,32,256]{3,2,1,0:T(8,128)(2,1)S(1)}, u32[]{:S(2)}, u32[]{:S(2)}) collective-permute-start(bf16[2,8,32,256]{3,2,1,0:T(8,128)(2,1)S(1)} %fusion.2.refs_5_), channel_id=1, source_target_pairs={{0,16},{4,20},{8,24},{12,28},{16,0},{20,4},{24,8},{28,12},{1,17},{... | collective-permute-start | bytes 786440 | tf_op jit(solution)/shard_map/ppermute | solution.py:432
  96.8 13.1 %collective-permute-start.19 = (bf16[128,1024]{1,0:T(8,128)(2,1)S(1)}, bf16[128,1024]{1,0:T(8,128)(2,1)S(1)}, u32[]{:S(2)}, u32[]{:S(2)}) collective-permute-start(bf16[128,1024]{1,0:T(8,128)(2,1)S(1)} %get-tuple-element.52), channel_id=1, source_target_pairs={{0,1},{1,2},{2,3},{3,0},{4,5},{5,6},{6,7},{7,4},{8,9},{9,10},{10,1... | collective-permute-start | bytes 786440 | tf_op jit(solution)/shard_map/ppermute | solution.py:329
  97.3 14.9 %collective-permute-start.20 = (bf16[128,1024]{1,0:T(8,128)(2,1)S(1)}, bf16[128,1024]{1,0:T(8,128)(2,1)S(1)}, u32[]{:S(2)}, u32[]{:S(2)}) collective-permute-start(bf16[128,1024]{1,0:T(8,128)(2,1)S(1)} %get-tuple-element.55), channel_id=1, source_target_pairs={{0,3},{1,0},{2,1},{3,2},{4,7},{5,4},{6,5},{7,6},{8,11},{9,8},{10,9... | collective-permute-start | bytes 786440 | tf_op jit(solution)/shard_map/ppermute | solution.py:329
  100.8 5.0 %collective-permute-start.22 = (bf16[8,32,256]{2,1,0:T(8,128)(2,1)S(1)}, bf16[8,32,256]{2,1,0:T(8,128)(2,1)S(1)}, u32[]{:S(2)}, u32[]{:S(2)}) collective-permute-start(bf16[8,32,256]{2,1,0:T(8,128)(2,1)S(1)} %fusion.7), channel_id=1, source_target_pairs={{0,16},{4,20},{8,24},{12,28},{16,0},{20,4},{24,8},{28,12},{1,17},{... | collective-permute-start | bytes 393224 | tf_op jit(solution)/shard_map/ppermute | solution.py:432
  102.6 5.0 %collective-permute-start.25 = (bf16[8,32,256]{2,1,0:T(8,128)(2,1)S(1)}, bf16[8,32,256]{2,1,0:T(8,128)(2,1)S(1)}, u32[]{:S(2)}, u32[]{:S(2)}) collective-permute-start(bf16[8,32,256]{2,1,0:T(8,128)(2,1)S(1)} %fusion.8), channel_id=1, source_target_pairs={{0,8},{4,12},{8,0},{12,4},{16,24},{20,28},{24,16},{28,20},{1,9},{5... | collective-permute-start | bytes 393224 | tf_op jit(solution)/shard_map/ppermute | solution.py:432
  105.9 8.9 %collective-permute-start.23 = (bf16[4,32,256]{2,1,0:T(8,128)(2,1)S(1)}, bf16[4,32,256]{2,1,0:T(8,128)(2,1)S(1)}, u32[]{:S(2)}, u32[]{:S(2)}) collective-permute-start(bf16[4,32,256]{2,1,0:T(8,128)(2,1)S(1)} %slice.131), channel_id=1, source_target_pairs={{0,1},{1,2},{2,3},{3,0},{4,5},{5,6},{6,7},{7,4},{8,9},{9,10},{10,1... | collective-permute-start | bytes 196616 | tf_op jit(solution)/shard_map/ppermute | solution.py:329
  107.7 7.1 %collective-permute-start.27 = (bf16[4,32,256]{2,1,0:T(8,128)(2,1)S(1)}, bf16[4,32,256]{2,1,0:T(8,128)(2,1)S(1)}, u32[]{:S(2)}, u32[]{:S(2)}) collective-permute-start(bf16[4,32,256]{2,1,0:T(8,128)(2,1)S(1)} %get-tuple-element.68), channel_id=1, source_target_pairs={{0,3},{1,0},{2,1},{3,2},{4,7},{5,4},{6,5},{7,6},{8,11},{9,8},{10,9... | collective-permute-start | bytes 196616 | tf_op jit(solution)/shard_map/ppermute | solution.py:329
  109.9 7.6 %collective-permute-start.26 = (bf16[4,32,256]{2,1,0:T(8,128)(2,1)S(1)}, bf16[4,32,256]{2,1,0:T(8,128)(2,1)S(1)}, u32[]{:S(2)}, u32[]{:S(2)}) collective-permute-start(bf16[4,32,256]{2,1,0:T(8,128)(2,1)S(1)} %get-tuple-element.69), channel_id=1, source_target_pairs={{0,2},{1,3},{2,0},{3,1},{4,6},{5,7},{6,4},{7,5},{8,10},{9,11},{10,... | collective-permute-start | bytes 196616 | tf_op jit(solution)/shard_map/ppermute | solution.py:329
  118.1 8.3 %collective-permute-start.28 = (bf16[128,1024]{1,0:T(8,128)(2,1)S(1)}, bf16[128,1024]{1,0:T(8,128)(2,1)S(1)}, u32[]{:S(2)}, u32[]{:S(2)}) collective-permute-start(bf16[128,1024]{1,0:T(8,128)(2,1)S(1)} %sums.5), channel_id=1, source_target_pairs={{0,3},{1,0},{2,1},{3,2},{4,7},{5,4},{6,5},{7,6},{8,11},{9,8},{10,9... | collective-permute-start | bytes 786440 | tf_op jit(solution)/shard_map/ppermute | solution.py:329

commit v2 on v1

--- a/solution.py
+++ b/solution.py
@@ -30,17 +30,18 @@
 
 def on_chip(kernel, name, at, operands, shapes, stored=(), limit=16 << 20, **more):
     held = [pltpu.with_memory_space_constraint(a, pltpu.VMEM) for a in operands]
+    held += [pltpu.with_memory_space_constraint(a, pltpu.HBM) for a in stored]
     out = [pltpu.VMEM(shape, dtype) for shape, dtype in shapes]
     return pl.pallas_call(
         kernel,
-        in_specs=[SMEM] + [VMEM] * len(held) + [pl.BlockSpec(memory_space=pl.ANY)] * len(stored),
+        in_specs=[SMEM] + [VMEM] * len(operands) + [pl.BlockSpec(memory_space=pltpu.HBM)] * len(stored),
         out_specs=[VMEM] * len(out),
         out_shape=out,
         compiler_params=pltpu.CompilerParams(vmem_limit_bytes=limit),
         cost_estimate=FREE,
         name=name,
         **more,
-    )(at, *held, *stored)
+    )(at, *held)
 
 
 def cut_kernel(nz, local, cols, kd, at_ref, f_ref, *outs):
@@ -128,11 +129,14 @@
 
 def layer_kernel(nz, local, width, cols, chunk, at_ref, *refs):
     x_refs = refs[:nz]
-    f_ref, cot_ref = refs[nz : nz + 2]
-    s_hbm, *dx_refs, og_ref, mixed, back, s_ref, arrived = refs[-(nz + 6) :]
-    fetch = [pltpu.make_async_copy(s_hbm.at[j], s_ref.at[j], arrived.at[j]) for j in range(local)]
-    for copy in fetch:
-        copy.start()
+    f_ref, cot_ref, s_ref = refs[nz : nz + 3]
+    if chunk == 0:
+        s_hbm, *dx_refs, og_ref, s_ref, mixed, back, arrived = refs[-(nz + 6) :]
+        fetch = [pltpu.make_async_copy(s_hbm.at[j], s_ref.at[j], arrived.at[j]) for j in range(local)]
+        for copy in fetch:
+            copy.start()
+    else:
+        *dx_refs, og_ref, mixed, back = refs[-(nz + 3) :]
     z = at_ref[0]
     group = cols // local
     rows, out_width = dx_refs[0].shape[0], mixed.shape[2]
@@ -153,7 +157,8 @@
     planes = [lax.rem(z + r, nz) for r in range(nz)]
 
     for j in range(local):
-        fetch[j].wait()
+        if chunk == 0:
+            fetch[j].wait()
         weight = jnp.concatenate(
             [s_ref[j, pl.ds(pl.multiple_of(p * cols, cols), cols), :] for p in planes], axis=0
         )
@@ -186,16 +191,17 @@
         functools.partial(layer_kernel, nz, local, width, cols, chunk),
         "layer",
         at,
-        list(xs) + [first, cot, *later],
-        [(piece, F32)] + [(piece, BF16)] * (nz - 1) + [((nz, rows, local * cols), BF16)],
+        list(xs) + [first, cot] + (list(later) if chunk == 0 else [second]),
+        [(piece, F32)]
+        + [(piece, BF16)] * (nz - 1)
+        + [((nz, rows, local * cols), BF16)]
+        + [(second.shape, BF16)] * (chunk == 0),
         scratch_shapes=[
             pltpu.VMEM((local, rows, out_width), BF16),
             pltpu.VMEM((local, rows, out_width), F32),
-            pltpu.VMEM(second.shape, BF16),
-            pltpu.SemaphoreType.DMA((local,)),
-        ],
-        stored=[second],
-        limit=28 << 20,
+        ]
+        + [pltpu.SemaphoreType.DMA((local,))] * (chunk == 0),
+        stored=[second] if chunk == 0 else (),
     )
 
 
@@ -250,14 +256,32 @@
     )
 
 
-def after(at, values, *earlier):
+def after(at, values, *earlier, stored=()):
     return on_chip(
         functools.partial(sums_kernel, [False] * len(values)),
         "after",
         at,
         list(values) + list(earlier),
         [(v.shape, v.dtype) for v in values],
-    )
+        stored=stored,
+    )
+
+
+def mark_kernel(at_ref, *refs):
+    refs[-1][...] = jnp.zeros_like(refs[-1])
+
+
+def mark(at, values):
+    held = [pltpu.with_memory_space_constraint(a, pltpu.VMEM) for a in values]
+    return pl.pallas_call(
+        mark_kernel,
+        in_specs=[SMEM] + [VMEM] * len(held),
+        out_specs=VMEM,
+        out_shape=pltpu.VMEM((8, 128), F32),
+        compiler_params=SMALL,
+        cost_estimate=pl.CostEstimate(flops=10**10, bytes_accessed=32 << 20, transcendentals=0),
+        name="mark",
+    )(at, *held)
 
 
 def halved_kernel(count, at_ref, *refs):
@@ -309,10 +333,10 @@
 def place(at, pieces, factor):
     nz = len(pieces)
     local, kd, cols = pieces[0].shape
-    held = [pltpu.with_memory_space_constraint(a, pltpu.VMEM) for a in pieces]
+    held = [pltpu.with_memory_space_constraint(a, pltpu.VMEM) for a in [*pieces, mark(at, pieces[1:])]]
     return pl.pallas_call(
         functools.partial(place_kernel, nz, local, cols, factor),
-        in_specs=[SMEM] + [VMEM] * nz,
+        in_specs=[SMEM] + [VMEM] * (nz + 1),
         out_specs=VMEM,
         out_shape=jax.ShapeDtypeStruct((kd, local, nz * cols), F32),
         compiler_params=SMALL,
@@ -353,8 +377,9 @@
     for c in range(len(steps)):
         xs[c][turn(c, 1)] = ring_step(xs[c][0], steps[c], nz)
 
-    def pass_on(n, *earlier, also=()):
-        came = after(at, [xs[c][turn(c, n - 1)] for c in range(len(steps))] + list(also), *earlier)
+    def pass_on(n, *earlier, also=(), stored=()):
+        arrived = [xs[c][turn(c, n - 1)] for c in range(len(steps))]
+        came = after(at, arrived + list(also), mark(at, arrived), *earlier, stored=stored)
         for c in range(len(steps)):
             xs[c][turn(c, n - 1)] = came[c]
             xs[c][turn(c, n)] = ring_step(came[c], steps[c], nz)
@@ -364,7 +389,7 @@
     sends = cut(at, first_factor, nz, nd)
     got = [ring_step(sends[r - 1], -r, nz) for r in range(1, nz)]
     if nz > 2:
-        pass_on(2, *got)
+        pass_on(2, *got, stored=[second])
     others = halved(at, got, *[xs[c][turn(c, 1)] for c in range(len(steps))])
     for k in range(max(bits - 1, 1)):
         if bits > 1:
@@ -372,8 +397,8 @@
         if k == 0:
             cot = turned(cotangent, others[0])
             own = own_columns(at, first_factor, others[1], nz)
-    if nz > 3:
-        others = pass_on(3, own, cot, also=others)
+            if nz > 3:
+                others = pass_on(3, own, cot, also=others)
     for n in range(4, nz):
         pass_on(n)
     pieces = []
@@ -389,10 +414,11 @@
 
     parts, ogs = [], []
     for c in range(len(steps)):
-        later = [xs[1][turn(1, nz - 1)]] if c == 0 else []
+        later = [mark(at, [x[turn(i, nz - 1)] for i, x in enumerate(xs)])] if c == 0 else []
         res = layer(at, xs[c], first, second, cot, later, c, rows, nz, local, width, cols)
         parts.append(res[:nz])
         ogs.append(res[nz])
+        second = res[-1] if c == 0 else second
     ring = [ring_step(parts[0][turn(0, 1)], steps[0], nz), None]
 
     def ring_next(n, *earlier):
@@ -434,7 +460,7 @@
     give = [blocks[r].astype(BF16) for r in range(1, nz)]
     pieces = [blocks[0]] + [ring_step(give[r - 1], r, nz) for r in range(1, nz)]
     for n in range(4, nz + 1):
-        ring_next(n, *pieces[1:], ring[0])
+        ring_next(n, *give, ring[0])
     first_sum = place(at, pieces, (tokens_here * nd) ** (-0.5))
     return join(at, [(parts[c][0], ring[c]) for c in range(len(steps))]), first_sum
 

time: 128 us -> 121 us (0.945)
  waiting for transfers between devices: 41.9 us -> 36.7 us
  local copies, waits for them, and re-layouts: 17.3 us -> 13.4 us
    unnamed x15 -> x11, local copies, waits for them, and re-layouts: 16.2 us -> 12.2 us
    ppermute x18, waiting for transfers between devices: 32.3 us -> 29.4 us  [ring_step(): lax.ppermute(value, 'tensor', [(i, (i + step) % nz) for i in range(nz)])]
    ppermute x4, waiting for transfers between devices: 5.3 us -> 2.97 us  [double_over_dp(): got = lax.ppermute(part, 'dp', swap(bit, nd))]
    pallas_call x10 -> x14, Pallas kernels: 20.8 us -> 21.6 us  [the longest x10 19.5 us: on_chip(): pl.pallas_call(kernel, in_specs=[SMEM] + [VMEM] * len(operands) + [pl.Blo...]
  transfers between devices with their start and end apart: 29 -> 29, of which waited for: 13 -> 15; matrix products, arithmetic and copies ran while one was open for 8% -> 9% of each run, Pallas kernels for 11% -> 12%
where the time goes in v2:
time: 121 us; the launch traced here: 120 us
  starting transfers between devices  39.6 us (33%)
  waiting for transfers between devices  36.7 us (30%)
  Pallas kernels  28.7 us (24%)
  local copies, waits for them, and re-layouts  13.4 us (11%)
    ppermute x18, starting transfers between devices, ring_step(): lax.ppermute(value, 'tensor', [(i, (i + step) % nz) for i in range(nz)])  29.8 us
    ppermute x18, waiting for transfers between devices, ring_step(): lax.ppermute(value, 'tensor', [(i, (i + step) % nz) for i in range(nz)])  29.4 us
    pallas_call x10, Pallas kernels, on_chip(): pl.pallas_call(kernel, in_specs=[SMEM] + [VMEM] * len(operands) + [pl.Blo...  19.5 us
    unnamed x11, local copies, waits for them, and re-layouts  12.2 us
    ppermute x4, starting transfers between devices, double_over_dp(): got = lax.ppermute(part, 'dp', swap(bit, nd))  5.14 us
    ppermute x4, starting transfers between devices, body(): lax.ppermute(give[i], 'dp', swap(orders[i][k], nd)).astype(F32)  4.41 us
    ppermute x4, waiting for transfers between devices, body(): lax.ppermute(give[i], 'dp', swap(orders[i][k], nd)).astype(F32)  4.3 us
    ppermute x4, waiting for transfers between devices, double_over_dp(): got = lax.ppermute(part, 'dp', swap(bit, nd))  2.97 us
  transfers between devices with their start and end apart: 29, of which 15 were waited for; matrix products, arithmetic and copies ran while one was open for 9% of the time, Pallas kernels for 12%

profile of v2, /device:TPU:0, one launch (start us, length us, event | category | flops | bytes accessed | tf_op | source)
XLA Modules:
  0.0 120.3 jit_solution(13772315964378859541)
XLA Ops:
  0.6 1.1 fusion.9
  1.7 5.1 %collective-permute-start.1 = (bf16[128,1024]{1,0:T(8,128)(2,1)S(1)}, bf16[128,1024]{1,0:T(8,128)(2,1)S(1)}, u32[]{:S(2)}, u32[]{:S(2)}) collective-permute-start(bf16[128,1024]{1,0:T(8,128)(2,1)S(1)} %get-tuple-element.60.refs_0_.refs_4_), channel_id=1, source_target_pairs={{0,3},{1,0},{2,1},{3,2},{4,7},{5,4},{6,5},{7,6},{8,11},{9,8},{10,9... | collective-permute-start | bytes 786440 | tf_op jit(solution)/shard_map/ppermute | solution.py:353
  6.8 0.1 pad_add_fusion.at_ref
  6.9 1.6 %copy-done = bf16[256,4,1024]{2,1,0:T(4,128)(2,1)S(1)} copy-done((bf16[256,4,1024]{2,1,0:T(4,128)(2,1)S(1)}, bf16[256,4,1024]{2,1,0:T(4,128)(2,1)}, u32[]{:S(2)}) %copy-start) | copy-done | bytes 2097176
  8.5 0.8 cut.1
  9.3 3.9 %collective-permute-start.2 = (bf16[4,32,256]{2,1,0:T(8,128)(2,1)S(1)}, bf16[4,32,256]{2,1,0:T(8,128)(2,1)S(1)}, u32[]{:S(2)}, u32[]{:S(2)}) collective-permute-start(bf16[4,32,256]{2,1,0:T(8,128)(2,1)S(1)} %get-tuple-element.30), channel_id=1, source_target_pairs={{0,3},{1,0},{2,1},{3,2},{4,7},{5,4},{6,5},{7,6},{8,11},{9,8},{10,9... | collective-permute-start | bytes 196616 | tf_op jit(solution)/shard_map/ppermute | solution.py:353
  13.2 0.6 collective-permute-start.4
  13.8 9.5 %copy.13 = bf16[1024,4,1024]{2,0,1:T(8,128)(2,1)} copy(bf16[1024,4,1024]{2,1,0:T(4,128)(2,1)} %param.6) | data formatting | bytes 16777216 | tf_op args[2]
  23.4 0.5 mark.4.refs_2_
  23.9 0.1 copy-done.3
  24.1 0.9 copy-done.4
  25.1 0.6 after.2
  25.6 0.6 halved.1
  26.2 1.6 %collective-permute-start.8 = (bf16[6,32,256]{2,1,0:T(8,128)(2,1)S(1)}, bf16[6,32,256]{2,1,0:T(8,128)(2,1)S(1)}, u32[]{:S(2)}, u32[]{:S(2)}) collective-permute-start(bf16[6,32,256]{2,1,0:T(8,128)(2,1)S(1)} %get-tuple-element.36), channel_id=1, source_target_pairs={{0,16},{4,20},{8,24},{12,28},{16,0},{20,4},{24,8},{28,12},{1,17},{... | collective-permute-start | bytes 294920 | tf_op jit(solution)/shard_map/ppermute | solution.py:357
  27.8 2.8 %collective-permute-start.5 = (bf16[128,1024]{1,0:T(8,128)(2,1)S(1)}, bf16[128,1024]{1,0:T(8,128)(2,1)S(1)}, u32[]{:S(2)}, u32[]{:S(2)}) collective-permute-start(bf16[128,1024]{1,0:T(8,128)(2,1)S(1)} %get-tuple-element.33.refs_3_), channel_id=1, source_target_pairs={{0,1},{1,2},{2,3},{3,0},{4,5},{5,6},{6,7},{7,4},{8,9},{9,10},{10,1... | collective-permute-start | bytes 786440 | tf_op jit(solution)/shard_map/ppermute | solution.py:353
  30.6 1.0 collective-permute-start.6
  31.6 1.5 %collective-permute-start.7 = (bf16[6,32,256]{2,1,0:T(8,128)(2,1)S(1)}, bf16[6,32,256]{2,1,0:T(8,128)(2,1)S(1)}, u32[]{:S(2)}, u32[]{:S(2)}) collective-permute-start(bf16[6,32,256]{2,1,0:T(8,128)(2,1)S(1)} %get-tuple-element.35), channel_id=1, source_target_pairs={{0,8},{4,12},{8,0},{12,4},{16,24},{20,28},{24,16},{28,20},{1,9},{5... | collective-permute-start | bytes 294920 | tf_op jit(solution)/shard_map/ppermute | solution.py:357
  33.2 2.0 %own_columns.1.refs_5_.own_ref = bf16[4,256,256]{2,1,0:T(8,128)(2,1)S(1)} custom-call(s32[2]{0:T(128)S(1)} %pad_add_fusion.at_ref, bf16[256,4,1024]{2,1,0:T(4,128)(2,1)S(1)} %copy-done.1, bf16[2,6,32,256]{3,2,1,0:T(8,128)(2,1)S(1)} %pad_maximum_fusion.3.later_ref.refs_3_), custom_call_target="tpu_custom_call" | custom-call | tf_op jit(solution)/shard_map/own_columns/pallas_call | solution.py:80
  35.2 1.1 collective-permute-done.7
  36.3 1.2 %turned.1.refs_6_.refs_5_ = bf16[256,4096]{1,0:T(8,128)(2,1)S(1)} custom-call(bf16[4096,256]{1,0:T(8,128)(2,1)S(1)} %copy-done.2, bf16[2,6,32,256]{3,2,1,0:T(8,128)(2,1)S(1)} %pad_maximum_fusion.2.later_ref.refs_2_), custom_call_target="tpu_custom_call" | custom-call | tf_op jit(solution)/shard_map/turned/pallas_call | solution.py:101
  37.5 1.3 %collective-permute-done.5.refs_0_ = bf16[128,1024]{1,0:T(8,128)(2,1)S(1)} collective-permute-done((bf16[128,1024]{1,0:T(8,128)(2,1)S(1)}, bf16[128,1024]{1,0:T(8,128)(2,1)S(1)}, u32[]{:S(2)}, u32[]{:S(2)}) %collective-permute-start.5) | collective-permute-done | bytes 262176 | tf_op jit(solution)/shard_map/ppermute | solution.py:353
  38.8 3.5 %collective-permute-done.6.refs_1_ = bf16[128,1024]{1,0:T(8,128)(2,1)S(1)} collective-permute-done((bf16[128,1024]{1,0:T(8,128)(2,1)S(1)}, bf16[128,1024]{1,0:T(8,128)(2,1)S(1)}, u32[]{:S(2)}, u32[]{:S(2)}) %collective-permute-start.6) | collective-permute-done | bytes 262176 | tf_op jit(solution)/shard_map/ppermute | solution.py:353
  42.3 0.5 mark.5.refs_4_
  42.9 0.6 after.3
  43.5 1.6 %collective-permute-start.12 = (bf16[2,6,32,256]{3,2,1,0:T(8,128)(2,1)S(1)}, bf16[2,6,32,256]{3,2,1,0:T(8,128)(2,1)S(1)}, u32[]{:S(2)}, u32[]{:S(2)}) collective-permute-start(bf16[2,6,32,256]{3,2,1,0:T(8,128)(2,1)S(1)} %get-tuple-element.39), channel_id=1, source_target_pairs={{0,8},{4,12},{8,0},{12,4},{16,24},{20,28},{24,16},{28,20},{1,9},{5... | collective-permute-start | bytes 589832 | tf_op jit(solution)/shard_map/ppermute | solution.py:357
  45.0 0.5 collective-permute-start.10
  45.6 0.3 collective-permute-start.9
  45.8 3.5 %collective-permute-start.14 = (bf16[128,1024]{1,0:T(8,128)(2,1)S(1)}, bf16[128,1024]{1,0:T(8,128)(2,1)S(1)}, u32[]{:S(2)}, u32[]{:S(2)}) collective-permute-start(bf16[128,1024]{1,0:T(8,128)(2,1)S(1)} %get-tuple-element.40.refs_2_.refs_6_), channel_id=1, source_target_pairs={{0,3},{1,0},{2,1},{3,2},{4,7},{5,4},{6,5},{7,6},{8,11},{9,8},{10,9... | collective-permute-start | bytes 786440 | tf_op jit(solution)/shard_map/ppermute | solution.py:353
  49.4 0.9 collective-permute-done.12
  50.3 0.1 collective-permute-start.13
  50.4 1.1 collective-permute-done.10
  51.6 5.0 %collective-permute-done.9.refs_0_.refs_1_ = bf16[128,1024]{1,0:T(8,128)(2,1)S(1)} collective-permute-done((bf16[128,1024]{1,0:T(8,128)(2,1)S(1)}, bf16[128,1024]{1,0:T(8,128)(2,1)S(1)}, u32[]{:S(2)}, u32[]{:S(2)}) %collective-permute-start.9) | collective-permute-done | bytes 262176 | tf_op jit(solution)/shard_map/ppermute | solution.py:353
  56.6 2.1 %collective-permute-done.14.refs_1_.refs_3_.refs_7_ = bf16[128,1024]{1,0:T(8,128)(2,1)S(1)} collective-permute-done((bf16[128,1024]{1,0:T(8,128)(2,1)S(1)}, bf16[128,1024]{1,0:T(8,128)(2,1)S(1)}, u32[]{:S(2)}, u32[]{:S(2)}) %collective-permute-start.14) | collective-permute-done | bytes 262176 | tf_op jit(solution)/shard_map/ppermute | solution.py:353
  58.7 0.5 mark.6.refs_6_
  59.3 0.7 assemble.1.refs_4_
  60.0 7.8 %layer.2 = (f32[128,1024]{1,0:T(8,128)S(1)}, bf16[128,1024]{1,0:T(8,128)(2,1)S(1)}, bf16[128,1024]{1,0:T(8,128)(2,1)S(1)}, bf16[128,1024]{1,0:T(8,128)(2,1)S(1)}...) custom-call(s32[2]{0:T(128)S(1)} %pad_add_fusion.at_ref, ...), custom_call_target="tpu_custom_call" | custom-call | tf_op jit(solution)/shard_map/layer/pallas_call | solution.py:35
  67.8 0.2 collective-permute-start.15
  68.1 5.9 %layer.3 = (f32[128,1024]{1,0:T(8,128)S(1)}, bf16[128,1024]{1,0:T(8,128)(2,1)S(1)}, bf16[128,1024]{1,0:T(8,128)(2,1)S(1)}, bf16[128,1024]{1,0:T(8,128)(2,1)S(1)}, bf16[4,128,1024]{2,1,0:T(8,128)(2,1)S(1)}) custom-call(s32[2]{0:T(128)S(1)} %pad_add_fusion.at_ref, bf16[128,1024]{1,0:T(8,128)(2,1)S(1)} %get-tuple-element.60.refs_0_.refs_4_, ...), custom_call_target="tpu_custom_call" | custom-call | tf_op jit(solution)/shard_map/layer/pallas_call | solution.py:35
  74.0 2.2 %collective-permute-done.15.refs_1_ = bf16[128,1024]{1,0:T(8,128)(2,1)S(1)} collective-permute-done((bf16[128,1024]{1,0:T(8,128)(2,1)S(1)}, bf16[128,1024]{1,0:T(8,128)(2,1)S(1)}, u32[]{:S(2)}, u32[]{:S(2)}) %collective-permute-start.15) | collective-permute-done | bytes 262176 | tf_op jit(solution)/shard_map/ppermute | solution.py:353
  76.2 0.6 sums.3
  76.8 1.4 %first_grad_terms.1 = (bf16[4,16,32,256]{3,2,1,0:T(8,128)(2,1)S(1)}, bf16[4,16,32,256]{3,2,1,0:T(8,128)(2,1)S(1)}) custom-call(s32[2]{0:T(128)S(1)} %pad_add_fusion.at_ref, bf16[128,1024]{1,0:T(8,128)(2,1)S(1)} %get-tuple-element.61.refs_0_, bf16[128,1024]{1,0:T(8,128)(2,1)S(1)} %collective-permute-done.9.refs_0_.refs_1_, ...), custom_call_target="tpu_custom_call" | custom-call | tf_op jit(solution)/shard_map/first_grad_terms/pallas_call | solution.py:35
  78.3 0.8 collective-permute-start.16
  79.1 3.1 %collective-permute-start.17 = (bf16[128,1024]{1,0:T(8,128)(2,1)S(1)}, bf16[128,1024]{1,0:T(8,128)(2,1)S(1)}, u32[]{:S(2)}, u32[]{:S(2)}) collective-permute-start(bf16[128,1024]{1,0:T(8,128)(2,1)S(1)} %get-tuple-element.49.refs_11_), channel_id=1, source_target_pairs={{0,3},{1,0},{2,1},{3,2},{4,7},{5,4},{6,5},{7,6},{8,11},{9,8},{10,9... | collective-permute-start | bytes 786440 | tf_op jit(solution)/shard_map/ppermute | solution.py:353
  82.2 0.4 convert_add_fusion
  82.6 0.6 collective-permute-start.21
  83.3 1.6 %collective-permute-start.23 = (bf16[2,8,32,256]{3,2,1,0:T(8,128)(2,1)S(1)}, bf16[2,8,32,256]{3,2,1,0:T(8,128)(2,1)S(1)}, u32[]{:S(2)}, u32[]{:S(2)}) collective-permute-start(bf16[2,8,32,256]{3,2,1,0:T(8,128)(2,1)S(1)} %fusion.2.refs_5_), channel_id=1, source_target_pairs={{0,16},{4,20},{8,24},{12,28},{16,0},{20,4},{24,8},{28,12},{1,17},{... | collective-permute-start | bytes 786440 | tf_op jit(solution)/shard_map/ppermute | solution.py:458
  84.9 4.4 %collective-permute-done.16.refs_1_ = bf16[128,1024]{1,0:T(8,128)(2,1)S(1)} collective-permute-done((bf16[128,1024]{1,0:T(8,128)(2,1)S(1)}, bf16[128,1024]{1,0:T(8,128)(2,1)S(1)}, u32[]{:S(2)}, u32[]{:S(2)}) %collective-permute-start.16) | collective-permute-done | bytes 262176 | tf_op jit(solution)/shard_map/ppermute | solution.py:353
  89.3 3.8 %collective-permute-done.17.refs_3_ = bf16[128,1024]{1,0:T(8,128)(2,1)S(1)} collective-permute-done((bf16[128,1024]{1,0:T(8,128)(2,1)S(1)}, bf16[128,1024]{1,0:T(8,128)(2,1)S(1)}, u32[]{:S(2)}, u32[]{:S(2)}) %collective-permute-start.17) | collective-permute-done | bytes 262176 | tf_op jit(solution)/shard_map/ppermute | solution.py:353
  93.1 0.7 sums.4
  93.8 0.8 collective-permute-start.19
  94.6 3.1 %collective-permute-start.20 = (bf16[128,1024]{1,0:T(8,128)(2,1)S(1)}, bf16[128,1024]{1,0:T(8,128)(2,1)S(1)}, u32[]{:S(2)}, u32[]{:S(2)}) collective-permute-start(bf16[128,1024]{1,0:T(8,128)(2,1)S(1)} %get-tuple-element.57), channel_id=1, source_target_pairs={{0,3},{1,0},{2,1},{3,2},{4,7},{5,4},{6,5},{7,6},{8,11},{9,8},{10,9... | collective-permute-start | bytes 786440 | tf_op jit(solution)/shard_map/ppermute | solution.py:353
  97.8 1.6 %collective-permute-start.22 = (bf16[8,32,256]{2,1,0:T(8,128)(2,1)S(1)}, bf16[8,32,256]{2,1,0:T(8,128)(2,1)S(1)}, u32[]{:S(2)}, u32[]{:S(2)}) collective-permute-start(bf16[8,32,256]{2,1,0:T(8,128)(2,1)S(1)} %fusion.7), channel_id=1, source_target_pairs={{0,16},{4,20},{8,24},{12,28},{16,0},{20,4},{24,8},{28,12},{1,17},{... | collective-permute-start | bytes 393224 | tf_op jit(solution)/shard_map/ppermute | solution.py:458
  99.5 0.6 collective-permute-start.24
  100.1 2.7 %collective-permute-done.22 = bf16[8,32,256]{2,1,0:T(8,128)(2,1)S(1)} collective-permute-done((bf16[8,32,256]{2,1,0:T(8,128)(2,1)S(1)}, bf16[8,32,256]{2,1,0:T(8,128)(2,1)S(1)}, u32[]{:S(2)}, u32[]{:S(2)}) %collective-permute-start.22) | collective-permute-done | bytes 131104 | tf_op jit(solution)/shard_map/ppermute | solution.py:458
  102.9 1.6 %collective-permute-done.24 = bf16[8,32,256]{2,1,0:T(8,128)(2,1)S(1)} collective-permute-done((bf16[8,32,256]{2,1,0:T(8,128)(2,1)S(1)}, bf16[8,32,256]{2,1,0:T(8,128)(2,1)S(1)}, u32[]{:S(2)}, u32[]{:S(2)}) %collective-permute-start.24) | collective-permute-done | bytes 131104 | tf_op jit(solution)/shard_map/ppermute | solution.py:458
  104.5 2.3 %collective-permute-start.28 = (bf16[4,32,256]{2,1,0:T(8,128)(2,1)S(1)}, bf16[4,32,256]{2,1,0:T(8,128)(2,1)S(1)}, u32[]{:S(2)}, u32[]{:S(2)}) collective-permute-start(bf16[4,32,256]{2,1,0:T(8,128)(2,1)S(1)} %get-tuple-element.70.refs_4_), channel_id=1, source_target_pairs={{0,3},{1,0},{2,1},{3,2},{4,7},{5,4},{6,5},{7,6},{8,11},{9,8},{10,9... | collective-permute-start | bytes 196616 | tf_op jit(solution)/shard_map/ppermute | solution.py:353
  106.9 2.3 %collective-permute-done.20.refs_1_ = bf16[128,1024]{1,0:T(8,128)(2,1)S(1)} collective-permute-done((bf16[128,1024]{1,0:T(8,128)(2,1)S(1)}, bf16[128,1024]{1,0:T(8,128)(2,1)S(1)}, u32[]{:S(2)}, u32[]{:S(2)}) %collective-permute-start.20) | collective-permute-done | bytes 262176 | tf_op jit(solution)/shard_map/ppermute | solution.py:353
  109.2 0.6 sums.5
  109.8 2.2 %collective-permute-start.25 = (bf16[128,1024]{1,0:T(8,128)(2,1)S(1)}, bf16[128,1024]{1,0:T(8,128)(2,1)S(1)}, u32[]{:S(2)}, u32[]{:S(2)}) collective-permute-start(bf16[128,1024]{1,0:T(8,128)(2,1)S(1)} %sums.5), channel_id=1, source_target_pairs={{0,3},{1,0},{2,1},{3,2},{4,7},{5,4},{6,5},{7,6},{8,11},{9,8},{10,9... | collective-permute-start | bytes 786440 | tf_op jit(solution)/shard_map/ppermute | solution.py:353
  112.0 2.5 %collective-permute-done.27.refs_1_.refs_2_ = bf16[4,32,256]{2,1,0:T(8,128)(2,1)S(1)} collective-permute-done((bf16[4,32,256]{2,1,0:T(8,128)(2,1)S(1)}, bf16[4,32,256]{2,1,0:T(8,128)(2,1)S(1)}, u32[]{:S(2)}, u32[]{:S(2)}) %collective-permute-start.27) | collective-permute-done | bytes 65568 | tf_op jit(solution)/shard_map/ppermute | solution.py:353
  114.5 0.5 mark.7.refs_4_
  115.1 1.5 %place.1 = f32[32,4,1024]{2,1,0:T(4,128)} custom-call(s32[2]{0:T(128)S(1)} %pad_add_fusion.at_ref, f32[4,32,256]{2,1,0:T(8,128)S(1)} %slice.102.refs_0_, bf16[4,32,256]{2,1,0:T(8,128)(2,1)S(1)} %collective-permute-done.26.refs_0_.refs_1_, bf16[4,32,256]{2,1,0:T(8,128)(2,1)S(1)} %collective-permute-done.27.refs_1_.refs_2_, ...), custom_call_target="tpu_custom_call" | custom-call | tf_op jit(solution)/shard_map/place/pallas_call | solution.py:337
  116.6 2.2 %collective-permute-done.25.refs_3_ = bf16[128,1024]{1,0:T(8,128)(2,1)S(1)} collective-permute-done((bf16[128,1024]{1,0:T(8,128)(2,1)S(1)}, bf16[128,1024]{1,0:T(8,128)(2,1)S(1)}, u32[]{:S(2)}, u32[]{:S(2)}) %collective-permute-start.25) | collective-permute-done | bytes 262176 | tf_op jit(solution)/shard_map/ppermute | solution.py:353
  118.8 1.5 %join.1 = bf16[256,1024]{1,0:T(8,128)(2,1)} custom-call(s32[2]{0:T(128)S(1)} %pad_add_fusion.at_ref, f32[128,1024]{1,0:T(8,128)S(1)} %get-tuple-element.41.refs_0_, bf16[128,1024]{1,0:T(8,128)(2,1)S(1)} %collective-permute-done.19.refs_5_.refs_1_, f32[128,1024]{1,0:T(8,128)S(1)} %get-tuple-element.55.refs_2_, ...), custom_call_target="tpu_custom_call" | custom-call | tf_op jit(solution)/shard_map/join/pallas_call | solution.py:314
  (46 shorter events, 0.8 us)
Async XLA Ops:
  1.7 21.7 %collective-permute-start.1 = (bf16[128,1024]{1,0:T(8,128)(2,1)S(1)}, bf16[128,1024]{1,0:T(8,128)(2,1)S(1)}, u32[]{:S(2)}, u32[]{:S(2)}) collective-permute-start(bf16[128,1024]{1,0:T(8,128)(2,1)S(1)} %get-tuple-element.60.refs_0_.refs_4_), channel_id=1, source_target_pairs={{0,3},{1,0},{2,1},{3,2},{4,7},{5,4},{6,5},{7,6},{8,11},{9,8},{10,9... | collective-permute-start | bytes 786440 | tf_op jit(solution)/shard_map/ppermute | solution.py:353
  6.8 16.6 %collective-permute-start = (bf16[128,1024]{1,0:T(8,128)(2,1)S(1)}, bf16[128,1024]{1,0:T(8,128)(2,1)S(1)}, u32[]{:S(2)}, u32[]{:S(2)}) collective-permute-start(bf16[128,1024]{1,0:T(8,128)(2,1)S(1)} %get-tuple-element.61.refs_0_), channel_id=1, source_target_pairs={{0,1},{1,2},{2,3},{3,0},{4,5},{5,6},{6,7},{7,4},{8,9},{9,10},{10,1... | collective-permute-start | bytes 786440 | tf_op jit(solution)/shard_map/ppermute | solution.py:353
  6.9 1.6 %copy-start = (bf16[256,4,1024]{2,1,0:T(4,128)(2,1)S(1)}, bf16[256,4,1024]{2,1,0:T(4,128)(2,1)}, u32[]{:S(2)}) copy-start(bf16[256,4,1024]{2,1,0:T(4,128)(2,1)} %f_ref.3) | copy-start | bytes 6291460
  9.3 14.8 %collective-permute-start.2 = (bf16[4,32,256]{2,1,0:T(8,128)(2,1)S(1)}, bf16[4,32,256]{2,1,0:T(8,128)(2,1)S(1)}, u32[]{:S(2)}, u32[]{:S(2)}) collective-permute-start(bf16[4,32,256]{2,1,0:T(8,128)(2,1)S(1)} %get-tuple-element.30), channel_id=1, source_target_pairs={{0,3},{1,0},{2,1},{3,2},{4,7},{5,4},{6,5},{7,6},{8,11},{9,8},{10,9... | collective-permute-start | bytes 196616 | tf_op jit(solution)/shard_map/ppermute | solution.py:353
  13.2 10.9 %collective-permute-start.3 = (bf16[4,32,256]{2,1,0:T(8,128)(2,1)S(1)}, bf16[4,32,256]{2,1,0:T(8,128)(2,1)S(1)}, u32[]{:S(2)}, u32[]{:S(2)}) collective-permute-start(bf16[4,32,256]{2,1,0:T(8,128)(2,1)S(1)} %get-tuple-element.31), channel_id=1, source_target_pairs={{0,2},{1,3},{2,0},{3,1},{4,6},{5,7},{6,4},{7,5},{8,10},{9,11},{10,... | collective-permute-start | bytes 196616 | tf_op jit(solution)/shard_map/ppermute | solution.py:353
  13.2 10.9 %collective-permute-start.4 = (bf16[4,32,256]{2,1,0:T(8,128)(2,1)S(1)}, bf16[4,32,256]{2,1,0:T(8,128)(2,1)S(1)}, u32[]{:S(2)}, u32[]{:S(2)}) collective-permute-start(bf16[4,32,256]{2,1,0:T(8,128)(2,1)S(1)} %get-tuple-element.32), channel_id=1, source_target_pairs={{0,1},{1,2},{2,3},{3,0},{4,5},{5,6},{6,7},{7,4},{8,9},{9,10},{10,1... | collective-permute-start | bytes 196616 | tf_op jit(solution)/shard_map/ppermute | solution.py:353
  23.4 0.7 copy-start.3
  24.1 1.0 copy-start.4
  25.0 8.1 %copy-start.1 = (bf16[256,4,1024]{2,1,0:T(4,128)(2,1)S(1)}, bf16[256,4,1024]{2,1,0:T(4,128)(2,1)}, u32[]{:S(2)}) copy-start(bf16[256,4,1024]{2,1,0:T(4,128)(2,1)} %f_ref.3) | copy-start | bytes 6291460
  26.2 6.9 %collective-permute-start.8 = (bf16[6,32,256]{2,1,0:T(8,128)(2,1)S(1)}, bf16[6,32,256]{2,1,0:T(8,128)(2,1)S(1)}, u32[]{:S(2)}, u32[]{:S(2)}) collective-permute-start(bf16[6,32,256]{2,1,0:T(8,128)(2,1)S(1)} %get-tuple-element.36), channel_id=1, source_target_pairs={{0,16},{4,20},{8,24},{12,28},{16,0},{20,4},{24,8},{28,12},{1,17},{... | collective-permute-start | bytes 294920 | tf_op jit(solution)/shard_map/ppermute | solution.py:357
  27.8 11.0 %collective-permute-start.5 = (bf16[128,1024]{1,0:T(8,128)(2,1)S(1)}, bf16[128,1024]{1,0:T(8,128)(2,1)S(1)}, u32[]{:S(2)}, u32[]{:S(2)}) collective-permute-start(bf16[128,1024]{1,0:T(8,128)(2,1)S(1)} %get-tuple-element.33.refs_3_), channel_id=1, source_target_pairs={{0,1},{1,2},{2,3},{3,0},{4,5},{5,6},{6,7},{7,4},{8,9},{9,10},{10,1... | collective-permute-start | bytes 786440 | tf_op jit(solution)/shard_map/ppermute | solution.py:353
  30.6 11.7 %collective-permute-start.6 = (bf16[128,1024]{1,0:T(8,128)(2,1)S(1)}, bf16[128,1024]{1,0:T(8,128)(2,1)S(1)}, u32[]{:S(2)}, u32[]{:S(2)}) collective-permute-start(bf16[128,1024]{1,0:T(8,128)(2,1)S(1)} %get-tuple-element.34.refs_4_.refs_1_.refs_5_), channel_id=1, source_target_pairs={{0,3},{1,0},{2,1},{3,2},{4,7},{5,4},{6,5},{7,6},{8,11},{9,8},{10,9... | collective-permute-start | bytes 786440 | tf_op jit(solution)/shard_map/ppermute | solution.py:353
  31.6 4.6 %collective-permute-start.7 = (bf16[6,32,256]{2,1,0:T(8,128)(2,1)S(1)}, bf16[6,32,256]{2,1,0:T(8,128)(2,1)S(1)}, u32[]{:S(2)}, u32[]{:S(2)}) collective-permute-start(bf16[6,32,256]{2,1,0:T(8,128)(2,1)S(1)} %get-tuple-element.35), channel_id=1, source_target_pairs={{0,8},{4,12},{8,0},{12,4},{16,24},{20,28},{24,16},{28,20},{1,9},{5... | collective-permute-start | bytes 294920 | tf_op jit(solution)/shard_map/ppermute | solution.py:357
  33.1 3.2 %copy-start.2 = (bf16[4096,256]{1,0:T(8,128)(2,1)S(1)}, bf16[4096,256]{1,0:T(8,128)(2,1)}, u32[]{:S(2)}) copy-start(bf16[4096,256]{1,0:T(8,128)(2,1)} %x_ref.1) | copy-start | bytes 6291460
  43.5 6.8 %collective-permute-start.12 = (bf16[2,6,32,256]{3,2,1,0:T(8,128)(2,1)S(1)}, bf16[2,6,32,256]{3,2,1,0:T(8,128)(2,1)S(1)}, u32[]{:S(2)}, u32[]{:S(2)}) collective-permute-start(bf16[2,6,32,256]{3,2,1,0:T(8,128)(2,1)S(1)} %get-tuple-element.39), channel_id=1, source_target_pairs={{0,8},{4,12},{8,0},{12,4},{16,24},{20,28},{24,16},{28,20},{1,9},{5... | collective-permute-start | bytes 589832 | tf_op jit(solution)/shard_map/ppermute | solution.py:357
  45.0 6.4 %collective-permute-start.10 = (bf16[2,6,32,256]{3,2,1,0:T(8,128)(2,1)S(1)}, bf16[2,6,32,256]{3,2,1,0:T(8,128)(2,1)S(1)}, u32[]{:S(2)}, u32[]{:S(2)}) collective-permute-start(bf16[2,6,32,256]{3,2,1,0:T(8,128)(2,1)S(1)} %get-tuple-element.38), channel_id=1, source_target_pairs={{0,16},{4,20},{8,24},{12,28},{16,0},{20,4},{24,8},{28,12},{1,17},{... | collective-permute-start | bytes 589832 | tf_op jit(solution)/shard_map/ppermute | solution.py:357
  45.6 11.0 %collective-permute-start.9 = (bf16[128,1024]{1,0:T(8,128)(2,1)S(1)}, bf16[128,1024]{1,0:T(8,128)(2,1)S(1)}, u32[]{:S(2)}, u32[]{:S(2)}) collective-permute-start(bf16[128,1024]{1,0:T(8,128)(2,1)S(1)} %get-tuple-element.37.refs_2_), channel_id=1, source_target_pairs={{0,1},{1,2},{2,3},{3,0},{4,5},{5,6},{6,7},{7,4},{8,9},{9,10},{10,1... | collective-permute-start | bytes 786440 | tf_op jit(solution)/shard_map/ppermute | solution.py:353
  45.8 12.9 %collective-permute-start.14 = (bf16[128,1024]{1,0:T(8,128)(2,1)S(1)}, bf16[128,1024]{1,0:T(8,128)(2,1)S(1)}, u32[]{:S(2)}, u32[]{:S(2)}) collective-permute-start(bf16[128,1024]{1,0:T(8,128)(2,1)S(1)} %get-tuple-element.40.refs_2_.refs_6_), channel_id=1, source_target_pairs={{0,3},{1,0},{2,1},{3,2},{4,7},{5,4},{6,5},{7,6},{8,11},{9,8},{10,9... | collective-permute-start | bytes 786440 | tf_op jit(solution)/shard_map/ppermute | solution.py:353
  50.3 8.9 %collective-permute-start.13 = (bf16[2,2,6,32,256]{4,3,2,1,0:T(8,128)(2,1)S(1)}, bf16[2,2,6,32,256]{4,3,2,1,0:T(8,128)(2,1)S(1)}, u32[]{:S(2)}, u32[]{:S(2)}) collective-permute-start(bf16[2,2,6,32,256]{4,3,2,1,0:T(8,128)(2,1)S(1)} %pad_maximum_fusion.1.refs_2_), channel_id=1, source_target_pairs={{0,4},{4,0},{8,12},{12,8},{16,20},{20,16},{24,28},{28,24},{1,5},{5... | collective-permute-start | bytes 1179656 | tf_op jit(solution)/shard_map/ppermute | solution.py:406
  51.5 7.7 %collective-permute-start.11 = (bf16[2,2,6,32,256]{4,3,2,1,0:T(8,128)(2,1)S(1)}, bf16[2,2,6,32,256]{4,3,2,1,0:T(8,128)(2,1)S(1)}, u32[]{:S(2)}, u32[]{:S(2)}) collective-permute-start(bf16[2,2,6,32,256]{4,3,2,1,0:T(8,128)(2,1)S(1)} %pad_maximum_fusion.refs_0_), channel_id=1, source_target_pairs={{0,4},{4,0},{8,12},{12,8},{16,20},{20,16},{24,28},{28,24},{1,5},{5... | collective-permute-start | bytes 1179656 | tf_op jit(solution)/shard_map/ppermute | solution.py:406
  67.8 8.4 %collective-permute-start.15 = (bf16[128,1024]{1,0:T(8,128)(2,1)S(1)}, bf16[128,1024]{1,0:T(8,128)(2,1)S(1)}, u32[]{:S(2)}, u32[]{:S(2)}) collective-permute-start(bf16[128,1024]{1,0:T(8,128)(2,1)S(1)} %get-tuple-element.44), channel_id=1, source_target_pairs={{0,1},{1,2},{2,3},{3,0},{4,5},{5,6},{6,7},{7,4},{8,9},{9,10},{10,1... | collective-permute-start | bytes 786440 | tf_op jit(solution)/shard_map/ppermute | solution.py:353
  78.2 4.0 %collective-permute-start.18 = (bf16[4,16,32,256]{3,2,1,0:T(8,128)(2,1)S(1)}, bf16[4,16,32,256]{3,2,1,0:T(8,128)(2,1)S(1)}, u32[]{:S(2)}, u32[]{:S(2)}) collective-permute-start(bf16[4,16,32,256]{3,2,1,0:T(8,128)(2,1)S(1)} %get-tuple-element.53), channel_id=1, source_target_pairs={{0,4},{4,0},{8,12},{12,8},{16,20},{20,16},{24,28},{28,24},{1,5},{5... | collective-permute-start | bytes 3145736 | tf_op jit(solution)/shard_map/ppermute | solution.py:438
  78.3 11.0 %collective-permute-start.16 = (bf16[128,1024]{1,0:T(8,128)(2,1)S(1)}, bf16[128,1024]{1,0:T(8,128)(2,1)S(1)}, u32[]{:S(2)}, u32[]{:S(2)}) collective-permute-start(bf16[128,1024]{1,0:T(8,128)(2,1)S(1)} %get-tuple-element.47.refs_10_), channel_id=1, source_target_pairs={{0,1},{1,2},{2,3},{3,0},{4,5},{5,6},{6,7},{7,4},{8,9},{9,10},{10,1... | collective-permute-start | bytes 786440 | tf_op jit(solution)/shard_map/ppermute | solution.py:353
  79.1 14.0 %collective-permute-start.17 = (bf16[128,1024]{1,0:T(8,128)(2,1)S(1)}, bf16[128,1024]{1,0:T(8,128)(2,1)S(1)}, u32[]{:S(2)}, u32[]{:S(2)}) collective-permute-start(bf16[128,1024]{1,0:T(8,128)(2,1)S(1)} %get-tuple-element.49.refs_11_), channel_id=1, source_target_pairs={{0,3},{1,0},{2,1},{3,2},{4,7},{5,4},{6,5},{7,6},{8,11},{9,8},{10,9... | collective-permute-start | bytes 786440 | tf_op jit(solution)/shard_map/ppermute | solution.py:353
  82.6 15.0 %collective-permute-start.21 = (bf16[2,8,32,256]{3,2,1,0:T(8,128)(2,1)S(1)}, bf16[2,8,32,256]{3,2,1,0:T(8,128)(2,1)S(1)}, u32[]{:S(2)}, u32[]{:S(2)}) collective-permute-start(bf16[2,8,32,256]{3,2,1,0:T(8,128)(2,1)S(1)} %fusion.3.refs_4_), channel_id=1, source_target_pairs={{0,8},{4,12},{8,0},{12,4},{16,24},{20,28},{24,16},{28,20},{1,9},{5... | collective-permute-start | bytes 786440 | tf_op jit(solution)/shard_map/ppermute | solution.py:458
  83.3 16.1 %collective-permute-start.23 = (bf16[2,8,32,256]{3,2,1,0:T(8,128)(2,1)S(1)}, bf16[2,8,32,256]{3,2,1,0:T(8,128)(2,1)S(1)}, u32[]{:S(2)}, u32[]{:S(2)}) collective-permute-start(bf16[2,8,32,256]{3,2,1,0:T(8,128)(2,1)S(1)} %fusion.2.refs_5_), channel_id=1, source_target_pairs={{0,16},{4,20},{8,24},{12,28},{16,0},{20,4},{24,8},{28,12},{1,17},{... | collective-permute-start | bytes 786440 | tf_op jit(solution)/shard_map/ppermute | solution.py:458
  93.8 13.1 %collective-permute-start.19 = (bf16[128,1024]{1,0:T(8,128)(2,1)S(1)}, bf16[128,1024]{1,0:T(8,128)(2,1)S(1)}, u32[]{:S(2)}, u32[]{:S(2)}) collective-permute-start(bf16[128,1024]{1,0:T(8,128)(2,1)S(1)} %get-tuple-element.54), channel_id=1, source_target_pairs={{0,1},{1,2},{2,3},{3,0},{4,5},{5,6},{6,7},{7,4},{8,9},{9,10},{10,1... | collective-permute-start | bytes 786440 | tf_op jit(solution)/shard_map/ppermute | solution.py:353
  94.6 14.6 %collective-permute-start.20 = (bf16[128,1024]{1,0:T(8,128)(2,1)S(1)}, bf16[128,1024]{1,0:T(8,128)(2,1)S(1)}, u32[]{:S(2)}, u32[]{:S(2)}) collective-permute-start(bf16[128,1024]{1,0:T(8,128)(2,1)S(1)} %get-tuple-element.57), channel_id=1, source_target_pairs={{0,3},{1,0},{2,1},{3,2},{4,7},{5,4},{6,5},{7,6},{8,11},{9,8},{10,9... | collective-permute-start | bytes 786440 | tf_op jit(solution)/shard_map/ppermute | solution.py:353
  97.8 5.0 %collective-permute-start.22 = (bf16[8,32,256]{2,1,0:T(8,128)(2,1)S(1)}, bf16[8,32,256]{2,1,0:T(8,128)(2,1)S(1)}, u32[]{:S(2)}, u32[]{:S(2)}) collective-permute-start(bf16[8,32,256]{2,1,0:T(8,128)(2,1)S(1)} %fusion.7), channel_id=1, source_target_pairs={{0,16},{4,20},{8,24},{12,28},{16,0},{20,4},{24,8},{28,12},{1,17},{... | collective-permute-start | bytes 393224 | tf_op jit(solution)/shard_map/ppermute | solution.py:458
  99.5 5.0 %collective-permute-start.24 = (bf16[8,32,256]{2,1,0:T(8,128)(2,1)S(1)}, bf16[8,32,256]{2,1,0:T(8,128)(2,1)S(1)}, u32[]{:S(2)}, u32[]{:S(2)}) collective-permute-start(bf16[8,32,256]{2,1,0:T(8,128)(2,1)S(1)} %fusion.8), channel_id=1, source_target_pairs={{0,8},{4,12},{8,0},{12,4},{16,24},{20,28},{24,16},{28,20},{1,9},{5... | collective-permute-start | bytes 393224 | tf_op jit(solution)/shard_map/ppermute | solution.py:458
  102.9 9.1 %collective-permute-start.26 = (bf16[4,32,256]{2,1,0:T(8,128)(2,1)S(1)}, bf16[4,32,256]{2,1,0:T(8,128)(2,1)S(1)}, u32[]{:S(2)}, u32[]{:S(2)}) collective-permute-start(bf16[4,32,256]{2,1,0:T(8,128)(2,1)S(1)} %slice.131.refs_2_), channel_id=1, source_target_pairs={{0,1},{1,2},{2,3},{3,0},{4,5},{5,6},{6,7},{7,4},{8,9},{9,10},{10,1... | collective-permute-start | bytes 196616 | tf_op jit(solution)/shard_map/ppermute | solution.py:353
  104.5 7.5 %collective-permute-start.28 = (bf16[4,32,256]{2,1,0:T(8,128)(2,1)S(1)}, bf16[4,32,256]{2,1,0:T(8,128)(2,1)S(1)}, u32[]{:S(2)}, u32[]{:S(2)}) collective-permute-start(bf16[4,32,256]{2,1,0:T(8,128)(2,1)S(1)} %get-tuple-element.70.refs_4_), channel_id=1, source_target_pairs={{0,3},{1,0},{2,1},{3,2},{4,7},{5,4},{6,5},{7,6},{8,11},{9,8},{10,9... | collective-permute-start | bytes 196616 | tf_op jit(solution)/shard_map/ppermute | solution.py:353
  106.8 7.7 %collective-permute-start.27 = (bf16[4,32,256]{2,1,0:T(8,128)(2,1)S(1)}, bf16[4,32,256]{2,1,0:T(8,128)(2,1)S(1)}, u32[]{:S(2)}, u32[]{:S(2)}) collective-permute-start(bf16[4,32,256]{2,1,0:T(8,128)(2,1)S(1)} %get-tuple-element.71.refs_3_), channel_id=1, source_target_pairs={{0,2},{1,3},{2,0},{3,1},{4,6},{5,7},{6,4},{7,5},{8,10},{9,11},{10,... | collective-permute-start | bytes 196616 | tf_op jit(solution)/shard_map/ppermute | solution.py:353
  109.8 9.0 %collective-permute-start.25 = (bf16[128,1024]{1,0:T(8,128)(2,1)S(1)}, bf16[128,1024]{1,0:T(8,128)(2,1)S(1)}, u32[]{:S(2)}, u32[]{:S(2)}) collective-permute-start(bf16[128,1024]{1,0:T(8,128)(2,1)S(1)} %sums.5), channel_id=1, source_target_pairs={{0,3},{1,0},{2,1},{3,2},{4,7},{5,4},{6,5},{7,6},{8,11},{9,8},{10,9... | collective-permute-start | bytes 786440 | tf_op jit(solution)/shard_map/ppermute | solution.py:353

commit v3 on v2

--- a/solution.py
+++ b/solution.py
@@ -301,21 +301,22 @@
     )
 
 
-def join_kernel(count, at_ref, *refs):
+def join_kernel(at_ref, *refs):
     out = refs[-1]
     rows = refs[0].shape[0]
-    for c in range(count):
-        out[c * rows : (c + 1) * rows] = (refs[2 * c][...] + refs[2 * c + 1][...].astype(F32)).astype(BF16)
-
-
-def join(at, pairs):
-    held = [pltpu.with_memory_space_constraint(a, pltpu.VMEM) for pair in pairs for a in pair]
+    for c in range(2):
+        own, up, down = [ref[...].astype(F32) for ref in refs[3 * c : 3 * c + 3]]
+        out[c * rows : (c + 1) * rows] = (own + up + down).astype(BF16)
+
+
+def join(at, halves):
+    held = [pltpu.with_memory_space_constraint(a, pltpu.VMEM) for half in halves for a in half]
     rows, width = held[0].shape
     return pl.pallas_call(
-        functools.partial(join_kernel, len(pairs)),
+        join_kernel,
         in_specs=[SMEM] + [VMEM] * len(held),
         out_specs=VMEM,
-        out_shape=jax.ShapeDtypeStruct((rows * len(pairs), width), BF16),
+        out_shape=jax.ShapeDtypeStruct((rows * 2, width), BF16),
         compiler_params=SMALL,
         cost_estimate=FREE,
         name="join",
@@ -367,40 +368,29 @@
     width, local, out_width = first_factor.shape
     cols = out_width // nz
     kd = width // nd
-    steps = (1, -1)
-    rows = tokens_here // len(steps)
+    rows = tokens_here // 2
     bits = nd.bit_length() - 1
     orders = [list(range(1, bits)), list(range(bits - 1, 0, -1))]
 
-    turn = lambda c, n: (-n * steps[c]) % nz
-    xs = [[inputs[c * rows : (c + 1) * rows]] + [None] * (nz - 1) for c in range(len(steps))]
-    for c in range(len(steps)):
-        xs[c][turn(c, 1)] = ring_step(xs[c][0], steps[c], nz)
-
-    def pass_on(n, *earlier, also=(), stored=()):
-        arrived = [xs[c][turn(c, n - 1)] for c in range(len(steps))]
-        came = after(at, arrived + list(also), mark(at, arrived), *earlier, stored=stored)
-        for c in range(len(steps)):
-            xs[c][turn(c, n - 1)] = came[c]
-            xs[c][turn(c, n)] = ring_step(came[c], steps[c], nz)
-        return came[len(steps) :]
-
+    xs = [[inputs[c * rows : (c + 1) * rows]] + [None] * (nz - 1) for c in range(2)]
+    xs[0][3] = ring_step(xs[0][0], 1, nz)
+    xs[0][1] = ring_step(xs[0][0], -1, nz)
     second = second_factor.transpose(1, 0, 2)
     sends = cut(at, first_factor, nz, nd)
     got = [ring_step(sends[r - 1], -r, nz) for r in range(1, nz)]
-    if nz > 2:
-        pass_on(2, *got, stored=[second])
-    others = halved(at, got, *[xs[c][turn(c, 1)] for c in range(len(steps))])
+    near = mark(at, [xs[0][3], xs[0][1]])
+    xs[0][3], xs[1][0] = after(at, [xs[0][3], xs[1][0]], near, *got, stored=[second])
+    xs[0][2] = ring_step(xs[0][3], 1, nz)
+    xs[1][1] = ring_step(xs[1][0], -1, nz)
+    xs[1][3] = ring_step(xs[1][0], 1, nz)
+
+    others = halved(at, got, xs[0][3])
     for k in range(max(bits - 1, 1)):
         if bits > 1:
             others = [double_over_dp(o, order[k], d, nd) for o, order in zip(others, orders)]
         if k == 0:
             cot = turned(cotangent, others[0])
             own = own_columns(at, first_factor, others[1], nz)
-            if nz > 3:
-                others = pass_on(3, own, cot, also=others)
-    for n in range(4, nz):
-        pass_on(n)
     pieces = []
     for o in others:
         pieces += [o, lax.ppermute(o, "dp", swap(0, nd))]
@@ -411,30 +401,20 @@
         [own] + pieces,
         [((nz * local, width, cols), BF16)],
     )[0]
-
-    parts, ogs = [], []
-    for c in range(len(steps)):
-        later = [mark(at, [x[turn(i, nz - 1)] for i, x in enumerate(xs)])] if c == 0 else []
-        res = layer(at, xs[c], first, second, cot, later, c, rows, nz, local, width, cols)
-        parts.append(res[:nz])
-        ogs.append(res[nz])
-        second = res[-1] if c == 0 else second
-    ring = [ring_step(parts[0][turn(0, 1)], steps[0], nz), None]
-
-    def ring_next(n, *earlier):
-        pairs, whose = [], []
-        if n < nz:
-            pairs.append((parts[0][turn(0, n)], ring[0]))
-            whose.append(0)
-        pairs.append((parts[1][turn(1, n - 1)], ring[1]))
-        whose.append(1)
-        sent = sums(at, pairs, *earlier)
-        for c, send in zip(whose, sent):
-            ring[c] = ring_step(send, steps[c], nz)
-        return sent
-
-    sent = ring_next(2)
-    give, keep = first_grad_terms(at, xs, ogs, sent, nz, local, width, cols, nd)
+    far = mark(at, [xs[0][2], xs[1][1], xs[1][3]])
+    (xs[1][1],) = after(at, [xs[1][1]], far)
+    xs[1][2] = ring_step(xs[1][1], -1, nz)
+
+    low = layer(at, xs[0], first, second, cot, [xs[1][1]], 0, rows, nz, local, width, cols)
+    low_far = ring_step(low[2], 1, nz)
+    low_down = ring_step(low[3], -1, nz)
+    high = layer(at, xs[1], first, low[-1], cot, [], 1, rows, nz, local, width, cols)
+    high_far = ring_step(high[2], -1, nz)
+    high_up = ring_step(high[1], 1, nz)
+    sent = sums(at, [(low[1], low_far)], mark(at, [low_far, low_down]))
+    low_up = ring_step(sent[0], 1, nz)
+
+    give, keep = first_grad_terms(at, xs, [low[nz], high[nz]], sent, nz, local, width, cols, nd)
     got = lax.ppermute(give, "dp", swap(0, nd))
     keep = keep.reshape([2] * (bits - 1) + list(keep.shape[1:]))
     got = got.reshape(keep.shape)
@@ -452,17 +432,15 @@
             pick = lambda n: lax.index_in_dim(totals[i], n, axis, keepdims=False)
             give.append(pick(1).astype(BF16))
             totals[i] = pick(0)
-        if k == 0 and nz > 2:
-            ring_next(3, *give)
         for i in range(2):
             totals[i] = totals[i] + lax.ppermute(give[i], "dp", swap(orders[i][k], nd)).astype(F32)
+    sent = sums(at, [(high[3], high_far)], mark(at, [high_far, high_up, low_up]), *give)
+    high_down = ring_step(sent[0], -1, nz)
     blocks = jnp.concatenate(totals, axis=0).reshape(nz, local, kd, cols)
     give = [blocks[r].astype(BF16) for r in range(1, nz)]
     pieces = [blocks[0]] + [ring_step(give[r - 1], r, nz) for r in range(1, nz)]
-    for n in range(4, nz + 1):
-        ring_next(n, *give, ring[0])
     first_sum = place(at, pieces, (tokens_here * nd) ** (-0.5))
-    return join(at, [(parts[c][0], ring[c]) for c in range(len(steps))]), first_sum
+    return join(at, [(low[0], low_up, low_down), (high[0], high_up, high_down)]), first_sum
 
 
 def plain_body(inputs, first_factor, second_factor, cotangent):
@@ -496,7 +474,7 @@
 
     def run(inputs, first_factor, second_factor, cotangent):
         width, local, _ = first_factor.shape
-        fits = local % 2 == 0 and width % (16 * nd) == 0 and nd & (nd - 1) == 0
+        fits = nz == 4 and local % 2 == 0 and width % (16 * nd) == 0 and nd & (nd - 1) == 0
         return (body if fits else plain_body)(inputs, first_factor, second_factor, cotangent)
 
     return jax.shard_map(

time: 121 us -> 112 us (0.926)
  waiting for transfers between devices: 36.7 us -> 24.6 us
  starting transfers between devices: 39.6 us -> 43.2 us
    ppermute x18, waiting for transfers between devices: 29.4 us -> 7.22 us  [ring_step(): lax.ppermute(value, 'tensor', [(i, (i + step) % nz) for i in range(nz)])]
    ppermute x4, waiting for transfers between devices: 4.3 us -> 8.5 us  [body(): lax.ppermute(give[i], 'dp', swap(orders[i][k], nd)).astype(F32)]
    ppermute x18, starting transfers between devices: 29.8 us -> 33.5 us  [ring_step(): lax.ppermute(value, 'tensor', [(i, (i + step) % nz) for i in range(nz)])]
    ppermute x4, waiting for transfers between devices: 2.97 us -> 6.24 us  [double_over_dp(): got = lax.ppermute(part, 'dp', swap(bit, nd))]
    ppermute x1, waiting for transfers between devices: 0.01 us -> 2.65 us  [body(): got = lax.ppermute(give, 'dp', swap(0, nd))]
    pallas_call x10 -> x9, Pallas kernels: 19.5 us -> 18.8 us  [on_chip(): pl.pallas_call(kernel, in_specs=[SMEM] + [VMEM] * len(operands) + [pl.Blo...]
    pallas_call x4 -> x5, Pallas kernels: 2.17 us -> 2.71 us  [mark(): pl.pallas_call(mark_kernel, in_specs=[SMEM] + [VMEM] * len(held), out_spe...]
  transfers between devices with their start and end apart: 29 -> 29, of which waited for: 15 -> 12; matrix products, arithmetic and copies ran while one was open for 9% -> 9% of each run, Pallas kernels for 12% -> 21%
where the time goes in v3:
time: 112 us
  starting transfers between devices  43.2 us (39%)
  Pallas kernels  28.5 us (25%)
  waiting for transfers between devices  24.6 us (22%)
  local copies, waits for them, and re-layouts  13.4 us (12%)
    ppermute x18, starting transfers between devices, ring_step(): lax.ppermute(value, 'tensor', [(i, (i + step) % nz) for i in range(nz)])  33.5 us
    pallas_call x9, Pallas kernels, on_chip(): pl.pallas_call(kernel, in_specs=[SMEM] + [VMEM] * len(operands) + [pl.Blo...  18.8 us
    unnamed x11, local copies, waits for them, and re-layouts  12.2 us
    ppermute x4, waiting for transfers between devices, body(): lax.ppermute(give[i], 'dp', swap(orders[i][k], nd)).astype(F32)  8.5 us
    ppermute x18, waiting for transfers between devices, ring_step(): lax.ppermute(value, 'tensor', [(i, (i + step) % nz) for i in range(nz)])  7.22 us
    ppermute x4, waiting for transfers between devices, double_over_dp(): got = lax.ppermute(part, 'dp', swap(bit, nd))  6.24 us
    ppermute x4, starting transfers between devices, body(): lax.ppermute(give[i], 'dp', swap(orders[i][k], nd)).astype(F32)  5.28 us
    ppermute x4, starting transfers between devices, double_over_dp(): got = lax.ppermute(part, 'dp', swap(bit, nd))  4.25 us
  transfers between devices with their start and end apart: 29, of which 12 were waited for; matrix products, arithmetic and copies ran while one was open for 9% of the time, Pallas kernels for 21%

profile of v3, /device:TPU:0, one launch (start us, length us, event | category | flops | bytes accessed | tf_op | source)
XLA Modules:
  0.0 111.7 jit_solution(4776721401340881162)
XLA Ops:
  0.6 1.1 fusion.9
  1.7 5.1 %collective-permute-start = (bf16[128,1024]{1,0:T(8,128)(2,1)S(1)}, bf16[128,1024]{1,0:T(8,128)(2,1)S(1)}, u32[]{:S(2)}, u32[]{:S(2)}) collective-permute-start(bf16[128,1024]{1,0:T(8,128)(2,1)S(1)} %get-tuple-element.45.refs_0_), channel_id=1, source_target_pairs={{0,3},{1,0},{2,1},{3,2},{4,7},{5,4},{6,5},{7,6},{8,11},{9,8},{10,9... | collective-permute-start | bytes 786440 | tf_op jit(solution)/shard_map/ppermute | solution.py:354
  6.8 0.1 pad_add_fusion.at_ref
  6.9 1.6 %copy-done = bf16[256,4,1024]{2,1,0:T(4,128)(2,1)S(1)} copy-done((bf16[256,4,1024]{2,1,0:T(4,128)(2,1)S(1)}, bf16[256,4,1024]{2,1,0:T(4,128)(2,1)}, u32[]{:S(2)}) %copy-start) | copy-done | bytes 2097176
  8.5 0.8 cut.1
  9.3 3.9 %collective-permute-start.2 = (bf16[4,32,256]{2,1,0:T(8,128)(2,1)S(1)}, bf16[4,32,256]{2,1,0:T(8,128)(2,1)S(1)}, u32[]{:S(2)}, u32[]{:S(2)}) collective-permute-start(bf16[4,32,256]{2,1,0:T(8,128)(2,1)S(1)} %get-tuple-element.22), channel_id=1, source_target_pairs={{0,3},{1,0},{2,1},{3,2},{4,7},{5,4},{6,5},{7,6},{8,11},{9,8},{10,9... | collective-permute-start | bytes 196616 | tf_op jit(solution)/shard_map/ppermute | solution.py:354
  13.2 0.6 collective-permute-start.4
  13.8 9.5 %copy.10 = bf16[1024,4,1024]{2,0,1:T(8,128)(2,1)} copy(bf16[1024,4,1024]{2,1,0:T(4,128)(2,1)} %param.6) | data formatting | bytes 16777216 | tf_op args[2]
  23.4 0.5 mark.5.refs_2_
  23.9 0.1 copy-done.3
  24.1 0.9 copy-done.4
  25.0 0.6 after.2
  25.6 0.6 halved.1
  26.2 1.6 %collective-permute-start.6 = (bf16[6,32,256]{2,1,0:T(8,128)(2,1)S(1)}, bf16[6,32,256]{2,1,0:T(8,128)(2,1)S(1)}, u32[]{:S(2)}, u32[]{:S(2)}) collective-permute-start(bf16[6,32,256]{2,1,0:T(8,128)(2,1)S(1)} %get-tuple-element.26), channel_id=1, source_target_pairs={{0,16},{4,20},{8,24},{12,28},{16,0},{20,4},{24,8},{28,12},{1,17},{... | collective-permute-start | bytes 294920 | tf_op jit(solution)/shard_map/ppermute | solution.py:358
  27.8 2.8 %collective-permute-start.5 = (bf16[128,1024]{1,0:T(8,128)(2,1)S(1)}, bf16[128,1024]{1,0:T(8,128)(2,1)S(1)}, u32[]{:S(2)}, u32[]{:S(2)}) collective-permute-start(bf16[128,1024]{1,0:T(8,128)(2,1)S(1)} %get-tuple-element.25.refs_3_), channel_id=1, source_target_pairs={{0,1},{1,2},{2,3},{3,0},{4,5},{5,6},{6,7},{7,4},{8,9},{9,10},{10,1... | collective-permute-start | bytes 786440 | tf_op jit(solution)/shard_map/ppermute | solution.py:354
  30.7 3.8 %collective-permute-start.12 = (bf16[128,1024]{1,0:T(8,128)(2,1)S(1)}, bf16[128,1024]{1,0:T(8,128)(2,1)S(1)}, u32[]{:S(2)}, u32[]{:S(2)}) collective-permute-start(bf16[128,1024]{1,0:T(8,128)(2,1)S(1)} %get-tuple-element.28.refs_0_.refs_4_), channel_id=1, source_target_pairs={{0,3},{1,0},{2,1},{3,2},{4,7},{5,4},{6,5},{7,6},{8,11},{9,8},{10,9... | collective-permute-start | bytes 786440 | tf_op jit(solution)/shard_map/ppermute | solution.py:354
  34.4 1.5 %collective-permute-start.7 = (bf16[6,32,256]{2,1,0:T(8,128)(2,1)S(1)}, bf16[6,32,256]{2,1,0:T(8,128)(2,1)S(1)}, u32[]{:S(2)}, u32[]{:S(2)}) collective-permute-start(bf16[6,32,256]{2,1,0:T(8,128)(2,1)S(1)} %get-tuple-element.27), channel_id=1, source_target_pairs={{0,8},{4,12},{8,0},{12,4},{16,24},{20,28},{24,16},{28,20},{1,9},{5... | collective-permute-start | bytes 294920 | tf_op jit(solution)/shard_map/ppermute | solution.py:358
  36.0 0.6 collective-permute-start.10
  36.6 2.5 %collective-permute-done.7 = bf16[6,32,256]{2,1,0:T(8,128)(2,1)S(1)} collective-permute-done((bf16[6,32,256]{2,1,0:T(8,128)(2,1)S(1)}, bf16[6,32,256]{2,1,0:T(8,128)(2,1)S(1)}, u32[]{:S(2)}, u32[]{:S(2)}) %collective-permute-start.7) | collective-permute-done | bytes 98336 | tf_op jit(solution)/shard_map/ppermute | solution.py:358
  39.1 2.0 %own_columns.1.own_ref = bf16[4,256,256]{2,1,0:T(8,128)(2,1)S(1)} custom-call(s32[2]{0:T(128)S(1)} %pad_add_fusion.at_ref, bf16[256,4,1024]{2,1,0:T(4,128)(2,1)S(1)} %copy-done.1, bf16[2,6,32,256]{3,2,1,0:T(8,128)(2,1)S(1)} %pad_maximum_fusion.2.later_ref), custom_call_target="tpu_custom_call" | custom-call | tf_op jit(solution)/shard_map/own_columns/pallas_call | solution.py:80
  41.1 0.6 collective-permute-start.8
  41.7 1.2 %turned.1.refs_5_ = bf16[256,4096]{1,0:T(8,128)(2,1)S(1)} custom-call(bf16[4096,256]{1,0:T(8,128)(2,1)S(1)} %copy-done.2, bf16[2,6,32,256]{3,2,1,0:T(8,128)(2,1)S(1)} %pad_maximum_fusion.3.later_ref), custom_call_target="tpu_custom_call" | custom-call | tf_op jit(solution)/shard_map/turned/pallas_call | solution.py:101
  43.0 0.1 collective-permute-start.11
  43.1 3.8 %collective-permute-done.8 = bf16[2,6,32,256]{3,2,1,0:T(8,128)(2,1)S(1)} collective-permute-done((bf16[2,6,32,256]{3,2,1,0:T(8,128)(2,1)S(1)}, bf16[2,6,32,256]{3,2,1,0:T(8,128)(2,1)S(1)}, u32[]{:S(2)}, u32[]{:S(2)}) %collective-permute-start.8) | collective-permute-done | bytes 196640 | tf_op jit(solution)/shard_map/ppermute | solution.py:358
  46.9 0.1 collective-permute-start.9
  47.0 0.9 collective-permute-done.12.refs_1_.refs_0_
  48.0 0.5 mark.6.refs_1_
  48.5 0.6 after.3.refs_6_.refs_1_.refs_5_
  49.1 2.1 %collective-permute-start.17 = (bf16[128,1024]{1,0:T(8,128)(2,1)S(1)}, bf16[128,1024]{1,0:T(8,128)(2,1)S(1)}, u32[]{:S(2)}, u32[]{:S(2)}) collective-permute-start(bf16[128,1024]{1,0:T(8,128)(2,1)S(1)} %after.3.refs_6_.refs_1_.refs_5_), channel_id=1, source_target_pairs={{0,3},{1,0},{2,1},{3,2},{4,7},{5,4},{6,5},{7,6},{8,11},{9,8},{10,9... | collective-permute-start | bytes 786440 | tf_op jit(solution)/shard_map/ppermute | solution.py:354
  51.2 0.7 assemble.1.refs_4_
  51.9 7.9 %layer.2 = (f32[128,1024]{1,0:T(8,128)S(1)}, bf16[128,1024]{1,0:T(8,128)(2,1)S(1)}, bf16[128,1024]{1,0:T(8,128)(2,1)S(1)}, bf16[128,1024]{1,0:T(8,128)(2,1)S(1)}...) custom-call(s32[2]{0:T(128)S(1)} %pad_add_fusion.at_ref, ...), custom_call_target="tpu_custom_call" | custom-call | tf_op jit(solution)/shard_map/layer/pallas_call | solution.py:35
  59.8 0.1 collective-permute-start.14
  59.8 3.8 %collective-permute-start.15 = (bf16[128,1024]{1,0:T(8,128)(2,1)S(1)}, bf16[128,1024]{1,0:T(8,128)(2,1)S(1)}, u32[]{:S(2)}, u32[]{:S(2)}) collective-permute-start(bf16[128,1024]{1,0:T(8,128)(2,1)S(1)} %get-tuple-element.32), channel_id=1, source_target_pairs={{0,3},{1,0},{2,1},{3,2},{4,7},{5,4},{6,5},{7,6},{8,11},{9,8},{10,9... | collective-permute-start | bytes 786440 | tf_op jit(solution)/shard_map/ppermute | solution.py:354
  63.6 5.9 %layer.3 = (f32[128,1024]{1,0:T(8,128)S(1)}, bf16[128,1024]{1,0:T(8,128)(2,1)S(1)}, bf16[128,1024]{1,0:T(8,128)(2,1)S(1)}, bf16[128,1024]{1,0:T(8,128)(2,1)S(1)}, bf16[4,128,1024]{2,1,0:T(8,128)(2,1)S(1)}) custom-call(s32[2]{0:T(128)S(1)} %pad_add_fusion.at_ref, bf16[128,1024]{1,0:T(8,128)(2,1)S(1)} %get-tuple-element.28.refs_0_.refs_4_, ...), custom_call_target="tpu_custom_call" | custom-call | tf_op jit(solution)/shard_map/layer/pallas_call | solution.py:35
  69.6 1.0 collective-permute-done.14.refs_0_.refs_1_
  70.6 2.4 %collective-permute-done.15.refs_1_.refs_2_ = bf16[128,1024]{1,0:T(8,128)(2,1)S(1)} collective-permute-done((bf16[128,1024]{1,0:T(8,128)(2,1)S(1)}, bf16[128,1024]{1,0:T(8,128)(2,1)S(1)}, u32[]{:S(2)}, u32[]{:S(2)}) %collective-permute-start.15) | collective-permute-done | bytes 262176 | tf_op jit(solution)/shard_map/ppermute | solution.py:354
  73.0 0.5 mark.7.refs_2_
  73.5 0.6 sums.2.refs_10_
  74.1 1.4 %first_grad_terms.1 = (bf16[4,16,32,256]{3,2,1,0:T(8,128)(2,1)S(1)}, bf16[4,16,32,256]{3,2,1,0:T(8,128)(2,1)S(1)}) custom-call(s32[2]{0:T(128)S(1)} %pad_add_fusion.at_ref, bf16[128,1024]{1,0:T(8,128)(2,1)S(1)} %get-tuple-element.45.refs_0_, bf16[128,1024]{1,0:T(8,128)(2,1)S(1)} %collective-permute-done.refs_1_, ...), custom_call_target="tpu_custom_call" | custom-call | tf_op jit(solution)/shard_map/first_grad_terms/pallas_call | solution.py:35
  75.5 0.1 collective-permute-start.20
  75.6 2.6 %collective-permute-done.20 = bf16[4,16,32,256]{3,2,1,0:T(8,128)(2,1)S(1)} collective-permute-done((bf16[4,16,32,256]{3,2,1,0:T(8,128)(2,1)S(1)}, bf16[4,16,32,256]{3,2,1,0:T(8,128)(2,1)S(1)}, u32[]{:S(2)}, u32[]{:S(2)}) %collective-permute-start.20) | collective-permute-done | bytes 1048608 | tf_op jit(solution)/shard_map/ppermute | solution.py:418
  78.2 0.4 convert_add_fusion
  78.7 0.6 collective-permute-start.22
  79.3 0.7 collective-permute-start.18
  80.0 3.1 %collective-permute-start.19 = (bf16[128,1024]{1,0:T(8,128)(2,1)S(1)}, bf16[128,1024]{1,0:T(8,128)(2,1)S(1)}, u32[]{:S(2)}, u32[]{:S(2)}) collective-permute-start(bf16[128,1024]{1,0:T(8,128)(2,1)S(1)} %get-tuple-element.37), channel_id=1, source_target_pairs={{0,3},{1,0},{2,1},{3,2},{4,7},{5,4},{6,5},{7,6},{8,11},{9,8},{10,9... | collective-permute-start | bytes 786440 | tf_op jit(solution)/shard_map/ppermute | solution.py:354
  83.1 1.6 %collective-permute-start.21 = (bf16[2,8,32,256]{3,2,1,0:T(8,128)(2,1)S(1)}, bf16[2,8,32,256]{3,2,1,0:T(8,128)(2,1)S(1)}, u32[]{:S(2)}, u32[]{:S(2)}) collective-permute-start(bf16[2,8,32,256]{3,2,1,0:T(8,128)(2,1)S(1)} %fusion.2), channel_id=1, source_target_pairs={{0,8},{4,12},{8,0},{12,4},{16,24},{20,28},{24,16},{28,20},{1,9},{5... | collective-permute-start | bytes 786440 | tf_op jit(solution)/shard_map/ppermute | solution.py:436
  84.7 2.4 %collective-permute-done.22 = bf16[2,8,32,256]{3,2,1,0:T(8,128)(2,1)S(1)} collective-permute-done((bf16[2,8,32,256]{3,2,1,0:T(8,128)(2,1)S(1)}, bf16[2,8,32,256]{3,2,1,0:T(8,128)(2,1)S(1)}, u32[]{:S(2)}, u32[]{:S(2)}) %collective-permute-start.22) | collective-permute-done | bytes 262176 | tf_op jit(solution)/shard_map/ppermute | solution.py:436
  87.1 0.1 fusion
  87.2 1.6 %collective-permute-start.26 = (bf16[8,32,256]{2,1,0:T(8,128)(2,1)S(1)}, bf16[8,32,256]{2,1,0:T(8,128)(2,1)S(1)}, u32[]{:S(2)}, u32[]{:S(2)}) collective-permute-start(bf16[8,32,256]{2,1,0:T(8,128)(2,1)S(1)} %fusion.8.refs_4_), channel_id=1, source_target_pairs={{0,8},{4,12},{8,0},{12,4},{16,24},{20,28},{24,16},{28,20},{1,9},{5... | collective-permute-start | bytes 393224 | tf_op jit(solution)/shard_map/ppermute | solution.py:436
  88.8 3.3 %collective-permute-done.21 = bf16[2,8,32,256]{3,2,1,0:T(8,128)(2,1)S(1)} collective-permute-done((bf16[2,8,32,256]{3,2,1,0:T(8,128)(2,1)S(1)}, bf16[2,8,32,256]{3,2,1,0:T(8,128)(2,1)S(1)}, u32[]{:S(2)}, u32[]{:S(2)}) %collective-permute-start.21) | collective-permute-done | bytes 262176 | tf_op jit(solution)/shard_map/ppermute | solution.py:436
  92.1 0.1 fusion.1
  92.2 1.6 %collective-permute-start.24 = (bf16[8,32,256]{2,1,0:T(8,128)(2,1)S(1)}, bf16[8,32,256]{2,1,0:T(8,128)(2,1)S(1)}, u32[]{:S(2)}, u32[]{:S(2)}) collective-permute-start(bf16[8,32,256]{2,1,0:T(8,128)(2,1)S(1)} %fusion.7.refs_3_), channel_id=1, source_target_pairs={{0,16},{4,20},{8,24},{12,28},{16,0},{20,4},{24,8},{28,12},{1,17},{... | collective-permute-start | bytes 393224 | tf_op jit(solution)/shard_map/ppermute | solution.py:436
  93.9 0.6 collective-permute-start.27
  94.5 2.8 %collective-permute-done.24 = bf16[8,32,256]{2,1,0:T(8,128)(2,1)S(1)} collective-permute-done((bf16[8,32,256]{2,1,0:T(8,128)(2,1)S(1)}, bf16[8,32,256]{2,1,0:T(8,128)(2,1)S(1)}, u32[]{:S(2)}, u32[]{:S(2)}) %collective-permute-start.24) | collective-permute-done | bytes 131104 | tf_op jit(solution)/shard_map/ppermute | solution.py:436
  97.2 3.5 %collective-permute-start.28 = (bf16[4,32,256]{2,1,0:T(8,128)(2,1)S(1)}, bf16[4,32,256]{2,1,0:T(8,128)(2,1)S(1)}, u32[]{:S(2)}, u32[]{:S(2)}) collective-permute-start(bf16[4,32,256]{2,1,0:T(8,128)(2,1)S(1)} %get-tuple-element.54), channel_id=1, source_target_pairs={{0,3},{1,0},{2,1},{3,2},{4,7},{5,4},{6,5},{7,6},{8,11},{9,8},{10,9... | collective-permute-start | bytes 196616 | tf_op jit(solution)/shard_map/ppermute | solution.py:354
  100.9 0.7 collective-permute-done.16.refs_2_.refs_1_
  101.6 0.5 mark.8.refs_2_
  102.2 0.6 sums.3
  102.8 3.2 %collective-permute-start.23 = (bf16[128,1024]{1,0:T(8,128)(2,1)S(1)}, bf16[128,1024]{1,0:T(8,128)(2,1)S(1)}, u32[]{:S(2)}, u32[]{:S(2)}) collective-permute-start(bf16[128,1024]{1,0:T(8,128)(2,1)S(1)} %sums.3), channel_id=1, source_target_pairs={{0,3},{1,0},{2,1},{3,2},{4,7},{5,4},{6,5},{7,6},{8,11},{9,8},{10,9... | collective-permute-start | bytes 786440 | tf_op jit(solution)/shard_map/ppermute | solution.py:354
  106.0 1.7 %collective-permute-done.25.refs_0_.refs_1_ = bf16[4,32,256]{2,1,0:T(8,128)(2,1)S(1)} collective-permute-done((bf16[4,32,256]{2,1,0:T(8,128)(2,1)S(1)}, bf16[4,32,256]{2,1,0:T(8,128)(2,1)S(1)}, u32[]{:S(2)}, u32[]{:S(2)}) %collective-permute-start.25) | collective-permute-done | bytes 65568 | tf_op jit(solution)/shard_map/ppermute | solution.py:354
  107.6 0.5 mark.9.refs_4_
  108.2 1.5 %place.1 = f32[32,4,1024]{2,1,0:T(4,128)} custom-call(s32[2]{0:T(128)S(1)} %pad_add_fusion.at_ref, f32[4,32,256]{2,1,0:T(8,128)S(1)} %slice.98.refs_0_, bf16[4,32,256]{2,1,0:T(8,128)(2,1)S(1)} %collective-permute-done.25.refs_0_.refs_1_, bf16[4,32,256]{2,1,0:T(8,128)(2,1)S(1)} %collective-permute-done.27.refs_1_.refs_2_, ...), custom_call_target="tpu_custom_call" | custom-call | tf_op jit(solution)/shard_map/place/pallas_call | solution.py:338
  109.7 0.5 collective-permute-done.23.refs_5_
  110.2 1.5 %join.1 = bf16[256,1024]{1,0:T(8,128)(2,1)} custom-call(s32[2]{0:T(128)S(1)} %pad_add_fusion.at_ref, f32[128,1024]{1,0:T(8,128)S(1)} %get-tuple-element.29.refs_0_, bf16[128,1024]{1,0:T(8,128)(2,1)S(1)} %collective-permute-done.16.refs_2_.refs_1_, bf16[128,1024]{1,0:T(8,128)(2,1)S(1)} %collective-permute-done.15.refs_1_.refs_2_, ...), custom_call_target="tpu_custom_call" | custom-call | tf_op jit(solution)/shard_map/join/pallas_call | solution.py:315
  (46 shorter events, 0.6 us)
Async XLA Ops:
  1.7 21.7 %collective-permute-start = (bf16[128,1024]{1,0:T(8,128)(2,1)S(1)}, bf16[128,1024]{1,0:T(8,128)(2,1)S(1)}, u32[]{:S(2)}, u32[]{:S(2)}) collective-permute-start(bf16[128,1024]{1,0:T(8,128)(2,1)S(1)} %get-tuple-element.45.refs_0_), channel_id=1, source_target_pairs={{0,3},{1,0},{2,1},{3,2},{4,7},{5,4},{6,5},{7,6},{8,11},{9,8},{10,9... | collective-permute-start | bytes 786440 | tf_op jit(solution)/shard_map/ppermute | solution.py:354
  6.8 16.6 %collective-permute-start.1 = (bf16[128,1024]{1,0:T(8,128)(2,1)S(1)}, bf16[128,1024]{1,0:T(8,128)(2,1)S(1)}, u32[]{:S(2)}, u32[]{:S(2)}) collective-permute-start(bf16[128,1024]{1,0:T(8,128)(2,1)S(1)} %get-tuple-element.45.refs_0_), channel_id=1, source_target_pairs={{0,1},{1,2},{2,3},{3,0},{4,5},{5,6},{6,7},{7,4},{8,9},{9,10},{10,1... | collective-permute-start | bytes 786440 | tf_op jit(solution)/shard_map/ppermute | solution.py:354
  6.9 1.6 %copy-start = (bf16[256,4,1024]{2,1,0:T(4,128)(2,1)S(1)}, bf16[256,4,1024]{2,1,0:T(4,128)(2,1)}, u32[]{:S(2)}) copy-start(bf16[256,4,1024]{2,1,0:T(4,128)(2,1)} %f_ref.3) | copy-start | bytes 6291460
  9.3 14.8 %collective-permute-start.2 = (bf16[4,32,256]{2,1,0:T(8,128)(2,1)S(1)}, bf16[4,32,256]{2,1,0:T(8,128)(2,1)S(1)}, u32[]{:S(2)}, u32[]{:S(2)}) collective-permute-start(bf16[4,32,256]{2,1,0:T(8,128)(2,1)S(1)} %get-tuple-element.22), channel_id=1, source_target_pairs={{0,3},{1,0},{2,1},{3,2},{4,7},{5,4},{6,5},{7,6},{8,11},{9,8},{10,9... | collective-permute-start | bytes 196616 | tf_op jit(solution)/shard_map/ppermute | solution.py:354
  13.2 10.9 %collective-permute-start.3 = (bf16[4,32,256]{2,1,0:T(8,128)(2,1)S(1)}, bf16[4,32,256]{2,1,0:T(8,128)(2,1)S(1)}, u32[]{:S(2)}, u32[]{:S(2)}) collective-permute-start(bf16[4,32,256]{2,1,0:T(8,128)(2,1)S(1)} %get-tuple-element.23), channel_id=1, source_target_pairs={{0,2},{1,3},{2,0},{3,1},{4,6},{5,7},{6,4},{7,5},{8,10},{9,11},{10,... | collective-permute-start | bytes 196616 | tf_op jit(solution)/shard_map/ppermute | solution.py:354
  13.2 10.9 %collective-permute-start.4 = (bf16[4,32,256]{2,1,0:T(8,128)(2,1)S(1)}, bf16[4,32,256]{2,1,0:T(8,128)(2,1)S(1)}, u32[]{:S(2)}, u32[]{:S(2)}) collective-permute-start(bf16[4,32,256]{2,1,0:T(8,128)(2,1)S(1)} %get-tuple-element.24), channel_id=1, source_target_pairs={{0,1},{1,2},{2,3},{3,0},{4,5},{5,6},{6,7},{7,4},{8,9},{9,10},{10,1... | collective-permute-start | bytes 196616 | tf_op jit(solution)/shard_map/ppermute | solution.py:354
  23.4 0.7 copy-start.3
  24.1 1.0 copy-start.4
  25.0 14.0 %copy-start.1 = (bf16[256,4,1024]{2,1,0:T(4,128)(2,1)S(1)}, bf16[256,4,1024]{2,1,0:T(4,128)(2,1)}, u32[]{:S(2)}) copy-start(bf16[256,4,1024]{2,1,0:T(4,128)(2,1)} %f_ref.3) | copy-start | bytes 6291460
  26.2 9.8 %collective-permute-start.6 = (bf16[6,32,256]{2,1,0:T(8,128)(2,1)S(1)}, bf16[6,32,256]{2,1,0:T(8,128)(2,1)S(1)}, u32[]{:S(2)}, u32[]{:S(2)}) collective-permute-start(bf16[6,32,256]{2,1,0:T(8,128)(2,1)S(1)} %get-tuple-element.26), channel_id=1, source_target_pairs={{0,16},{4,20},{8,24},{12,28},{16,0},{20,4},{24,8},{28,12},{1,17},{... | collective-permute-start | bytes 294920 | tf_op jit(solution)/shard_map/ppermute | solution.py:358
  27.8 19.3 %collective-permute-start.5 = (bf16[128,1024]{1,0:T(8,128)(2,1)S(1)}, bf16[128,1024]{1,0:T(8,128)(2,1)S(1)}, u32[]{:S(2)}, u32[]{:S(2)}) collective-permute-start(bf16[128,1024]{1,0:T(8,128)(2,1)S(1)} %get-tuple-element.25.refs_3_), channel_id=1, source_target_pairs={{0,1},{1,2},{2,3},{3,0},{4,5},{5,6},{6,7},{7,4},{8,9},{9,10},{10,1... | collective-permute-start | bytes 786440 | tf_op jit(solution)/shard_map/ppermute | solution.py:354
  30.6 16.4 %collective-permute-start.13 = (bf16[128,1024]{1,0:T(8,128)(2,1)S(1)}, bf16[128,1024]{1,0:T(8,128)(2,1)S(1)}, u32[]{:S(2)}, u32[]{:S(2)}) collective-permute-start(bf16[128,1024]{1,0:T(8,128)(2,1)S(1)} %get-tuple-element.28.refs_0_.refs_4_), channel_id=1, source_target_pairs={{0,1},{1,2},{2,3},{3,0},{4,5},{5,6},{6,7},{7,4},{8,9},{9,10},{10,1... | collective-permute-start | bytes 786440 | tf_op jit(solution)/shard_map/ppermute | solution.py:354
  30.7 17.3 %collective-permute-start.12 = (bf16[128,1024]{1,0:T(8,128)(2,1)S(1)}, bf16[128,1024]{1,0:T(8,128)(2,1)S(1)}, u32[]{:S(2)}, u32[]{:S(2)}) collective-permute-start(bf16[128,1024]{1,0:T(8,128)(2,1)S(1)} %get-tuple-element.28.refs_0_.refs_4_), channel_id=1, source_target_pairs={{0,3},{1,0},{2,1},{3,2},{4,7},{5,4},{6,5},{7,6},{8,11},{9,8},{10,9... | collective-permute-start | bytes 786440 | tf_op jit(solution)/shard_map/ppermute | solution.py:354
  34.4 4.6 %collective-permute-start.7 = (bf16[6,32,256]{2,1,0:T(8,128)(2,1)S(1)}, bf16[6,32,256]{2,1,0:T(8,128)(2,1)S(1)}, u32[]{:S(2)}, u32[]{:S(2)}) collective-permute-start(bf16[6,32,256]{2,1,0:T(8,128)(2,1)S(1)} %get-tuple-element.27), channel_id=1, source_target_pairs={{0,8},{4,12},{8,0},{12,4},{16,24},{20,28},{24,16},{28,20},{1,9},{5... | collective-permute-start | bytes 294920 | tf_op jit(solution)/shard_map/ppermute | solution.py:358
  36.0 5.7 %copy-start.2 = (bf16[4096,256]{1,0:T(8,128)(2,1)S(1)}, bf16[4096,256]{1,0:T(8,128)(2,1)}, u32[]{:S(2)}) copy-start(bf16[4096,256]{1,0:T(8,128)(2,1)} %x_ref.1) | copy-start | bytes 6291460
  36.0 6.9 %collective-permute-start.10 = (bf16[2,6,32,256]{3,2,1,0:T(8,128)(2,1)S(1)}, bf16[2,6,32,256]{3,2,1,0:T(8,128)(2,1)S(1)}, u32[]{:S(2)}, u32[]{:S(2)}) collective-permute-start(bf16[2,6,32,256]{3,2,1,0:T(8,128)(2,1)S(1)} %pad_maximum_fusion.2.later_ref), channel_id=1, source_target_pairs={{0,8},{4,12},{8,0},{12,4},{16,24},{20,28},{24,16},{28,20},{1,9},{5... | collective-permute-start | bytes 589832 | tf_op jit(solution)/shard_map/ppermute | solution.py:358
  41.1 5.7 %collective-permute-start.8 = (bf16[2,6,32,256]{3,2,1,0:T(8,128)(2,1)S(1)}, bf16[2,6,32,256]{3,2,1,0:T(8,128)(2,1)S(1)}, u32[]{:S(2)}, u32[]{:S(2)}) collective-permute-start(bf16[2,6,32,256]{3,2,1,0:T(8,128)(2,1)S(1)} %pad_maximum_fusion.3.later_ref), channel_id=1, source_target_pairs={{0,16},{4,20},{8,24},{12,28},{16,0},{20,4},{24,8},{28,12},{1,17},{... | collective-permute-start | bytes 589832 | tf_op jit(solution)/shard_map/ppermute | solution.py:358
  43.0 8.2 %collective-permute-start.11 = (bf16[2,2,6,32,256]{4,3,2,1,0:T(8,128)(2,1)S(1)}, bf16[2,2,6,32,256]{4,3,2,1,0:T(8,128)(2,1)S(1)}, u32[]{:S(2)}, u32[]{:S(2)}) collective-permute-start(bf16[2,2,6,32,256]{4,3,2,1,0:T(8,128)(2,1)S(1)} %pad_maximum_fusion.1.refs_2_), channel_id=1, source_target_pairs={{0,4},{4,0},{8,12},{12,8},{16,20},{20,16},{24,28},{28,24},{1,5},{5... | collective-permute-start | bytes 1179656 | tf_op jit(solution)/shard_map/ppermute | solution.py:396
  46.9 4.3 %collective-permute-start.9 = (bf16[2,2,6,32,256]{4,3,2,1,0:T(8,128)(2,1)S(1)}, bf16[2,2,6,32,256]{4,3,2,1,0:T(8,128)(2,1)S(1)}, u32[]{:S(2)}, u32[]{:S(2)}) collective-permute-start(bf16[2,2,6,32,256]{4,3,2,1,0:T(8,128)(2,1)S(1)} %pad_maximum_fusion.refs_0_), channel_id=1, source_target_pairs={{0,4},{4,0},{8,12},{12,8},{16,20},{20,16},{24,28},{28,24},{1,5},{5... | collective-permute-start | bytes 1179656 | tf_op jit(solution)/shard_map/ppermute | solution.py:396
  49.1 14.6 %collective-permute-start.17 = (bf16[128,1024]{1,0:T(8,128)(2,1)S(1)}, bf16[128,1024]{1,0:T(8,128)(2,1)S(1)}, u32[]{:S(2)}, u32[]{:S(2)}) collective-permute-start(bf16[128,1024]{1,0:T(8,128)(2,1)S(1)} %after.3.refs_6_.refs_1_.refs_5_), channel_id=1, source_target_pairs={{0,3},{1,0},{2,1},{3,2},{4,7},{5,4},{6,5},{7,6},{8,11},{9,8},{10,9... | collective-permute-start | bytes 786440 | tf_op jit(solution)/shard_map/ppermute | solution.py:354
  59.8 10.8 %collective-permute-start.14 = (bf16[128,1024]{1,0:T(8,128)(2,1)S(1)}, bf16[128,1024]{1,0:T(8,128)(2,1)S(1)}, u32[]{:S(2)}, u32[]{:S(2)}) collective-permute-start(bf16[128,1024]{1,0:T(8,128)(2,1)S(1)} %get-tuple-element.31), channel_id=1, source_target_pairs={{0,1},{1,2},{2,3},{3,0},{4,5},{5,6},{6,7},{7,4},{8,9},{9,10},{10,1... | collective-permute-start | bytes 786440 | tf_op jit(solution)/shard_map/ppermute | solution.py:354
  59.8 13.1 %collective-permute-start.15 = (bf16[128,1024]{1,0:T(8,128)(2,1)S(1)}, bf16[128,1024]{1,0:T(8,128)(2,1)S(1)}, u32[]{:S(2)}, u32[]{:S(2)}) collective-permute-start(bf16[128,1024]{1,0:T(8,128)(2,1)S(1)} %get-tuple-element.32), channel_id=1, source_target_pairs={{0,3},{1,0},{2,1},{3,2},{4,7},{5,4},{6,5},{7,6},{8,11},{9,8},{10,9... | collective-permute-start | bytes 786440 | tf_op jit(solution)/shard_map/ppermute | solution.py:354
  75.5 2.7 %collective-permute-start.20 = (bf16[4,16,32,256]{3,2,1,0:T(8,128)(2,1)S(1)}, bf16[4,16,32,256]{3,2,1,0:T(8,128)(2,1)S(1)}, u32[]{:S(2)}, u32[]{:S(2)}) collective-permute-start(bf16[4,16,32,256]{3,2,1,0:T(8,128)(2,1)S(1)} %get-tuple-element.41), channel_id=1, source_target_pairs={{0,4},{4,0},{8,12},{12,8},{16,20},{20,16},{24,28},{28,24},{1,5},{5... | collective-permute-start | bytes 3145736 | tf_op jit(solution)/shard_map/ppermute | solution.py:418
  78.7 8.4 %collective-permute-start.22 = (bf16[2,8,32,256]{3,2,1,0:T(8,128)(2,1)S(1)}, bf16[2,8,32,256]{3,2,1,0:T(8,128)(2,1)S(1)}, u32[]{:S(2)}, u32[]{:S(2)}) collective-permute-start(bf16[2,8,32,256]{3,2,1,0:T(8,128)(2,1)S(1)} %fusion.3), channel_id=1, source_target_pairs={{0,16},{4,20},{8,24},{12,28},{16,0},{20,4},{24,8},{28,12},{1,17},{... | collective-permute-start | bytes 786440 | tf_op jit(solution)/shard_map/ppermute | solution.py:436
  79.3 21.6 %collective-permute-start.18 = (bf16[128,1024]{1,0:T(8,128)(2,1)S(1)}, bf16[128,1024]{1,0:T(8,128)(2,1)S(1)}, u32[]{:S(2)}, u32[]{:S(2)}) collective-permute-start(bf16[128,1024]{1,0:T(8,128)(2,1)S(1)} %get-tuple-element.35), channel_id=1, source_target_pairs={{0,1},{1,2},{2,3},{3,0},{4,5},{5,6},{6,7},{7,4},{8,9},{9,10},{10,1... | collective-permute-start | bytes 786440 | tf_op jit(solution)/shard_map/ppermute | solution.py:354
  80.0 20.9 %collective-permute-start.19 = (bf16[128,1024]{1,0:T(8,128)(2,1)S(1)}, bf16[128,1024]{1,0:T(8,128)(2,1)S(1)}, u32[]{:S(2)}, u32[]{:S(2)}) collective-permute-start(bf16[128,1024]{1,0:T(8,128)(2,1)S(1)} %get-tuple-element.37), channel_id=1, source_target_pairs={{0,3},{1,0},{2,1},{3,2},{4,7},{5,4},{6,5},{7,6},{8,11},{9,8},{10,9... | collective-permute-start | bytes 786440 | tf_op jit(solution)/shard_map/ppermute | solution.py:354
  83.1 18.5 %collective-permute-start.16 = (bf16[128,1024]{1,0:T(8,128)(2,1)S(1)}, bf16[128,1024]{1,0:T(8,128)(2,1)S(1)}, u32[]{:S(2)}, u32[]{:S(2)}) collective-permute-start(bf16[128,1024]{1,0:T(8,128)(2,1)S(1)} %sums.2.refs_10_), channel_id=1, source_target_pairs={{0,1},{1,2},{2,3},{3,0},{4,5},{5,6},{6,7},{7,4},{8,9},{9,10},{10,1... | collective-permute-start | bytes 786440 | tf_op jit(solution)/shard_map/ppermute | solution.py:354
  83.1 9.0 %collective-permute-start.21 = (bf16[2,8,32,256]{3,2,1,0:T(8,128)(2,1)S(1)}, bf16[2,8,32,256]{3,2,1,0:T(8,128)(2,1)S(1)}, u32[]{:S(2)}, u32[]{:S(2)}) collective-permute-start(bf16[2,8,32,256]{3,2,1,0:T(8,128)(2,1)S(1)} %fusion.2), channel_id=1, source_target_pairs={{0,8},{4,12},{8,0},{12,4},{16,24},{20,28},{24,16},{28,20},{1,9},{5... | collective-permute-start | bytes 786440 | tf_op jit(solution)/shard_map/ppermute | solution.py:436
  87.2 6.6 %collective-permute-start.26 = (bf16[8,32,256]{2,1,0:T(8,128)(2,1)S(1)}, bf16[8,32,256]{2,1,0:T(8,128)(2,1)S(1)}, u32[]{:S(2)}, u32[]{:S(2)}) collective-permute-start(bf16[8,32,256]{2,1,0:T(8,128)(2,1)S(1)} %fusion.8.refs_4_), channel_id=1, source_target_pairs={{0,8},{4,12},{8,0},{12,4},{16,24},{20,28},{24,16},{28,20},{1,9},{5... | collective-permute-start | bytes 393224 | tf_op jit(solution)/shard_map/ppermute | solution.py:436
  92.2 5.0 %collective-permute-start.24 = (bf16[8,32,256]{2,1,0:T(8,128)(2,1)S(1)}, bf16[8,32,256]{2,1,0:T(8,128)(2,1)S(1)}, u32[]{:S(2)}, u32[]{:S(2)}) collective-permute-start(bf16[8,32,256]{2,1,0:T(8,128)(2,1)S(1)} %fusion.7.refs_3_), channel_id=1, source_target_pairs={{0,16},{4,20},{8,24},{12,28},{16,0},{20,4},{24,8},{28,12},{1,17},{... | collective-permute-start | bytes 393224 | tf_op jit(solution)/shard_map/ppermute | solution.py:436
  93.9 12.1 %collective-permute-start.27 = (bf16[4,32,256]{2,1,0:T(8,128)(2,1)S(1)}, bf16[4,32,256]{2,1,0:T(8,128)(2,1)S(1)}, u32[]{:S(2)}, u32[]{:S(2)}) collective-permute-start(bf16[4,32,256]{2,1,0:T(8,128)(2,1)S(1)} %get-tuple-element.55), channel_id=1, source_target_pairs={{0,2},{1,3},{2,0},{3,1},{4,6},{5,7},{6,4},{7,5},{8,10},{9,11},{10,... | collective-permute-start | bytes 196616 | tf_op jit(solution)/shard_map/ppermute | solution.py:354
  97.2 8.7 %collective-permute-start.28 = (bf16[4,32,256]{2,1,0:T(8,128)(2,1)S(1)}, bf16[4,32,256]{2,1,0:T(8,128)(2,1)S(1)}, u32[]{:S(2)}, u32[]{:S(2)}) collective-permute-start(bf16[4,32,256]{2,1,0:T(8,128)(2,1)S(1)} %get-tuple-element.54), channel_id=1, source_target_pairs={{0,3},{1,0},{2,1},{3,2},{4,7},{5,4},{6,5},{7,6},{8,11},{9,8},{10,9... | collective-permute-start | bytes 196616 | tf_op jit(solution)/shard_map/ppermute | solution.py:354
  100.8 6.8 %collective-permute-start.25 = (bf16[4,32,256]{2,1,0:T(8,128)(2,1)S(1)}, bf16[4,32,256]{2,1,0:T(8,128)(2,1)S(1)}, u32[]{:S(2)}, u32[]{:S(2)}) collective-permute-start(bf16[4,32,256]{2,1,0:T(8,128)(2,1)S(1)} %slice.134), channel_id=1, source_target_pairs={{0,1},{1,2},{2,3},{3,0},{4,5},{5,6},{6,7},{7,4},{8,9},{9,10},{10,1... | collective-permute-start | bytes 196616 | tf_op jit(solution)/shard_map/ppermute | solution.py:354
  102.8 7.4 %collective-permute-start.23 = (bf16[128,1024]{1,0:T(8,128)(2,1)S(1)}, bf16[128,1024]{1,0:T(8,128)(2,1)S(1)}, u32[]{:S(2)}, u32[]{:S(2)}) collective-permute-start(bf16[128,1024]{1,0:T(8,128)(2,1)S(1)} %sums.3), channel_id=1, source_target_pairs={{0,3},{1,0},{2,1},{3,2},{4,7},{5,4},{6,5},{7,6},{8,11},{9,8},{10,9... | collective-permute-start | bytes 786440 | tf_op jit(solution)/shard_map/ppermute | solution.py:354

commit v4 on v3

--- a/solution.py
+++ b/solution.py
@@ -310,7 +310,8 @@
 
 
 def join(at, halves):
-    held = [pltpu.with_memory_space_constraint(a, pltpu.VMEM) for half in halves for a in half]
+    late = mark(at, [halves[0][1], halves[1][1]])
+    held = [pltpu.with_memory_space_constraint(a, pltpu.VMEM) for half in halves for a in half] + [late]
     rows, width = held[0].shape
     return pl.pallas_call(
         join_kernel,
@@ -385,12 +386,11 @@
     xs[1][3] = ring_step(xs[1][0], 1, nz)
 
     others = halved(at, got, xs[0][3])
-    for k in range(max(bits - 1, 1)):
-        if bits > 1:
-            others = [double_over_dp(o, order[k], d, nd) for o, order in zip(others, orders)]
+    for k in range(bits - 1):
+        others = [double_over_dp(o, order[k], d, nd) for o, order in zip(others, orders)]
         if k == 0:
-            cot = turned(cotangent, others[0])
-            own = own_columns(at, first_factor, others[1], nz)
+            own = own_columns(at, first_factor, others[0], nz)
+    cot = turned(cotangent, others[1])
     pieces = []
     for o in others:
         pieces += [o, lax.ppermute(o, "dp", swap(0, nd))]
@@ -401,7 +401,7 @@
         [own] + pieces,
         [((nz * local, width, cols), BF16)],
     )[0]
-    far = mark(at, [xs[0][2], xs[1][1], xs[1][3]])
+    far = mark(at, [xs[0][2], xs[1][1], xs[1][3], own, cot])
     (xs[1][1],) = after(at, [xs[1][1]], far)
     xs[1][2] = ring_step(xs[1][1], -1, nz)
 
@@ -411,10 +411,10 @@
     high = layer(at, xs[1], first, low[-1], cot, [], 1, rows, nz, local, width, cols)
     high_far = ring_step(high[2], -1, nz)
     high_up = ring_step(high[1], 1, nz)
-    sent = sums(at, [(low[1], low_far)], mark(at, [low_far, low_down]))
+    give, keep = first_grad_terms(at, xs, [low[nz], high[nz]], [], nz, local, width, cols, nd)
+    sent = sums(at, [(low[1], low_far)], mark(at, [low_far, low_down, give]))
     low_up = ring_step(sent[0], 1, nz)
 
-    give, keep = first_grad_terms(at, xs, [low[nz], high[nz]], sent, nz, local, width, cols, nd)
     got = lax.ppermute(give, "dp", swap(0, nd))
     keep = keep.reshape([2] * (bits - 1) + list(keep.shape[1:]))
     got = got.reshape(keep.shape)
@@ -432,9 +432,10 @@
             pick = lambda n: lax.index_in_dim(totals[i], n, axis, keepdims=False)
             give.append(pick(1).astype(BF16))
             totals[i] = pick(0)
+        if k == 0:
+            sent = sums(at, [(high[3], high_far)], mark(at, [high_far, *give]))
         for i in range(2):
             totals[i] = totals[i] + lax.ppermute(give[i], "dp", swap(orders[i][k], nd)).astype(F32)
-    sent = sums(at, [(high[3], high_far)], mark(at, [high_far, high_up, low_up]), *give)
     high_down = ring_step(sent[0], -1, nz)
     blocks = jnp.concatenate(totals, axis=0).reshape(nz, local, kd, cols)
     give = [blocks[r].astype(BF16) for r in range(1, nz)]
@@ -474,7 +475,7 @@
 
     def run(inputs, first_factor, second_factor, cotangent):
         width, local, _ = first_factor.shape
-        fits = nz == 4 and local % 2 == 0 and width % (16 * nd) == 0 and nd & (nd - 1) == 0
+        fits = nz == 4 and nd > 2 and local % 2 == 0 and width % (16 * nd) == 0 and nd & (nd - 1) == 0
         return (body if fits else plain_body)(inputs, first_factor, second_factor, cotangent)
 
     return jax.shard_map(

time: 112 us -> 106 us (0.946)
  starting transfers between devices: 43.2 us -> 40 us
  waiting for transfers between devices: 24.6 us -> 21.7 us
    ppermute x4, waiting for transfers between devices: 8.5 us -> 3.85 us  [body(): lax.ppermute(give[i], 'dp', swap(orders[i][k], nd)).astype(F32)]
    ppermute x18, waiting for transfers between devices: 7.22 us -> 11.6 us  [ring_step(): lax.ppermute(value, 'tensor', [(i, (i + step) % nz) for i in range(nz)])]
    ppermute x1, waiting for transfers between devices: 2.65 us -> 0.01 us  [body(): got = lax.ppermute(give, 'dp', swap(0, nd))]
    ppermute x18, starting transfers between devices: 33.5 us -> 31.3 us  [ring_step(): lax.ppermute(value, 'tensor', [(i, (i + step) % nz) for i in range(nz)])]
    pallas_call x5 -> x6, Pallas kernels: 2.71 us -> 3.25 us  [mark(): pl.pallas_call(mark_kernel, in_specs=[SMEM] + [VMEM] * len(held), out_spe...]
  transfers between devices with their start and end apart: 29 -> 29, of which waited for: 12 -> 9; matrix products, arithmetic and copies ran while one was open for 9% -> 10% of each run, Pallas kernels for 21% -> 24%
where the time goes in v4:
time: 106 us
  starting transfers between devices  40 us (38%)
  Pallas kernels  29.1 us (27%)
  waiting for transfers between devices  21.7 us (20%)
  local copies, waits for them, and re-layouts  13.4 us (13%)
    ppermute x18, starting transfers between devices, ring_step(): lax.ppermute(value, 'tensor', [(i, (i + step) % nz) for i in range(nz)])  31.3 us
    pallas_call x9, Pallas kernels, on_chip(): pl.pallas_call(kernel, in_specs=[SMEM] + [VMEM] * len(operands) + [pl.Blo...  18.7 us
    unnamed x11, local copies, waits for them, and re-layouts  12.2 us
    ppermute x18, waiting for transfers between devices, ring_step(): lax.ppermute(value, 'tensor', [(i, (i + step) % nz) for i in range(nz)])  11.6 us
    ppermute x4, waiting for transfers between devices, double_over_dp(): got = lax.ppermute(part, 'dp', swap(bit, nd))  6.24 us
    ppermute x4, starting transfers between devices, body(): lax.ppermute(give[i], 'dp', swap(orders[i][k], nd)).astype(F32)  4.26 us
    ppermute x4, starting transfers between devices, double_over_dp(): got = lax.ppermute(part, 'dp', swap(bit, nd))  4.25 us
    ppermute x4, waiting for transfers between devices, body(): lax.ppermute(give[i], 'dp', swap(orders[i][k], nd)).astype(F32)  3.85 us
  transfers between devices with their start and end apart: 29, of which 9 were waited for; matrix products, arithmetic and copies ran while one was open for 10% of the time, Pallas kernels for 24%

profile of v4, /device:TPU:0, one launch (start us, length us, event | category | flops | bytes accessed | tf_op | source)
XLA Modules:
  0.0 106.1 jit_solution(1378839789144168796)
XLA Ops:
  0.6 1.1 %fusion.9 = (bf16[128,1024]{1,0:T(8,128)(2,1)S(1)}, bf16[128,1024]{1,0:T(8,128)(2,1)S(1)}) fusion(bf16[256,1024]{1,0:T(8,128)(2,1)} %param.4), kind=kLoop, calls=%fused_computation.34 | loop fusion | bytes 1048576 | tf_op jit(solution)/shard_map/slice | solution.py:376
  1.7 5.1 %collective-permute-start = (bf16[128,1024]{1,0:T(8,128)(2,1)S(1)}, bf16[128,1024]{1,0:T(8,128)(2,1)S(1)}, u32[]{:S(2)}, u32[]{:S(2)}) collective-permute-start(bf16[128,1024]{1,0:T(8,128)(2,1)S(1)} %get-tuple-element.45.refs_0_), channel_id=1, source_target_pairs={{0,3},{1,0},{2,1},{3,2},{4,7},{5,4},{6,5},{7,6},{8,11},{9,8},{10,9... | collective-permute-start | bytes 786440 | tf_op jit(solution)/shard_map/ppermute | solution.py:355
  6.8 0.1 pad_add_fusion.at_ref
  6.9 1.6 %copy-done = bf16[256,4,1024]{2,1,0:T(4,128)(2,1)S(1)} copy-done((bf16[256,4,1024]{2,1,0:T(4,128)(2,1)S(1)}, bf16[256,4,1024]{2,1,0:T(4,128)(2,1)}, u32[]{:S(2)}) %copy-start) | copy-done | bytes 2097176
  8.5 0.8 cut.1
  9.3 3.9 %collective-permute-start.2 = (bf16[4,32,256]{2,1,0:T(8,128)(2,1)S(1)}, bf16[4,32,256]{2,1,0:T(8,128)(2,1)S(1)}, u32[]{:S(2)}, u32[]{:S(2)}) collective-permute-start(bf16[4,32,256]{2,1,0:T(8,128)(2,1)S(1)} %get-tuple-element.22), channel_id=1, source_target_pairs={{0,3},{1,0},{2,1},{3,2},{4,7},{5,4},{6,5},{7,6},{8,11},{9,8},{10,9... | collective-permute-start | bytes 196616 | tf_op jit(solution)/shard_map/ppermute | solution.py:355
  13.2 0.6 collective-permute-start.4
  13.8 9.5 %copy.13 = bf16[1024,4,1024]{2,0,1:T(8,128)(2,1)} copy(bf16[1024,4,1024]{2,1,0:T(4,128)(2,1)} %param.6) | data formatting | bytes 16777216 | tf_op args[2]
  23.4 0.5 mark.6.refs_2_
  23.9 0.1 copy-done.3
  24.1 0.9 copy-done.4
  25.0 0.6 after.2
  25.6 0.6 halved.1
  26.2 1.6 %collective-permute-start.9 = (bf16[6,32,256]{2,1,0:T(8,128)(2,1)S(1)}, bf16[6,32,256]{2,1,0:T(8,128)(2,1)S(1)}, u32[]{:S(2)}, u32[]{:S(2)}) collective-permute-start(bf16[6,32,256]{2,1,0:T(8,128)(2,1)S(1)} %get-tuple-element.27), channel_id=1, source_target_pairs={{0,16},{4,20},{8,24},{12,28},{16,0},{20,4},{24,8},{28,12},{1,17},{... | collective-permute-start | bytes 294920 | tf_op jit(solution)/shard_map/ppermute | solution.py:359
  27.8 2.8 %collective-permute-start.5 = (bf16[128,1024]{1,0:T(8,128)(2,1)S(1)}, bf16[128,1024]{1,0:T(8,128)(2,1)S(1)}, u32[]{:S(2)}, u32[]{:S(2)}) collective-permute-start(bf16[128,1024]{1,0:T(8,128)(2,1)S(1)} %get-tuple-element.25.refs_3_), channel_id=1, source_target_pairs={{0,1},{1,2},{2,3},{3,0},{4,5},{5,6},{6,7},{7,4},{8,9},{9,10},{10,1... | collective-permute-start | bytes 786440 | tf_op jit(solution)/shard_map/ppermute | solution.py:355
  30.7 3.8 %collective-permute-start.12 = (bf16[128,1024]{1,0:T(8,128)(2,1)S(1)}, bf16[128,1024]{1,0:T(8,128)(2,1)S(1)}, u32[]{:S(2)}, u32[]{:S(2)}) collective-permute-start(bf16[128,1024]{1,0:T(8,128)(2,1)S(1)} %get-tuple-element.28.refs_0_.refs_4_), channel_id=1, source_target_pairs={{0,3},{1,0},{2,1},{3,2},{4,7},{5,4},{6,5},{7,6},{8,11},{9,8},{10,9... | collective-permute-start | bytes 786440 | tf_op jit(solution)/shard_map/ppermute | solution.py:355
  34.4 1.5 %collective-permute-start.6 = (bf16[6,32,256]{2,1,0:T(8,128)(2,1)S(1)}, bf16[6,32,256]{2,1,0:T(8,128)(2,1)S(1)}, u32[]{:S(2)}, u32[]{:S(2)}) collective-permute-start(bf16[6,32,256]{2,1,0:T(8,128)(2,1)S(1)} %get-tuple-element.26), channel_id=1, source_target_pairs={{0,8},{4,12},{8,0},{12,4},{16,24},{20,28},{24,16},{28,20},{1,9},{5... | collective-permute-start | bytes 294920 | tf_op jit(solution)/shard_map/ppermute | solution.py:359
  36.0 0.6 collective-permute-start.10
  36.6 2.5 %collective-permute-done.6 = bf16[6,32,256]{2,1,0:T(8,128)(2,1)S(1)} collective-permute-done((bf16[6,32,256]{2,1,0:T(8,128)(2,1)S(1)}, bf16[6,32,256]{2,1,0:T(8,128)(2,1)S(1)}, u32[]{:S(2)}, u32[]{:S(2)}) %collective-permute-start.6) | collective-permute-done | bytes 98336 | tf_op jit(solution)/shard_map/ppermute | solution.py:359
  39.1 2.0 %own_columns.1.own_ref.refs_3_ = bf16[4,256,256]{2,1,0:T(8,128)(2,1)S(1)} custom-call(s32[2]{0:T(128)S(1)} %pad_add_fusion.at_ref, bf16[256,4,1024]{2,1,0:T(4,128)(2,1)S(1)} %copy-done.1, bf16[2,6,32,256]{3,2,1,0:T(8,128)(2,1)S(1)} %pad_maximum_fusion.2.later_ref), custom_call_target="tpu_custom_call" | custom-call | tf_op jit(solution)/shard_map/own_columns/pallas_call | solution.py:80
  41.1 0.6 collective-permute-start.7
  41.8 0.1 collective-permute-start.11
  41.9 1.2 %turned.1.refs_4_.refs_5_ = bf16[256,4096]{1,0:T(8,128)(2,1)S(1)} custom-call(bf16[4096,256]{1,0:T(8,128)(2,1)S(1)} %copy-done.2, bf16[2,2,6,32,256]{4,3,2,1,0:T(8,128)(2,1)S(1)} %pad_maximum_fusion.1.refs_2_.later_ref), custom_call_target="tpu_custom_call" | custom-call | tf_op jit(solution)/shard_map/turned/pallas_call | solution.py:101
  43.1 3.7 %collective-permute-done.7 = bf16[2,6,32,256]{3,2,1,0:T(8,128)(2,1)S(1)} collective-permute-done((bf16[2,6,32,256]{3,2,1,0:T(8,128)(2,1)S(1)}, bf16[2,6,32,256]{3,2,1,0:T(8,128)(2,1)S(1)}, u32[]{:S(2)}, u32[]{:S(2)}) %collective-permute-start.7) | collective-permute-done | bytes 196640 | tf_op jit(solution)/shard_map/ppermute | solution.py:359
  47.0 0.1 collective-permute-start.8
  47.1 0.9 collective-permute-done.12.refs_1_.refs_0_
  48.0 0.5 mark.7.refs_1_
  48.5 0.6 after.3.refs_6_.refs_1_.refs_5_
  49.1 2.1 %collective-permute-start.16 = (bf16[128,1024]{1,0:T(8,128)(2,1)S(1)}, bf16[128,1024]{1,0:T(8,128)(2,1)S(1)}, u32[]{:S(2)}, u32[]{:S(2)}) collective-permute-start(bf16[128,1024]{1,0:T(8,128)(2,1)S(1)} %after.3.refs_6_.refs_1_.refs_5_), channel_id=1, source_target_pairs={{0,3},{1,0},{2,1},{3,2},{4,7},{5,4},{6,5},{7,6},{8,11},{9,8},{10,9... | collective-permute-start | bytes 786440 | tf_op jit(solution)/shard_map/ppermute | solution.py:355
  51.2 0.7 assemble.1.refs_4_
  51.9 7.9 %layer.2 = (f32[128,1024]{1,0:T(8,128)S(1)}, bf16[128,1024]{1,0:T(8,128)(2,1)S(1)}, bf16[128,1024]{1,0:T(8,128)(2,1)S(1)}, bf16[128,1024]{1,0:T(8,128)(2,1)S(1)}...) custom-call(s32[2]{0:T(128)S(1)} %pad_add_fusion.at_ref, ...), custom_call_target="tpu_custom_call" | custom-call | tf_op jit(solution)/shard_map/layer/pallas_call | solution.py:35
  59.7 0.1 collective-permute-start.14
  59.8 3.8 %collective-permute-start.15 = (bf16[128,1024]{1,0:T(8,128)(2,1)S(1)}, bf16[128,1024]{1,0:T(8,128)(2,1)S(1)}, u32[]{:S(2)}, u32[]{:S(2)}) collective-permute-start(bf16[128,1024]{1,0:T(8,128)(2,1)S(1)} %get-tuple-element.32), channel_id=1, source_target_pairs={{0,3},{1,0},{2,1},{3,2},{4,7},{5,4},{6,5},{7,6},{8,11},{9,8},{10,9... | collective-permute-start | bytes 786440 | tf_op jit(solution)/shard_map/ppermute | solution.py:355
  63.6 5.9 %layer.3 = (f32[128,1024]{1,0:T(8,128)S(1)}, bf16[128,1024]{1,0:T(8,128)(2,1)S(1)}, bf16[128,1024]{1,0:T(8,128)(2,1)S(1)}, bf16[128,1024]{1,0:T(8,128)(2,1)S(1)}, bf16[4,128,1024]{2,1,0:T(8,128)(2,1)S(1)}) custom-call(s32[2]{0:T(128)S(1)} %pad_add_fusion.at_ref, bf16[128,1024]{1,0:T(8,128)(2,1)S(1)} %get-tuple-element.28.refs_0_.refs_4_, ...), custom_call_target="tpu_custom_call" | custom-call | tf_op jit(solution)/shard_map/layer/pallas_call | solution.py:35
  69.6 1.4 %first_grad_terms.1 = (bf16[4,16,32,256]{3,2,1,0:T(8,128)(2,1)S(1)}, bf16[4,16,32,256]{3,2,1,0:T(8,128)(2,1)S(1)}) custom-call(s32[2]{0:T(128)S(1)} %pad_add_fusion.at_ref, bf16[128,1024]{1,0:T(8,128)(2,1)S(1)} %get-tuple-element.45.refs_0_, bf16[128,1024]{1,0:T(8,128)(2,1)S(1)} %collective-permute-done.refs_1_, ...), custom_call_target="tpu_custom_call" | custom-call | tf_op jit(solution)/shard_map/first_grad_terms/pallas_call | solution.py:35
  71.0 0.1 collective-permute-start.20
  71.0 0.1 collective-permute-start.18
  71.1 3.8 %collective-permute-start.19 = (bf16[128,1024]{1,0:T(8,128)(2,1)S(1)}, bf16[128,1024]{1,0:T(8,128)(2,1)S(1)}, u32[]{:S(2)}, u32[]{:S(2)}) collective-permute-start(bf16[128,1024]{1,0:T(8,128)(2,1)S(1)} %get-tuple-element.40), channel_id=1, source_target_pairs={{0,3},{1,0},{2,1},{3,2},{4,7},{5,4},{6,5},{7,6},{8,11},{9,8},{10,9... | collective-permute-start | bytes 786440 | tf_op jit(solution)/shard_map/ppermute | solution.py:355
  74.9 0.5 mark.8.refs_2_
  75.5 0.6 sums.2
  76.1 0.1 collective-permute-start.17
  76.2 0.4 convert_add_fusion
  76.6 0.6 collective-permute-start.25
  77.2 1.6 %collective-permute-start.22 = (bf16[2,8,32,256]{3,2,1,0:T(8,128)(2,1)S(1)}, bf16[2,8,32,256]{3,2,1,0:T(8,128)(2,1)S(1)}, u32[]{:S(2)}, u32[]{:S(2)}) collective-permute-start(bf16[2,8,32,256]{3,2,1,0:T(8,128)(2,1)S(1)} %fusion.3.refs_1_), channel_id=1, source_target_pairs={{0,8},{4,12},{8,0},{12,4},{16,24},{20,28},{24,16},{28,20},{1,9},{5... | collective-permute-start | bytes 786440 | tf_op jit(solution)/shard_map/ppermute | solution.py:438
  78.8 6.6 %collective-permute-done.19.refs_0_.refs_1_ = bf16[128,1024]{1,0:T(8,128)(2,1)S(1)} collective-permute-done((bf16[128,1024]{1,0:T(8,128)(2,1)S(1)}, bf16[128,1024]{1,0:T(8,128)(2,1)S(1)}, u32[]{:S(2)}, u32[]{:S(2)}) %collective-permute-start.19) | collective-permute-done | bytes 262176 | tf_op jit(solution)/shard_map/ppermute | solution.py:355
  85.4 0.5 mark.9.refs_2_
  85.9 0.6 sums.3
  86.5 2.4 %collective-permute-start.21 = (bf16[128,1024]{1,0:T(8,128)(2,1)S(1)}, bf16[128,1024]{1,0:T(8,128)(2,1)S(1)}, u32[]{:S(2)}, u32[]{:S(2)}) collective-permute-start(bf16[128,1024]{1,0:T(8,128)(2,1)S(1)} %sums.3), channel_id=1, source_target_pairs={{0,3},{1,0},{2,1},{3,2},{4,7},{5,4},{6,5},{7,6},{8,11},{9,8},{10,9... | collective-permute-start | bytes 786440 | tf_op jit(solution)/shard_map/ppermute | solution.py:355
  88.9 0.1 fusion
  89.0 1.6 %collective-permute-start.26 = (bf16[8,32,256]{2,1,0:T(8,128)(2,1)S(1)}, bf16[8,32,256]{2,1,0:T(8,128)(2,1)S(1)}, u32[]{:S(2)}, u32[]{:S(2)}) collective-permute-start(bf16[8,32,256]{2,1,0:T(8,128)(2,1)S(1)} %fusion.8), channel_id=1, source_target_pairs={{0,8},{4,12},{8,0},{12,4},{16,24},{20,28},{24,16},{28,20},{1,9},{5... | collective-permute-start | bytes 393224 | tf_op jit(solution)/shard_map/ppermute | solution.py:438
  90.6 0.1 fusion.1
  90.7 0.6 collective-permute-start.23
  91.3 2.8 %collective-permute-done.26 = bf16[8,32,256]{2,1,0:T(8,128)(2,1)S(1)} collective-permute-done((bf16[8,32,256]{2,1,0:T(8,128)(2,1)S(1)}, bf16[8,32,256]{2,1,0:T(8,128)(2,1)S(1)}, u32[]{:S(2)}, u32[]{:S(2)}) %collective-permute-start.26) | collective-permute-done | bytes 131104 | tf_op jit(solution)/shard_map/ppermute | solution.py:438
  94.1 0.6 collective-permute-start.27
  94.7 1.1 collective-permute-done.23
  95.8 1.9 %collective-permute-start.28 = (bf16[4,32,256]{2,1,0:T(8,128)(2,1)S(1)}, bf16[4,32,256]{2,1,0:T(8,128)(2,1)S(1)}, u32[]{:S(2)}, u32[]{:S(2)}) collective-permute-start(bf16[4,32,256]{2,1,0:T(8,128)(2,1)S(1)} %get-tuple-element.54), channel_id=1, source_target_pairs={{0,3},{1,0},{2,1},{3,2},{4,7},{5,4},{6,5},{7,6},{8,11},{9,8},{10,9... | collective-permute-start | bytes 196616 | tf_op jit(solution)/shard_map/ppermute | solution.py:355
  97.8 0.1 collective-permute-start.24
  97.9 0.5 mark.10.refs_6_
  98.5 0.1 collective-permute-done.21.refs_5_
  98.5 1.5 %join.1 = bf16[256,1024]{1,0:T(8,128)(2,1)} custom-call(s32[2]{0:T(128)S(1)} %pad_add_fusion.at_ref, f32[128,1024]{1,0:T(8,128)S(1)} %get-tuple-element.29.refs_0_, bf16[128,1024]{1,0:T(8,128)(2,1)S(1)} %collective-permute-done.17.refs_0_.refs_1_, bf16[128,1024]{1,0:T(8,128)(2,1)S(1)} %collective-permute-done.15.refs_1_.refs_2_, ...), custom_call_target="tpu_custom_call" | custom-call | tf_op jit(solution)/shard_map/join/pallas_call | solution.py:316
  100.1 1.7 %collective-permute-done.27.refs_1_.refs_2_ = bf16[4,32,256]{2,1,0:T(8,128)(2,1)S(1)} collective-permute-done((bf16[4,32,256]{2,1,0:T(8,128)(2,1)S(1)}, bf16[4,32,256]{2,1,0:T(8,128)(2,1)S(1)}, u32[]{:S(2)}, u32[]{:S(2)}) %collective-permute-start.27) | collective-permute-done | bytes 65568 | tf_op jit(solution)/shard_map/ppermute | solution.py:355
  101.8 2.2 %collective-permute-done.24.refs_0_.refs_1_ = bf16[4,32,256]{2,1,0:T(8,128)(2,1)S(1)} collective-permute-done((bf16[4,32,256]{2,1,0:T(8,128)(2,1)S(1)}, bf16[4,32,256]{2,1,0:T(8,128)(2,1)S(1)}, u32[]{:S(2)}, u32[]{:S(2)}) %collective-permute-start.24) | collective-permute-done | bytes 65568 | tf_op jit(solution)/shard_map/ppermute | solution.py:355
  104.0 0.5 mark.11.refs_4_
  104.5 1.5 %place.1 = f32[32,4,1024]{2,1,0:T(4,128)} custom-call(s32[2]{0:T(128)S(1)} %pad_add_fusion.at_ref, f32[4,32,256]{2,1,0:T(8,128)S(1)} %slice.96.refs_0_, bf16[4,32,256]{2,1,0:T(8,128)(2,1)S(1)} %collective-permute-done.24.refs_0_.refs_1_, bf16[4,32,256]{2,1,0:T(8,128)(2,1)S(1)} %collective-permute-done.27.refs_1_.refs_2_, ...), custom_call_target="tpu_custom_call" | custom-call | tf_op jit(solution)/shard_map/place/pallas_call | solution.py:339
  (47 shorter events, 0.5 us)
Async XLA Ops:
  1.7 21.7 %collective-permute-start = (bf16[128,1024]{1,0:T(8,128)(2,1)S(1)}, bf16[128,1024]{1,0:T(8,128)(2,1)S(1)}, u32[]{:S(2)}, u32[]{:S(2)}) collective-permute-start(bf16[128,1024]{1,0:T(8,128)(2,1)S(1)} %get-tuple-element.45.refs_0_), channel_id=1, source_target_pairs={{0,3},{1,0},{2,1},{3,2},{4,7},{5,4},{6,5},{7,6},{8,11},{9,8},{10,9... | collective-permute-start | bytes 786440 | tf_op jit(solution)/shard_map/ppermute | solution.py:355
  6.8 16.6 %collective-permute-start.1 = (bf16[128,1024]{1,0:T(8,128)(2,1)S(1)}, bf16[128,1024]{1,0:T(8,128)(2,1)S(1)}, u32[]{:S(2)}, u32[]{:S(2)}) collective-permute-start(bf16[128,1024]{1,0:T(8,128)(2,1)S(1)} %get-tuple-element.45.refs_0_), channel_id=1, source_target_pairs={{0,1},{1,2},{2,3},{3,0},{4,5},{5,6},{6,7},{7,4},{8,9},{9,10},{10,1... | collective-permute-start | bytes 786440 | tf_op jit(solution)/shard_map/ppermute | solution.py:355
  6.9 1.6 %copy-start = (bf16[256,4,1024]{2,1,0:T(4,128)(2,1)S(1)}, bf16[256,4,1024]{2,1,0:T(4,128)(2,1)}, u32[]{:S(2)}) copy-start(bf16[256,4,1024]{2,1,0:T(4,128)(2,1)} %f_ref.3) | copy-start | bytes 6291460
  9.3 14.8 %collective-permute-start.2 = (bf16[4,32,256]{2,1,0:T(8,128)(2,1)S(1)}, bf16[4,32,256]{2,1,0:T(8,128)(2,1)S(1)}, u32[]{:S(2)}, u32[]{:S(2)}) collective-permute-start(bf16[4,32,256]{2,1,0:T(8,128)(2,1)S(1)} %get-tuple-element.22), channel_id=1, source_target_pairs={{0,3},{1,0},{2,1},{3,2},{4,7},{5,4},{6,5},{7,6},{8,11},{9,8},{10,9... | collective-permute-start | bytes 196616 | tf_op jit(solution)/shard_map/ppermute | solution.py:355
  13.2 10.9 %collective-permute-start.3 = (bf16[4,32,256]{2,1,0:T(8,128)(2,1)S(1)}, bf16[4,32,256]{2,1,0:T(8,128)(2,1)S(1)}, u32[]{:S(2)}, u32[]{:S(2)}) collective-permute-start(bf16[4,32,256]{2,1,0:T(8,128)(2,1)S(1)} %get-tuple-element.23), channel_id=1, source_target_pairs={{0,2},{1,3},{2,0},{3,1},{4,6},{5,7},{6,4},{7,5},{8,10},{9,11},{10,... | collective-permute-start | bytes 196616 | tf_op jit(solution)/shard_map/ppermute | solution.py:355
  13.2 10.9 %collective-permute-start.4 = (bf16[4,32,256]{2,1,0:T(8,128)(2,1)S(1)}, bf16[4,32,256]{2,1,0:T(8,128)(2,1)S(1)}, u32[]{:S(2)}, u32[]{:S(2)}) collective-permute-start(bf16[4,32,256]{2,1,0:T(8,128)(2,1)S(1)} %get-tuple-element.24), channel_id=1, source_target_pairs={{0,1},{1,2},{2,3},{3,0},{4,5},{5,6},{6,7},{7,4},{8,9},{9,10},{10,1... | collective-permute-start | bytes 196616 | tf_op jit(solution)/shard_map/ppermute | solution.py:355
  23.4 0.7 copy-start.3
  24.1 1.0 copy-start.4
  25.0 14.1 %copy-start.1 = (bf16[256,4,1024]{2,1,0:T(4,128)(2,1)S(1)}, bf16[256,4,1024]{2,1,0:T(4,128)(2,1)}, u32[]{:S(2)}) copy-start(bf16[256,4,1024]{2,1,0:T(4,128)(2,1)} %f_ref.3) | copy-start | bytes 6291460
  26.2 9.8 %collective-permute-start.9 = (bf16[6,32,256]{2,1,0:T(8,128)(2,1)S(1)}, bf16[6,32,256]{2,1,0:T(8,128)(2,1)S(1)}, u32[]{:S(2)}, u32[]{:S(2)}) collective-permute-start(bf16[6,32,256]{2,1,0:T(8,128)(2,1)S(1)} %get-tuple-element.27), channel_id=1, source_target_pairs={{0,16},{4,20},{8,24},{12,28},{16,0},{20,4},{24,8},{28,12},{1,17},{... | collective-permute-start | bytes 294920 | tf_op jit(solution)/shard_map/ppermute | solution.py:359
  27.8 19.3 %collective-permute-start.5 = (bf16[128,1024]{1,0:T(8,128)(2,1)S(1)}, bf16[128,1024]{1,0:T(8,128)(2,1)S(1)}, u32[]{:S(2)}, u32[]{:S(2)}) collective-permute-start(bf16[128,1024]{1,0:T(8,128)(2,1)S(1)} %get-tuple-element.25.refs_3_), channel_id=1, source_target_pairs={{0,1},{1,2},{2,3},{3,0},{4,5},{5,6},{6,7},{7,4},{8,9},{9,10},{10,1... | collective-permute-start | bytes 786440 | tf_op jit(solution)/shard_map/ppermute | solution.py:355
  30.6 16.4 %collective-permute-start.13 = (bf16[128,1024]{1,0:T(8,128)(2,1)S(1)}, bf16[128,1024]{1,0:T(8,128)(2,1)S(1)}, u32[]{:S(2)}, u32[]{:S(2)}) collective-permute-start(bf16[128,1024]{1,0:T(8,128)(2,1)S(1)} %get-tuple-element.28.refs_0_.refs_4_), channel_id=1, source_target_pairs={{0,1},{1,2},{2,3},{3,0},{4,5},{5,6},{6,7},{7,4},{8,9},{9,10},{10,1... | collective-permute-start | bytes 786440 | tf_op jit(solution)/shard_map/ppermute | solution.py:355
  30.7 17.3 %collective-permute-start.12 = (bf16[128,1024]{1,0:T(8,128)(2,1)S(1)}, bf16[128,1024]{1,0:T(8,128)(2,1)S(1)}, u32[]{:S(2)}, u32[]{:S(2)}) collective-permute-start(bf16[128,1024]{1,0:T(8,128)(2,1)S(1)} %get-tuple-element.28.refs_0_.refs_4_), channel_id=1, source_target_pairs={{0,3},{1,0},{2,1},{3,2},{4,7},{5,4},{6,5},{7,6},{8,11},{9,8},{10,9... | collective-permute-start | bytes 786440 | tf_op jit(solution)/shard_map/ppermute | solution.py:355
  34.4 4.6 %collective-permute-start.6 = (bf16[6,32,256]{2,1,0:T(8,128)(2,1)S(1)}, bf16[6,32,256]{2,1,0:T(8,128)(2,1)S(1)}, u32[]{:S(2)}, u32[]{:S(2)}) collective-permute-start(bf16[6,32,256]{2,1,0:T(8,128)(2,1)S(1)} %get-tuple-element.26), channel_id=1, source_target_pairs={{0,8},{4,12},{8,0},{12,4},{16,24},{20,28},{24,16},{28,20},{1,9},{5... | collective-permute-start | bytes 294920 | tf_op jit(solution)/shard_map/ppermute | solution.py:359
  36.0 5.7 %collective-permute-start.10 = (bf16[2,6,32,256]{3,2,1,0:T(8,128)(2,1)S(1)}, bf16[2,6,32,256]{3,2,1,0:T(8,128)(2,1)S(1)}, u32[]{:S(2)}, u32[]{:S(2)}) collective-permute-start(bf16[2,6,32,256]{3,2,1,0:T(8,128)(2,1)S(1)} %pad_maximum_fusion.3), channel_id=1, source_target_pairs={{0,8},{4,12},{8,0},{12,4},{16,24},{20,28},{24,16},{28,20},{1,9},{5... | collective-permute-start | bytes 589832 | tf_op jit(solution)/shard_map/ppermute | solution.py:359
  39.1 2.8 %copy-start.2 = (bf16[4096,256]{1,0:T(8,128)(2,1)S(1)}, bf16[4096,256]{1,0:T(8,128)(2,1)}, u32[]{:S(2)}) copy-start(bf16[4096,256]{1,0:T(8,128)(2,1)} %x_ref.1) | copy-start | bytes 6291460
  41.1 5.7 %collective-permute-start.7 = (bf16[2,6,32,256]{3,2,1,0:T(8,128)(2,1)S(1)}, bf16[2,6,32,256]{3,2,1,0:T(8,128)(2,1)S(1)}, u32[]{:S(2)}, u32[]{:S(2)}) collective-permute-start(bf16[2,6,32,256]{3,2,1,0:T(8,128)(2,1)S(1)} %pad_maximum_fusion.2.later_ref), channel_id=1, source_target_pairs={{0,16},{4,20},{8,24},{12,28},{16,0},{20,4},{24,8},{28,12},{1,17},{... | collective-permute-start | bytes 589832 | tf_op jit(solution)/shard_map/ppermute | solution.py:359
  41.8 9.4 %collective-permute-start.11 = (bf16[2,2,6,32,256]{4,3,2,1,0:T(8,128)(2,1)S(1)}, bf16[2,2,6,32,256]{4,3,2,1,0:T(8,128)(2,1)S(1)}, u32[]{:S(2)}, u32[]{:S(2)}) collective-permute-start(bf16[2,2,6,32,256]{4,3,2,1,0:T(8,128)(2,1)S(1)} %pad_maximum_fusion.1.refs_2_.later_ref), channel_id=1, source_target_pairs={{0,4},{4,0},{8,12},{12,8},{16,20},{20,16},{24,28},{28,24},{1,5},{5... | collective-permute-start | bytes 1179656 | tf_op jit(solution)/shard_map/ppermute | solution.py:396
  47.0 4.2 %collective-permute-start.8 = (bf16[2,2,6,32,256]{4,3,2,1,0:T(8,128)(2,1)S(1)}, bf16[2,2,6,32,256]{4,3,2,1,0:T(8,128)(2,1)S(1)}, u32[]{:S(2)}, u32[]{:S(2)}) collective-permute-start(bf16[2,2,6,32,256]{4,3,2,1,0:T(8,128)(2,1)S(1)} %pad_maximum_fusion.refs_0_), channel_id=1, source_target_pairs={{0,4},{4,0},{8,12},{12,8},{16,20},{20,16},{24,28},{28,24},{1,5},{5... | collective-permute-start | bytes 1179656 | tf_op jit(solution)/shard_map/ppermute | solution.py:396
  49.1 14.5 %collective-permute-start.16 = (bf16[128,1024]{1,0:T(8,128)(2,1)S(1)}, bf16[128,1024]{1,0:T(8,128)(2,1)S(1)}, u32[]{:S(2)}, u32[]{:S(2)}) collective-permute-start(bf16[128,1024]{1,0:T(8,128)(2,1)S(1)} %after.3.refs_6_.refs_1_.refs_5_), channel_id=1, source_target_pairs={{0,3},{1,0},{2,1},{3,2},{4,7},{5,4},{6,5},{7,6},{8,11},{9,8},{10,9... | collective-permute-start | bytes 786440 | tf_op jit(solution)/shard_map/ppermute | solution.py:355
  59.7 15.2 %collective-permute-start.14 = (bf16[128,1024]{1,0:T(8,128)(2,1)S(1)}, bf16[128,1024]{1,0:T(8,128)(2,1)S(1)}, u32[]{:S(2)}, u32[]{:S(2)}) collective-permute-start(bf16[128,1024]{1,0:T(8,128)(2,1)S(1)} %get-tuple-element.31), channel_id=1, source_target_pairs={{0,1},{1,2},{2,3},{3,0},{4,5},{5,6},{6,7},{7,4},{8,9},{9,10},{10,1... | collective-permute-start | bytes 786440 | tf_op jit(solution)/shard_map/ppermute | solution.py:355
  59.8 15.1 %collective-permute-start.15 = (bf16[128,1024]{1,0:T(8,128)(2,1)S(1)}, bf16[128,1024]{1,0:T(8,128)(2,1)S(1)}, u32[]{:S(2)}, u32[]{:S(2)}) collective-permute-start(bf16[128,1024]{1,0:T(8,128)(2,1)S(1)} %get-tuple-element.32), channel_id=1, source_target_pairs={{0,3},{1,0},{2,1},{3,2},{4,7},{5,4},{6,5},{7,6},{8,11},{9,8},{10,9... | collective-permute-start | bytes 786440 | tf_op jit(solution)/shard_map/ppermute | solution.py:355
  71.0 5.2 %collective-permute-start.20 = (bf16[4,16,32,256]{3,2,1,0:T(8,128)(2,1)S(1)}, bf16[4,16,32,256]{3,2,1,0:T(8,128)(2,1)S(1)}, u32[]{:S(2)}, u32[]{:S(2)}) collective-permute-start(bf16[4,16,32,256]{3,2,1,0:T(8,128)(2,1)S(1)} %get-tuple-element.36.refs_2_), channel_id=1, source_target_pairs={{0,4},{4,0},{8,12},{12,8},{16,20},{20,16},{24,28},{28,24},{1,5},{5... | collective-permute-start | bytes 3145736 | tf_op jit(solution)/shard_map/ppermute | solution.py:418
  71.0 26.7 %collective-permute-start.18 = (bf16[128,1024]{1,0:T(8,128)(2,1)S(1)}, bf16[128,1024]{1,0:T(8,128)(2,1)S(1)}, u32[]{:S(2)}, u32[]{:S(2)}) collective-permute-start(bf16[128,1024]{1,0:T(8,128)(2,1)S(1)} %get-tuple-element.38), channel_id=1, source_target_pairs={{0,1},{1,2},{2,3},{3,0},{4,5},{5,6},{6,7},{7,4},{8,9},{9,10},{10,1... | collective-permute-start | bytes 786440 | tf_op jit(solution)/shard_map/ppermute | solution.py:355
  71.1 14.3 %collective-permute-start.19 = (bf16[128,1024]{1,0:T(8,128)(2,1)S(1)}, bf16[128,1024]{1,0:T(8,128)(2,1)S(1)}, u32[]{:S(2)}, u32[]{:S(2)}) collective-permute-start(bf16[128,1024]{1,0:T(8,128)(2,1)S(1)} %get-tuple-element.40), channel_id=1, source_target_pairs={{0,3},{1,0},{2,1},{3,2},{4,7},{5,4},{6,5},{7,6},{8,11},{9,8},{10,9... | collective-permute-start | bytes 786440 | tf_op jit(solution)/shard_map/ppermute | solution.py:355
  76.1 21.8 %collective-permute-start.17 = (bf16[128,1024]{1,0:T(8,128)(2,1)S(1)}, bf16[128,1024]{1,0:T(8,128)(2,1)S(1)}, u32[]{:S(2)}, u32[]{:S(2)}) collective-permute-start(bf16[128,1024]{1,0:T(8,128)(2,1)S(1)} %sums.2), channel_id=1, source_target_pairs={{0,1},{1,2},{2,3},{3,0},{4,5},{5,6},{6,7},{7,4},{8,9},{9,10},{10,1... | collective-permute-start | bytes 786440 | tf_op jit(solution)/shard_map/ppermute | solution.py:355
  76.6 12.3 %collective-permute-start.25 = (bf16[2,8,32,256]{3,2,1,0:T(8,128)(2,1)S(1)}, bf16[2,8,32,256]{3,2,1,0:T(8,128)(2,1)S(1)}, u32[]{:S(2)}, u32[]{:S(2)}) collective-permute-start(bf16[2,8,32,256]{3,2,1,0:T(8,128)(2,1)S(1)} %fusion.2.refs_2_), channel_id=1, source_target_pairs={{0,16},{4,20},{8,24},{12,28},{16,0},{20,4},{24,8},{28,12},{1,17},{... | collective-permute-start | bytes 786440 | tf_op jit(solution)/shard_map/ppermute | solution.py:438
  77.2 13.4 %collective-permute-start.22 = (bf16[2,8,32,256]{3,2,1,0:T(8,128)(2,1)S(1)}, bf16[2,8,32,256]{3,2,1,0:T(8,128)(2,1)S(1)}, u32[]{:S(2)}, u32[]{:S(2)}) collective-permute-start(bf16[2,8,32,256]{3,2,1,0:T(8,128)(2,1)S(1)} %fusion.3.refs_1_), channel_id=1, source_target_pairs={{0,8},{4,12},{8,0},{12,4},{16,24},{20,28},{24,16},{28,20},{1,9},{5... | collective-permute-start | bytes 786440 | tf_op jit(solution)/shard_map/ppermute | solution.py:438
  86.5 12.0 %collective-permute-start.21 = (bf16[128,1024]{1,0:T(8,128)(2,1)S(1)}, bf16[128,1024]{1,0:T(8,128)(2,1)S(1)}, u32[]{:S(2)}, u32[]{:S(2)}) collective-permute-start(bf16[128,1024]{1,0:T(8,128)(2,1)S(1)} %sums.3), channel_id=1, source_target_pairs={{0,3},{1,0},{2,1},{3,2},{4,7},{5,4},{6,5},{7,6},{8,11},{9,8},{10,9... | collective-permute-start | bytes 786440 | tf_op jit(solution)/shard_map/ppermute | solution.py:355
  89.0 5.0 %collective-permute-start.26 = (bf16[8,32,256]{2,1,0:T(8,128)(2,1)S(1)}, bf16[8,32,256]{2,1,0:T(8,128)(2,1)S(1)}, u32[]{:S(2)}, u32[]{:S(2)}) collective-permute-start(bf16[8,32,256]{2,1,0:T(8,128)(2,1)S(1)} %fusion.8), channel_id=1, source_target_pairs={{0,8},{4,12},{8,0},{12,4},{16,24},{20,28},{24,16},{28,20},{1,9},{5... | collective-permute-start | bytes 393224 | tf_op jit(solution)/shard_map/ppermute | solution.py:438
  90.7 5.0 %collective-permute-start.23 = (bf16[8,32,256]{2,1,0:T(8,128)(2,1)S(1)}, bf16[8,32,256]{2,1,0:T(8,128)(2,1)S(1)}, u32[]{:S(2)}, u32[]{:S(2)}) collective-permute-start(bf16[8,32,256]{2,1,0:T(8,128)(2,1)S(1)} %fusion.7), channel_id=1, source_target_pairs={{0,16},{4,20},{8,24},{12,28},{16,0},{20,4},{24,8},{28,12},{1,17},{... | collective-permute-start | bytes 393224 | tf_op jit(solution)/shard_map/ppermute | solution.py:438
  94.1 7.7 %collective-permute-start.27 = (bf16[4,32,256]{2,1,0:T(8,128)(2,1)S(1)}, bf16[4,32,256]{2,1,0:T(8,128)(2,1)S(1)}, u32[]{:S(2)}, u32[]{:S(2)}) collective-permute-start(bf16[4,32,256]{2,1,0:T(8,128)(2,1)S(1)} %get-tuple-element.55), channel_id=1, source_target_pairs={{0,2},{1,3},{2,0},{3,1},{4,6},{5,7},{6,4},{7,5},{8,10},{9,11},{10,... | collective-permute-start | bytes 196616 | tf_op jit(solution)/shard_map/ppermute | solution.py:355
  95.8 6.0 %collective-permute-start.28 = (bf16[4,32,256]{2,1,0:T(8,128)(2,1)S(1)}, bf16[4,32,256]{2,1,0:T(8,128)(2,1)S(1)}, u32[]{:S(2)}, u32[]{:S(2)}) collective-permute-start(bf16[4,32,256]{2,1,0:T(8,128)(2,1)S(1)} %get-tuple-element.54), channel_id=1, source_target_pairs={{0,3},{1,0},{2,1},{3,2},{4,7},{5,4},{6,5},{7,6},{8,11},{9,8},{10,9... | collective-permute-start | bytes 196616 | tf_op jit(solution)/shard_map/ppermute | solution.py:355
  97.8 6.2 %collective-permute-start.24 = (bf16[4,32,256]{2,1,0:T(8,128)(2,1)S(1)}, bf16[4,32,256]{2,1,0:T(8,128)(2,1)S(1)}, u32[]{:S(2)}, u32[]{:S(2)}) collective-permute-start(bf16[4,32,256]{2,1,0:T(8,128)(2,1)S(1)} %slice.131), channel_id=1, source_target_pairs={{0,1},{1,2},{2,3},{3,0},{4,5},{5,6},{6,7},{7,4},{8,9},{9,10},{10,1... | collective-permute-start | bytes 196616 | tf_op jit(solution)/shard_map/ppermute | solution.py:355

commit v5 on v4

--- a/solution.py
+++ b/solution.py
@@ -22,13 +22,14 @@
     return 0.5 + 0.5 * t + (0.5 * v) * (1.0 - t * t) * (c + (3.0 * c * 0.044715) * v2)
 
 
+LATE = pl.CostEstimate(flops=10**10, bytes_accessed=32 << 20, transcendentals=0)
 VMEM = pl.BlockSpec(memory_space=pltpu.VMEM)
 SMALL = pltpu.CompilerParams(vmem_limit_bytes=16 << 20)
 FREE = pl.CostEstimate(flops=0, bytes_accessed=0, transcendentals=0)
 SMEM = pl.BlockSpec(memory_space=pltpu.SMEM)
 
 
-def on_chip(kernel, name, at, operands, shapes, stored=(), limit=16 << 20, **more):
+def on_chip(kernel, name, at, operands, shapes, stored=(), limit=16 << 20, cost=FREE, **more):
     held = [pltpu.with_memory_space_constraint(a, pltpu.VMEM) for a in operands]
     held += [pltpu.with_memory_space_constraint(a, pltpu.HBM) for a in stored]
     out = [pltpu.VMEM(shape, dtype) for shape, dtype in shapes]
@@ -38,7 +39,7 @@
         out_specs=[VMEM] * len(out),
         out_shape=out,
         compiler_params=pltpu.CompilerParams(vmem_limit_bytes=limit),
-        cost_estimate=FREE,
+        cost_estimate=cost,
         name=name,
         **more,
     )(at, *held)
@@ -108,6 +109,27 @@
         cost_estimate=FREE,
         name="turned",
     )(cotangent, pltpu.with_memory_space_constraint(earlier, pltpu.VMEM))
+
+
+def fetch_kernel(parts, at_ref, later_ref, a_hbm, out, arrived):
+    copies = [pltpu.make_async_copy(a_hbm.at[j], out.at[j], arrived.at[j]) for j in range(parts)]
+    for copy in copies:
+        copy.start()
+    for copy in copies:
+        copy.wait()
+
+
+def fetched(at, a, earlier):
+    parts = a.shape[0]
+    return on_chip(
+        functools.partial(fetch_kernel, parts),
+        "fetched",
+        at,
+        [earlier],
+        [(a.shape, a.dtype)],
+        stored=[a],
+        scratch_shapes=[pltpu.SemaphoreType.DMA((parts,))],
+    )[0]
 
 
 def assemble_kernel(local, kd, orders, at_ref, own_ref, *refs):
@@ -130,13 +152,7 @@
 def layer_kernel(nz, local, width, cols, chunk, at_ref, *refs):
     x_refs = refs[:nz]
     f_ref, cot_ref, s_ref = refs[nz : nz + 3]
-    if chunk == 0:
-        s_hbm, *dx_refs, og_ref, s_ref, mixed, back, arrived = refs[-(nz + 6) :]
-        fetch = [pltpu.make_async_copy(s_hbm.at[j], s_ref.at[j], arrived.at[j]) for j in range(local)]
-        for copy in fetch:
-            copy.start()
-    else:
-        *dx_refs, og_ref, mixed, back = refs[-(nz + 3) :]
+    *dx_refs, og_ref, mixed, back = refs[-(nz + 3) :]
     z = at_ref[0]
     group = cols // local
     rows, out_width = dx_refs[0].shape[0], mixed.shape[2]
@@ -157,8 +173,6 @@
     planes = [lax.rem(z + r, nz) for r in range(nz)]
 
     for j in range(local):
-        if chunk == 0:
-            fetch[j].wait()
         weight = jnp.concatenate(
             [s_ref[j, pl.ds(pl.multiple_of(p * cols, cols), cols), :] for p in planes], axis=0
         )
@@ -191,17 +205,12 @@
         functools.partial(layer_kernel, nz, local, width, cols, chunk),
         "layer",
         at,
-        list(xs) + [first, cot] + (list(later) if chunk == 0 else [second]),
-        [(piece, F32)]
-        + [(piece, BF16)] * (nz - 1)
-        + [((nz, rows, local * cols), BF16)]
-        + [(second.shape, BF16)] * (chunk == 0),
+        list(xs) + [first, cot, second, *later],
+        [(piece, F32)] + [(piece, BF16)] * (nz - 1) + [((nz, rows, local * cols), BF16)],
         scratch_shapes=[
             pltpu.VMEM((local, rows, out_width), BF16),
             pltpu.VMEM((local, rows, out_width), F32),
-        ]
-        + [pltpu.SemaphoreType.DMA((local,))] * (chunk == 0),
-        stored=[second] if chunk == 0 else (),
+        ],
     )
 
 
@@ -253,6 +262,7 @@
         at,
         [a for pair in pairs for a in pair if a is not None] + list(earlier),
         [(part.shape, BF16) for part, _ in pairs],
+        cost=LATE,
     )
 
 
@@ -264,6 +274,7 @@
         list(values) + list(earlier),
         [(v.shape, v.dtype) for v in values],
         stored=stored,
+        cost=LATE,
     )
 
 
@@ -279,9 +290,18 @@
         out_specs=VMEM,
         out_shape=pltpu.VMEM((8, 128), F32),
         compiler_params=SMALL,
-        cost_estimate=pl.CostEstimate(flops=10**10, bytes_accessed=32 << 20, transcendentals=0),
+        cost_estimate=LATE,
         name="mark",
     )(at, *held)
+
+
+def pass_kernel(at_ref, first_ref, *refs):
+    inputs_hbm, first_out, second_out, arrived = refs[-4:]
+    rows = second_out.shape[0]
+    copy = pltpu.make_async_copy(inputs_hbm.at[pl.ds(rows, rows)], second_out, arrived)
+    copy.start()
+    first_out[...] = first_ref[...]
+    copy.wait()
 
 
 def halved_kernel(count, at_ref, *refs):
@@ -335,14 +355,14 @@
 def place(at, pieces, factor):
     nz = len(pieces)
     local, kd, cols = pieces[0].shape
-    held = [pltpu.with_memory_space_constraint(a, pltpu.VMEM) for a in [*pieces, mark(at, pieces[1:])]]
+    held = [pltpu.with_memory_space_constraint(a, pltpu.VMEM) for a in pieces]
     return pl.pallas_call(
         functools.partial(place_kernel, nz, local, cols, factor),
-        in_specs=[SMEM] + [VMEM] * (nz + 1),
+        in_specs=[SMEM] + [VMEM] * nz,
         out_specs=VMEM,
         out_shape=jax.ShapeDtypeStruct((kd, local, nz * cols), F32),
         compiler_params=SMALL,
-        cost_estimate=FREE,
+        cost_estimate=LATE,
         name="place",
     )(at, *held)
 
@@ -373,14 +393,22 @@
     bits = nd.bit_length() - 1
     orders = [list(range(1, bits)), list(range(bits - 1, 0, -1))]
 
-    xs = [[inputs[c * rows : (c + 1) * rows]] + [None] * (nz - 1) for c in range(2)]
+    xs = [[inputs[:rows]] + [None] * (nz - 1), [None] * nz]
     xs[0][3] = ring_step(xs[0][0], 1, nz)
     xs[0][1] = ring_step(xs[0][0], -1, nz)
     second = second_factor.transpose(1, 0, 2)
     sends = cut(at, first_factor, nz, nd)
     got = [ring_step(sends[r - 1], -r, nz) for r in range(1, nz)]
-    near = mark(at, [xs[0][3], xs[0][1]])
-    xs[0][3], xs[1][0] = after(at, [xs[0][3], xs[1][0]], near, *got, stored=[second])
+    xs[0][3], xs[1][0] = on_chip(
+        pass_kernel,
+        "pass_on",
+        at,
+        [xs[0][3], xs[0][1], *got],
+        [(xs[0][0].shape, BF16)] * 2,
+        stored=[second, inputs],
+        cost=LATE,
+        scratch_shapes=[pltpu.SemaphoreType.DMA],
+    )
     xs[0][2] = ring_step(xs[0][3], 1, nz)
     xs[1][1] = ring_step(xs[1][0], -1, nz)
     xs[1][3] = ring_step(xs[1][0], 1, nz)
@@ -401,18 +429,18 @@
         [own] + pieces,
         [((nz * local, width, cols), BF16)],
     )[0]
-    far = mark(at, [xs[0][2], xs[1][1], xs[1][3], own, cot])
-    (xs[1][1],) = after(at, [xs[1][1]], far)
+    second = fetched(at, second, others[0])
+    (xs[1][1],) = after(at, [xs[1][1]], xs[0][2], xs[1][3], own, cot, second)
     xs[1][2] = ring_step(xs[1][1], -1, nz)
 
     low = layer(at, xs[0], first, second, cot, [xs[1][1]], 0, rows, nz, local, width, cols)
     low_far = ring_step(low[2], 1, nz)
     low_down = ring_step(low[3], -1, nz)
-    high = layer(at, xs[1], first, low[-1], cot, [], 1, rows, nz, local, width, cols)
+    high = layer(at, xs[1], first, second, cot, [], 1, rows, nz, local, width, cols)
     high_far = ring_step(high[2], -1, nz)
     high_up = ring_step(high[1], 1, nz)
     give, keep = first_grad_terms(at, xs, [low[nz], high[nz]], [], nz, local, width, cols, nd)
-    sent = sums(at, [(low[1], low_far)], mark(at, [low_far, low_down, give]))
+    sent = sums(at, [(low[1], low_far)], low_down, give)
     low_up = ring_step(sent[0], 1, nz)
 
     got = lax.ppermute(give, "dp", swap(0, nd))
@@ -433,7 +461,7 @@
             give.append(pick(1).astype(BF16))
             totals[i] = pick(0)
         if k == 0:
-            sent = sums(at, [(high[3], high_far)], mark(at, [high_far, *give]))
+            sent = sums(at, [(high[3], high_far)], *give)
         for i in range(2):
             totals[i] = totals[i] + lax.ppermute(give[i], "dp", swap(orders[i][k], nd)).astype(F32)
     high_down = ring_step(sent[0], -1, nz)

time: 106 us -> 104 us (0.981)
  starting transfers between devices: 40 us -> 36.8 us
    ppermute x18, starting transfers between devices: 31.3 us -> 27.6 us  [ring_step(): lax.ppermute(value, 'tensor', [(i, (i + step) % nz) for i in range(nz)])]
    pallas_call x9 -> x10, Pallas kernels: 18.7 us -> 22 us  [on_chip(): pl.pallas_call(kernel, in_specs=[SMEM] + [VMEM] * len(operands) + [pl.Blo...]
    pallas_call x6 -> x1, Pallas kernels: 3.25 us -> 0.54 us  [mark(): pl.pallas_call(mark_kernel, in_specs=[SMEM] + [VMEM] * len(held), out_spe...]
    ppermute x4, waiting for transfers between devices: 6.24 us -> 4.29 us  [double_over_dp(): got = lax.ppermute(part, 'dp', swap(bit, nd))]
    ppermute x18, waiting for transfers between devices: 11.6 us -> 13.3 us  [ring_step(): lax.ppermute(value, 'tensor', [(i, (i + step) % nz) for i in range(nz)])]
  transfers between devices with their start and end apart: 29 -> 29, of which waited for: 9 -> 11; matrix products, arithmetic and copies ran while one was open for 10% -> 10% of each run, Pallas kernels for 24% -> 25%
where the time goes in v5:
time: 104 us
  starting transfers between devices  36.8 us (35%)
  Pallas kernels  29.6 us (28%)
  waiting for transfers between devices  21.8 us (21%)
  local copies, waits for them, and re-layouts  13.9 us (13%)
    ppermute x18, starting transfers between devices, ring_step(): lax.ppermute(value, 'tensor', [(i, (i + step) % nz) for i in range(nz)])  27.6 us
    pallas_call x10, Pallas kernels, on_chip(): pl.pallas_call(kernel, in_specs=[SMEM] + [VMEM] * len(operands) + [pl.Blo...  22 us
    ppermute x18, waiting for transfers between devices, ring_step(): lax.ppermute(value, 'tensor', [(i, (i + step) % nz) for i in range(nz)])  13.3 us
    unnamed x11, local copies, waits for them, and re-layouts  12.8 us
    ppermute x4, starting transfers between devices, body(): lax.ppermute(give[i], 'dp', swap(orders[i][k], nd)).astype(F32)  4.76 us
    ppermute x4, waiting for transfers between devices, double_over_dp(): got = lax.ppermute(part, 'dp', swap(bit, nd))  4.29 us
    ppermute x4, starting transfers between devices, double_over_dp(): got = lax.ppermute(part, 'dp', swap(bit, nd))  4.25 us
    ppermute x4, waiting for transfers between devices, body(): lax.ppermute(give[i], 'dp', swap(orders[i][k], nd)).astype(F32)  4.23 us
  transfers between devices with their start and end apart: 29, of which 11 were waited for; matrix products, arithmetic and copies ran while one was open for 10% of the time, Pallas kernels for 25%

profile of v5, /device:TPU:0, one launch (start us, length us, event | category | flops | bytes accessed | tf_op | source)
XLA Modules:
  0.0 104.0 jit_solution(7507289442437361360)
XLA Ops:
  0.6 1.0 slice.66.refs_0_
  1.6 3.1 %collective-permute-start.1 = (bf16[128,1024]{1,0:T(8,128)(2,1)S(1)}, bf16[128,1024]{1,0:T(8,128)(2,1)S(1)}, u32[]{:S(2)}, u32[]{:S(2)}) collective-permute-start(bf16[128,1024]{1,0:T(8,128)(2,1)S(1)} %slice.66.refs_0_), channel_id=1, source_target_pairs={{0,1},{1,2},{2,3},{3,0},{4,5},{5,6},{6,7},{7,4},{8,9},{9,10},{10,1... | collective-permute-start | bytes 786440 | tf_op jit(solution)/shard_map/ppermute | solution.py:375
  4.7 2.1 %collective-permute-start = (bf16[128,1024]{1,0:T(8,128)(2,1)S(1)}, bf16[128,1024]{1,0:T(8,128)(2,1)S(1)}, u32[]{:S(2)}, u32[]{:S(2)}) collective-permute-start(bf16[128,1024]{1,0:T(8,128)(2,1)S(1)} %slice.66.refs_0_), channel_id=1, source_target_pairs={{0,3},{1,0},{2,1},{3,2},{4,7},{5,4},{6,5},{7,6},{8,11},{9,8},{10,9... | collective-permute-start | bytes 786440 | tf_op jit(solution)/shard_map/ppermute | solution.py:375
  6.8 0.1 pad_add_fusion.at_ref
  6.8 1.6 %copy-done = bf16[256,4,1024]{2,1,0:T(4,128)(2,1)S(1)} copy-done((bf16[256,4,1024]{2,1,0:T(4,128)(2,1)S(1)}, bf16[256,4,1024]{2,1,0:T(4,128)(2,1)}, u32[]{:S(2)}) %copy-start) | copy-done | bytes 2097176
  8.4 0.8 cut.1
  9.3 2.0 %collective-permute-start.2 = (bf16[4,32,256]{2,1,0:T(8,128)(2,1)S(1)}, bf16[4,32,256]{2,1,0:T(8,128)(2,1)S(1)}, u32[]{:S(2)}, u32[]{:S(2)}) collective-permute-start(bf16[4,32,256]{2,1,0:T(8,128)(2,1)S(1)} %get-tuple-element.21), channel_id=1, source_target_pairs={{0,3},{1,0},{2,1},{3,2},{4,7},{5,4},{6,5},{7,6},{8,11},{9,8},{10,9... | collective-permute-start | bytes 196616 | tf_op jit(solution)/shard_map/ppermute | solution.py:375
  11.3 1.0 collective-permute-start.4
  12.3 9.5 %copy.13 = bf16[1024,4,1024]{2,0,1:T(8,128)(2,1)} copy(bf16[1024,4,1024]{2,1,0:T(4,128)(2,1)} %param.6) | data formatting | bytes 16777216 | tf_op args[2]
  21.8 2.4 %collective-permute-done.3.refs_2_.refs_1_ = bf16[4,32,256]{2,1,0:T(8,128)(2,1)S(1)} collective-permute-done((bf16[4,32,256]{2,1,0:T(8,128)(2,1)S(1)}, bf16[4,32,256]{2,1,0:T(8,128)(2,1)S(1)}, u32[]{:S(2)}, u32[]{:S(2)}) %collective-permute-start.3) | collective-permute-done | bytes 65568 | tf_op jit(solution)/shard_map/ppermute | solution.py:375
  24.3 0.7 copy-done.3
  25.0 0.9 copy-done.4
  25.9 1.6 %pass_on.1 = (bf16[128,1024]{1,0:T(8,128)(2,1)S(1)}, bf16[128,1024]{1,0:T(8,128)(2,1)S(1)}) custom-call(s32[2]{0:T(128)S(1)} %pad_add_fusion.at_ref, bf16[128,1024]{1,0:T(8,128)(2,1)S(1)} %copy-done.4, bf16[128,1024]{1,0:T(8,128)(2,1)S(1)} %collective-permute-done.refs_0_.refs_1_, bf16[4,32,256]{2,1,0:T(8,128)(2,1)S(1)} %collective-permute-done.2.refs_1_.refs_0_, ...), custom_call_target="tpu_custom_call" | custom-call | flops 10000000000 | bytes 33554432 | tf_op jit(solution)/shard_map/pass_on/pallas_call | solution.py:36
  27.5 0.6 halved.1
  28.1 1.6 %collective-permute-start.6 = (bf16[6,32,256]{2,1,0:T(8,128)(2,1)S(1)}, bf16[6,32,256]{2,1,0:T(8,128)(2,1)S(1)}, u32[]{:S(2)}, u32[]{:S(2)}) collective-permute-start(bf16[6,32,256]{2,1,0:T(8,128)(2,1)S(1)} %get-tuple-element.25), channel_id=1, source_target_pairs={{0,8},{4,12},{8,0},{12,4},{16,24},{20,28},{24,16},{28,20},{1,9},{5... | collective-permute-start | bytes 294920 | tf_op jit(solution)/shard_map/ppermute | solution.py:379
  29.6 0.1 collective-permute-start.5
  29.7 1.2 %collective-permute-start.13 = (bf16[128,1024]{1,0:T(8,128)(2,1)S(1)}, bf16[128,1024]{1,0:T(8,128)(2,1)S(1)}, u32[]{:S(2)}, u32[]{:S(2)}) collective-permute-start(bf16[128,1024]{1,0:T(8,128)(2,1)S(1)} %get-tuple-element.27.refs_0_.refs_4_), channel_id=1, source_target_pairs={{0,1},{1,2},{2,3},{3,0},{4,5},{5,6},{6,7},{7,4},{8,9},{9,10},{10,1... | collective-permute-start | bytes 786440 | tf_op jit(solution)/shard_map/ppermute | solution.py:375
  30.9 2.6 %collective-permute-start.12 = (bf16[128,1024]{1,0:T(8,128)(2,1)S(1)}, bf16[128,1024]{1,0:T(8,128)(2,1)S(1)}, u32[]{:S(2)}, u32[]{:S(2)}) collective-permute-start(bf16[128,1024]{1,0:T(8,128)(2,1)S(1)} %get-tuple-element.27.refs_0_.refs_4_), channel_id=1, source_target_pairs={{0,3},{1,0},{2,1},{3,2},{4,7},{5,4},{6,5},{7,6},{8,11},{9,8},{10,9... | collective-permute-start | bytes 786440 | tf_op jit(solution)/shard_map/ppermute | solution.py:375
  33.5 1.5 %collective-permute-start.9 = (bf16[6,32,256]{2,1,0:T(8,128)(2,1)S(1)}, bf16[6,32,256]{2,1,0:T(8,128)(2,1)S(1)}, u32[]{:S(2)}, u32[]{:S(2)}) collective-permute-start(bf16[6,32,256]{2,1,0:T(8,128)(2,1)S(1)} %get-tuple-element.26), channel_id=1, source_target_pairs={{0,16},{4,20},{8,24},{12,28},{16,0},{20,4},{24,8},{28,12},{1,17},{... | collective-permute-start | bytes 294920 | tf_op jit(solution)/shard_map/ppermute | solution.py:379
  35.1 0.6 collective-permute-start.7
  35.7 3.4 %collective-permute-done.9 = bf16[6,32,256]{2,1,0:T(8,128)(2,1)S(1)} collective-permute-done((bf16[6,32,256]{2,1,0:T(8,128)(2,1)S(1)}, bf16[6,32,256]{2,1,0:T(8,128)(2,1)S(1)}, u32[]{:S(2)}, u32[]{:S(2)}) %collective-permute-start.9) | collective-permute-done | bytes 98336 | tf_op jit(solution)/shard_map/ppermute | solution.py:379
  39.2 2.0 %own_columns.1.own_ref.refs_3_ = bf16[4,256,256]{2,1,0:T(8,128)(2,1)S(1)} custom-call(s32[2]{0:T(128)S(1)} %pad_add_fusion.at_ref, bf16[256,4,1024]{2,1,0:T(4,128)(2,1)S(1)} %copy-done.1, bf16[2,6,32,256]{3,2,1,0:T(8,128)(2,1)S(1)} %pad_maximum_fusion.2.later_ref), custom_call_target="tpu_custom_call" | custom-call | tf_op jit(solution)/shard_map/own_columns/pallas_call | solution.py:81
  41.2 0.6 collective-permute-start.10
  41.8 0.1 collective-permute-done.7
  42.0 0.0 copy-start.2
  42.0 4.1 %fetched.1.refs_5_.refs_6_ = bf16[4,1024,1024]{2,1,0:T(8,128)(2,1)S(1)} custom-call(s32[2]{0:T(128)S(1)} %pad_add_fusion.at_ref, bf16[2,2,6,32,256]{4,3,2,1,0:T(8,128)(2,1)S(1)} %pad_maximum_fusion.refs_0_.later_ref, bf16[4,1024,1024]{2,1,0:T(8,128)(2,1)} %bitcast.51), custom_call_target="tpu_custom_call" | custom-call | tf_op jit(solution)/shard_map/fetched/pallas_call | solution.py:36
  46.1 0.1 collective-permute-start.8
  46.2 0.7 collective-permute-done.10
  47.0 0.1 collective-permute-start.11
  47.1 1.2 %turned.1.refs_4_.refs_5_ = bf16[256,4096]{1,0:T(8,128)(2,1)S(1)} custom-call(bf16[4096,256]{1,0:T(8,128)(2,1)S(1)} %copy-done.2, bf16[2,2,6,32,256]{4,3,2,1,0:T(8,128)(2,1)S(1)} %pad_maximum_fusion.1.refs_2_.later_ref), custom_call_target="tpu_custom_call" | custom-call | tf_op jit(solution)/shard_map/turned/pallas_call | solution.py:102
  48.3 0.5 collective-permute-done.12.refs_0_
  48.8 0.6 after.1.refs_7_.refs_1_.refs_5_
  49.4 2.1 %collective-permute-start.16 = (bf16[128,1024]{1,0:T(8,128)(2,1)S(1)}, bf16[128,1024]{1,0:T(8,128)(2,1)S(1)}, u32[]{:S(2)}, u32[]{:S(2)}) collective-permute-start(bf16[128,1024]{1,0:T(8,128)(2,1)S(1)} %after.1.refs_7_.refs_1_.refs_5_), channel_id=1, source_target_pairs={{0,3},{1,0},{2,1},{3,2},{4,7},{5,4},{6,5},{7,6},{8,11},{9,8},{10,9... | collective-permute-start | bytes 786440 | tf_op jit(solution)/shard_map/ppermute | solution.py:375
  51.5 0.7 assemble.1.refs_4_
  52.2 5.9 %layer.2 = (f32[128,1024]{1,0:T(8,128)S(1)}, bf16[128,1024]{1,0:T(8,128)(2,1)S(1)}, bf16[128,1024]{1,0:T(8,128)(2,1)S(1)}, bf16[128,1024]{1,0:T(8,128)(2,1)S(1)}, bf16[4,128,1024]{2,1,0:T(8,128)(2,1)S(1)}) custom-call(s32[2]{0:T(128)S(1)} %pad_add_fusion.at_ref, bf16[128,1024]{1,0:T(8,128)(2,1)S(1)} %slice.66.refs_0_, ...), custom_call_target="tpu_custom_call" | custom-call | tf_op jit(solution)/shard_map/layer/pallas_call | solution.py:36
  58.2 0.4 collective-permute-start.14
  58.5 3.5 %collective-permute-start.15 = (bf16[128,1024]{1,0:T(8,128)(2,1)S(1)}, bf16[128,1024]{1,0:T(8,128)(2,1)S(1)}, u32[]{:S(2)}, u32[]{:S(2)}) collective-permute-start(bf16[128,1024]{1,0:T(8,128)(2,1)S(1)} %get-tuple-element.31), channel_id=1, source_target_pairs={{0,3},{1,0},{2,1},{3,2},{4,7},{5,4},{6,5},{7,6},{8,11},{9,8},{10,9... | collective-permute-start | bytes 786440 | tf_op jit(solution)/shard_map/ppermute | solution.py:375
  62.0 5.9 %layer.3 = (f32[128,1024]{1,0:T(8,128)S(1)}, bf16[128,1024]{1,0:T(8,128)(2,1)S(1)}, bf16[128,1024]{1,0:T(8,128)(2,1)S(1)}, bf16[128,1024]{1,0:T(8,128)(2,1)S(1)}, bf16[4,128,1024]{2,1,0:T(8,128)(2,1)S(1)}) custom-call(s32[2]{0:T(128)S(1)} %pad_add_fusion.at_ref, bf16[128,1024]{1,0:T(8,128)(2,1)S(1)} %get-tuple-element.27.refs_0_.refs_4_, ...), custom_call_target="tpu_custom_call" | custom-call | tf_op jit(solution)/shard_map/layer/pallas_call | solution.py:36
  68.0 1.4 %first_grad_terms.1 = (bf16[4,16,32,256]{3,2,1,0:T(8,128)(2,1)S(1)}, bf16[4,16,32,256]{3,2,1,0:T(8,128)(2,1)S(1)}) custom-call(s32[2]{0:T(128)S(1)} %pad_add_fusion.at_ref, bf16[128,1024]{1,0:T(8,128)(2,1)S(1)} %slice.66.refs_0_, bf16[128,1024]{1,0:T(8,128)(2,1)S(1)} %collective-permute-done.refs_0_.refs_1_, ...), custom_call_target="tpu_custom_call" | custom-call | tf_op jit(solution)/shard_map/first_grad_terms/pallas_call | solution.py:36
  69.4 0.1 collective-permute-start.20
  69.4 0.1 collective-permute-start.18
  69.5 3.8 %collective-permute-start.19 = (bf16[128,1024]{1,0:T(8,128)(2,1)S(1)}, bf16[128,1024]{1,0:T(8,128)(2,1)S(1)}, u32[]{:S(2)}, u32[]{:S(2)}) collective-permute-start(bf16[128,1024]{1,0:T(8,128)(2,1)S(1)} %get-tuple-element.38), channel_id=1, source_target_pairs={{0,3},{1,0},{2,1},{3,2},{4,7},{5,4},{6,5},{7,6},{8,11},{9,8},{10,9... | collective-permute-start | bytes 786440 | tf_op jit(solution)/shard_map/ppermute | solution.py:375
  73.3 0.6 sums.2
  73.9 0.8 collective-permute-start.17
  74.8 0.4 convert_add_fusion
  75.2 0.8 collective-permute-start.22
  76.1 1.7 %collective-permute-start.25 = (bf16[2,8,32,256]{3,2,1,0:T(8,128)(2,1)S(1)}, bf16[2,8,32,256]{3,2,1,0:T(8,128)(2,1)S(1)}, u32[]{:S(2)}, u32[]{:S(2)}) collective-permute-start(bf16[2,8,32,256]{3,2,1,0:T(8,128)(2,1)S(1)} %fusion.2.refs_3_), channel_id=1, source_target_pairs={{0,16},{4,20},{8,24},{12,28},{16,0},{20,4},{24,8},{28,12},{1,17},{... | collective-permute-start | bytes 786440 | tf_op jit(solution)/shard_map/ppermute | solution.py:466
  77.8 6.0 %collective-permute-done.19.refs_1_ = bf16[128,1024]{1,0:T(8,128)(2,1)S(1)} collective-permute-done((bf16[128,1024]{1,0:T(8,128)(2,1)S(1)}, bf16[128,1024]{1,0:T(8,128)(2,1)S(1)}, u32[]{:S(2)}, u32[]{:S(2)}) %collective-permute-start.19) | collective-permute-done | bytes 262176 | tf_op jit(solution)/shard_map/ppermute | solution.py:375
  83.8 0.6 sums.3
  84.4 2.4 %collective-permute-start.21 = (bf16[128,1024]{1,0:T(8,128)(2,1)S(1)}, bf16[128,1024]{1,0:T(8,128)(2,1)S(1)}, u32[]{:S(2)}, u32[]{:S(2)}) collective-permute-start(bf16[128,1024]{1,0:T(8,128)(2,1)S(1)} %sums.3), channel_id=1, source_target_pairs={{0,3},{1,0},{2,1},{3,2},{4,7},{5,4},{6,5},{7,6},{8,11},{9,8},{10,9... | collective-permute-start | bytes 786440 | tf_op jit(solution)/shard_map/ppermute | solution.py:375
  86.8 0.1 fusion.1
  86.9 1.6 %collective-permute-start.23 = (bf16[8,32,256]{2,1,0:T(8,128)(2,1)S(1)}, bf16[8,32,256]{2,1,0:T(8,128)(2,1)S(1)}, u32[]{:S(2)}, u32[]{:S(2)}) collective-permute-start(bf16[8,32,256]{2,1,0:T(8,128)(2,1)S(1)} %fusion.7), channel_id=1, source_target_pairs={{0,16},{4,20},{8,24},{12,28},{16,0},{20,4},{24,8},{28,12},{1,17},{... | collective-permute-start | bytes 393224 | tf_op jit(solution)/shard_map/ppermute | solution.py:466
  88.5 0.1 fusion
  88.6 0.7 collective-permute-start.26
  89.3 2.6 %collective-permute-done.23 = bf16[8,32,256]{2,1,0:T(8,128)(2,1)S(1)} collective-permute-done((bf16[8,32,256]{2,1,0:T(8,128)(2,1)S(1)}, bf16[8,32,256]{2,1,0:T(8,128)(2,1)S(1)}, u32[]{:S(2)}, u32[]{:S(2)}) %collective-permute-start.23) | collective-permute-done | bytes 131104 | tf_op jit(solution)/shard_map/ppermute | solution.py:466
  92.0 0.1 collective-permute-start.24
  92.1 1.6 %collective-permute-done.26 = bf16[8,32,256]{2,1,0:T(8,128)(2,1)S(1)} collective-permute-done((bf16[8,32,256]{2,1,0:T(8,128)(2,1)S(1)}, bf16[8,32,256]{2,1,0:T(8,128)(2,1)S(1)}, u32[]{:S(2)}, u32[]{:S(2)}) %collective-permute-start.26) | collective-permute-done | bytes 131104 | tf_op jit(solution)/shard_map/ppermute | solution.py:466
  93.7 2.3 %collective-permute-start.28 = (bf16[4,32,256]{2,1,0:T(8,128)(2,1)S(1)}, bf16[4,32,256]{2,1,0:T(8,128)(2,1)S(1)}, u32[]{:S(2)}, u32[]{:S(2)}) collective-permute-start(bf16[4,32,256]{2,1,0:T(8,128)(2,1)S(1)} %get-tuple-element.50), channel_id=1, source_target_pairs={{0,3},{1,0},{2,1},{3,2},{4,7},{5,4},{6,5},{7,6},{8,11},{9,8},{10,9... | collective-permute-start | bytes 196616 | tf_op jit(solution)/shard_map/ppermute | solution.py:375
  96.0 0.5 mark.1.refs_6_
  96.5 0.9 collective-permute-done.21.refs_5_
  97.4 1.5 %join.1 = bf16[256,1024]{1,0:T(8,128)(2,1)} custom-call(s32[2]{0:T(128)S(1)} %pad_add_fusion.at_ref, f32[128,1024]{1,0:T(8,128)S(1)} %get-tuple-element.28.refs_0_, bf16[128,1024]{1,0:T(8,128)(2,1)S(1)} %collective-permute-done.17.refs_0_.refs_1_, bf16[128,1024]{1,0:T(8,128)(2,1)S(1)} %collective-permute-done.15.refs_2_, ...), custom_call_target="tpu_custom_call" | custom-call | tf_op jit(solution)/shard_map/join/pallas_call | solution.py:336
  98.9 0.7 collective-permute-done.28.refs_3_
  99.7 2.8 %collective-permute-done.27.refs_2_ = bf16[4,32,256]{2,1,0:T(8,128)(2,1)S(1)} collective-permute-done((bf16[4,32,256]{2,1,0:T(8,128)(2,1)S(1)}, bf16[4,32,256]{2,1,0:T(8,128)(2,1)S(1)}, u32[]{:S(2)}, u32[]{:S(2)}) %collective-permute-start.27) | collective-permute-done | bytes 65568 | tf_op jit(solution)/shard_map/ppermute | solution.py:375
  102.5 1.5 %place.1 = f32[32,4,1024]{2,1,0:T(4,128)} custom-call(s32[2]{0:T(128)S(1)} %pad_add_fusion.at_ref, f32[4,32,256]{2,1,0:T(8,128)S(1)} %slice.92.refs_0_, bf16[4,32,256]{2,1,0:T(8,128)(2,1)S(1)} %collective-permute-done.24.refs_1_, bf16[4,32,256]{2,1,0:T(8,128)(2,1)S(1)} %collective-permute-done.27.refs_2_, bf16[4,32,256]{2,1,0:T(8,128)(2,1)S(1)} %collective-permute-done.28.refs_3_), custom_call_target="tpu_custom_call" | custom-call | flops 10000000000 | bytes 33554432 | tf_op jit(solution)/shard_map/place/pallas_call | solution.py:359
  (43 shorter events, 0.5 us)
Async XLA Ops:
  1.6 22.6 %collective-permute-start.1 = (bf16[128,1024]{1,0:T(8,128)(2,1)S(1)}, bf16[128,1024]{1,0:T(8,128)(2,1)S(1)}, u32[]{:S(2)}, u32[]{:S(2)}) collective-permute-start(bf16[128,1024]{1,0:T(8,128)(2,1)S(1)} %slice.66.refs_0_), channel_id=1, source_target_pairs={{0,1},{1,2},{2,3},{3,0},{4,5},{5,6},{6,7},{7,4},{8,9},{9,10},{10,1... | collective-permute-start | bytes 786440 | tf_op jit(solution)/shard_map/ppermute | solution.py:375
  4.7 20.3 %collective-permute-start = (bf16[128,1024]{1,0:T(8,128)(2,1)S(1)}, bf16[128,1024]{1,0:T(8,128)(2,1)S(1)}, u32[]{:S(2)}, u32[]{:S(2)}) collective-permute-start(bf16[128,1024]{1,0:T(8,128)(2,1)S(1)} %slice.66.refs_0_), channel_id=1, source_target_pairs={{0,3},{1,0},{2,1},{3,2},{4,7},{5,4},{6,5},{7,6},{8,11},{9,8},{10,9... | collective-permute-start | bytes 786440 | tf_op jit(solution)/shard_map/ppermute | solution.py:375
  6.8 1.6 %copy-start = (bf16[256,4,1024]{2,1,0:T(4,128)(2,1)S(1)}, bf16[256,4,1024]{2,1,0:T(4,128)(2,1)}, u32[]{:S(2)}) copy-start(bf16[256,4,1024]{2,1,0:T(4,128)(2,1)} %f_ref.3) | copy-start | bytes 6291460
  9.3 12.5 %collective-permute-start.2 = (bf16[4,32,256]{2,1,0:T(8,128)(2,1)S(1)}, bf16[4,32,256]{2,1,0:T(8,128)(2,1)S(1)}, u32[]{:S(2)}, u32[]{:S(2)}) collective-permute-start(bf16[4,32,256]{2,1,0:T(8,128)(2,1)S(1)} %get-tuple-element.21), channel_id=1, source_target_pairs={{0,3},{1,0},{2,1},{3,2},{4,7},{5,4},{6,5},{7,6},{8,11},{9,8},{10,9... | collective-permute-start | bytes 196616 | tf_op jit(solution)/shard_map/ppermute | solution.py:375
  11.3 12.9 %collective-permute-start.3 = (bf16[4,32,256]{2,1,0:T(8,128)(2,1)S(1)}, bf16[4,32,256]{2,1,0:T(8,128)(2,1)S(1)}, u32[]{:S(2)}, u32[]{:S(2)}) collective-permute-start(bf16[4,32,256]{2,1,0:T(8,128)(2,1)S(1)} %get-tuple-element.22), channel_id=1, source_target_pairs={{0,2},{1,3},{2,0},{3,1},{4,6},{5,7},{6,4},{7,5},{8,10},{9,11},{10,... | collective-permute-start | bytes 196616 | tf_op jit(solution)/shard_map/ppermute | solution.py:375
  11.3 12.9 %collective-permute-start.4 = (bf16[4,32,256]{2,1,0:T(8,128)(2,1)S(1)}, bf16[4,32,256]{2,1,0:T(8,128)(2,1)S(1)}, u32[]{:S(2)}, u32[]{:S(2)}) collective-permute-start(bf16[4,32,256]{2,1,0:T(8,128)(2,1)S(1)} %get-tuple-element.23), channel_id=1, source_target_pairs={{0,1},{1,2},{2,3},{3,0},{4,5},{5,6},{6,7},{7,4},{8,9},{9,10},{10,1... | collective-permute-start | bytes 196616 | tf_op jit(solution)/shard_map/ppermute | solution.py:375
  24.3 0.7 copy-start.3
  25.0 1.0 copy-start.4
  25.9 13.2 %copy-start.1 = (bf16[256,4,1024]{2,1,0:T(4,128)(2,1)S(1)}, bf16[256,4,1024]{2,1,0:T(4,128)(2,1)}, u32[]{:S(2)}) copy-start(bf16[256,4,1024]{2,1,0:T(4,128)(2,1)} %f_ref.3) | copy-start | bytes 6291460
  28.1 7.0 %collective-permute-start.6 = (bf16[6,32,256]{2,1,0:T(8,128)(2,1)S(1)}, bf16[6,32,256]{2,1,0:T(8,128)(2,1)S(1)}, u32[]{:S(2)}, u32[]{:S(2)}) collective-permute-start(bf16[6,32,256]{2,1,0:T(8,128)(2,1)S(1)} %get-tuple-element.25), channel_id=1, source_target_pairs={{0,8},{4,12},{8,0},{12,4},{16,24},{20,28},{24,16},{28,20},{1,9},{5... | collective-permute-start | bytes 294920 | tf_op jit(solution)/shard_map/ppermute | solution.py:379
  29.6 18.7 %collective-permute-start.5 = (bf16[128,1024]{1,0:T(8,128)(2,1)S(1)}, bf16[128,1024]{1,0:T(8,128)(2,1)S(1)}, u32[]{:S(2)}, u32[]{:S(2)}) collective-permute-start(bf16[128,1024]{1,0:T(8,128)(2,1)S(1)} %get-tuple-element.24.refs_3_), channel_id=1, source_target_pairs={{0,1},{1,2},{2,3},{3,0},{4,5},{5,6},{6,7},{7,4},{8,9},{9,10},{10,1... | collective-permute-start | bytes 786440 | tf_op jit(solution)/shard_map/ppermute | solution.py:375
  29.7 18.6 %collective-permute-start.13 = (bf16[128,1024]{1,0:T(8,128)(2,1)S(1)}, bf16[128,1024]{1,0:T(8,128)(2,1)S(1)}, u32[]{:S(2)}, u32[]{:S(2)}) collective-permute-start(bf16[128,1024]{1,0:T(8,128)(2,1)S(1)} %get-tuple-element.27.refs_0_.refs_4_), channel_id=1, source_target_pairs={{0,1},{1,2},{2,3},{3,0},{4,5},{5,6},{6,7},{7,4},{8,9},{9,10},{10,1... | collective-permute-start | bytes 786440 | tf_op jit(solution)/shard_map/ppermute | solution.py:375
  30.9 17.9 %collective-permute-start.12 = (bf16[128,1024]{1,0:T(8,128)(2,1)S(1)}, bf16[128,1024]{1,0:T(8,128)(2,1)S(1)}, u32[]{:S(2)}, u32[]{:S(2)}) collective-permute-start(bf16[128,1024]{1,0:T(8,128)(2,1)S(1)} %get-tuple-element.27.refs_0_.refs_4_), channel_id=1, source_target_pairs={{0,3},{1,0},{2,1},{3,2},{4,7},{5,4},{6,5},{7,6},{8,11},{9,8},{10,9... | collective-permute-start | bytes 786440 | tf_op jit(solution)/shard_map/ppermute | solution.py:375
  33.5 5.6 %collective-permute-start.9 = (bf16[6,32,256]{2,1,0:T(8,128)(2,1)S(1)}, bf16[6,32,256]{2,1,0:T(8,128)(2,1)S(1)}, u32[]{:S(2)}, u32[]{:S(2)}) collective-permute-start(bf16[6,32,256]{2,1,0:T(8,128)(2,1)S(1)} %get-tuple-element.26), channel_id=1, source_target_pairs={{0,16},{4,20},{8,24},{12,28},{16,0},{20,4},{24,8},{28,12},{1,17},{... | collective-permute-start | bytes 294920 | tf_op jit(solution)/shard_map/ppermute | solution.py:379
  35.1 6.8 %collective-permute-start.7 = (bf16[2,6,32,256]{3,2,1,0:T(8,128)(2,1)S(1)}, bf16[2,6,32,256]{3,2,1,0:T(8,128)(2,1)S(1)}, u32[]{:S(2)}, u32[]{:S(2)}) collective-permute-start(bf16[2,6,32,256]{3,2,1,0:T(8,128)(2,1)S(1)} %pad_maximum_fusion.2.later_ref), channel_id=1, source_target_pairs={{0,16},{4,20},{8,24},{12,28},{16,0},{20,4},{24,8},{28,12},{1,17},{... | collective-permute-start | bytes 589832 | tf_op jit(solution)/shard_map/ppermute | solution.py:379
  41.2 5.7 %collective-permute-start.10 = (bf16[2,6,32,256]{3,2,1,0:T(8,128)(2,1)S(1)}, bf16[2,6,32,256]{3,2,1,0:T(8,128)(2,1)S(1)}, u32[]{:S(2)}, u32[]{:S(2)}) collective-permute-start(bf16[2,6,32,256]{3,2,1,0:T(8,128)(2,1)S(1)} %pad_maximum_fusion.3), channel_id=1, source_target_pairs={{0,8},{4,12},{8,0},{12,4},{16,24},{20,28},{24,16},{28,20},{1,9},{5... | collective-permute-start | bytes 589832 | tf_op jit(solution)/shard_map/ppermute | solution.py:379
  42.0 5.1 %copy-start.2 = (bf16[4096,256]{1,0:T(8,128)(2,1)S(1)}, bf16[4096,256]{1,0:T(8,128)(2,1)}, u32[]{:S(2)}) copy-start(bf16[4096,256]{1,0:T(8,128)(2,1)} %x_ref.1) | copy-start | bytes 6291460
  46.1 5.4 %collective-permute-start.8 = (bf16[2,2,6,32,256]{4,3,2,1,0:T(8,128)(2,1)S(1)}, bf16[2,2,6,32,256]{4,3,2,1,0:T(8,128)(2,1)S(1)}, u32[]{:S(2)}, u32[]{:S(2)}) collective-permute-start(bf16[2,2,6,32,256]{4,3,2,1,0:T(8,128)(2,1)S(1)} %pad_maximum_fusion.refs_0_.later_ref), channel_id=1, source_target_pairs={{0,4},{4,0},{8,12},{12,8},{16,20},{20,16},{24,28},{28,24},{1,5},{5... | collective-permute-start | bytes 1179656 | tf_op jit(solution)/shard_map/ppermute | solution.py:424
  47.0 4.5 %collective-permute-start.11 = (bf16[2,2,6,32,256]{4,3,2,1,0:T(8,128)(2,1)S(1)}, bf16[2,2,6,32,256]{4,3,2,1,0:T(8,128)(2,1)S(1)}, u32[]{:S(2)}, u32[]{:S(2)}) collective-permute-start(bf16[2,2,6,32,256]{4,3,2,1,0:T(8,128)(2,1)S(1)} %pad_maximum_fusion.1.refs_2_.later_ref), channel_id=1, source_target_pairs={{0,4},{4,0},{8,12},{12,8},{16,20},{20,16},{24,28},{28,24},{1,5},{5... | collective-permute-start | bytes 1179656 | tf_op jit(solution)/shard_map/ppermute | solution.py:424
  49.4 12.7 %collective-permute-start.16 = (bf16[128,1024]{1,0:T(8,128)(2,1)S(1)}, bf16[128,1024]{1,0:T(8,128)(2,1)S(1)}, u32[]{:S(2)}, u32[]{:S(2)}) collective-permute-start(bf16[128,1024]{1,0:T(8,128)(2,1)S(1)} %after.1.refs_7_.refs_1_.refs_5_), channel_id=1, source_target_pairs={{0,3},{1,0},{2,1},{3,2},{4,7},{5,4},{6,5},{7,6},{8,11},{9,8},{10,9... | collective-permute-start | bytes 786440 | tf_op jit(solution)/shard_map/ppermute | solution.py:375
  58.2 15.2 %collective-permute-start.14 = (bf16[128,1024]{1,0:T(8,128)(2,1)S(1)}, bf16[128,1024]{1,0:T(8,128)(2,1)S(1)}, u32[]{:S(2)}, u32[]{:S(2)}) collective-permute-start(bf16[128,1024]{1,0:T(8,128)(2,1)S(1)} %get-tuple-element.30), channel_id=1, source_target_pairs={{0,1},{1,2},{2,3},{3,0},{4,5},{5,6},{6,7},{7,4},{8,9},{9,10},{10,1... | collective-permute-start | bytes 786440 | tf_op jit(solution)/shard_map/ppermute | solution.py:375
  58.5 14.8 %collective-permute-start.15 = (bf16[128,1024]{1,0:T(8,128)(2,1)S(1)}, bf16[128,1024]{1,0:T(8,128)(2,1)S(1)}, u32[]{:S(2)}, u32[]{:S(2)}) collective-permute-start(bf16[128,1024]{1,0:T(8,128)(2,1)S(1)} %get-tuple-element.31), channel_id=1, source_target_pairs={{0,3},{1,0},{2,1},{3,2},{4,7},{5,4},{6,5},{7,6},{8,11},{9,8},{10,9... | collective-permute-start | bytes 786440 | tf_op jit(solution)/shard_map/ppermute | solution.py:375
  69.4 5.4 %collective-permute-start.20 = (bf16[4,16,32,256]{3,2,1,0:T(8,128)(2,1)S(1)}, bf16[4,16,32,256]{3,2,1,0:T(8,128)(2,1)S(1)}, u32[]{:S(2)}, u32[]{:S(2)}) collective-permute-start(bf16[4,16,32,256]{3,2,1,0:T(8,128)(2,1)S(1)} %get-tuple-element.34.refs_3_), channel_id=1, source_target_pairs={{0,4},{4,0},{8,12},{12,8},{16,20},{20,16},{24,28},{28,24},{1,5},{5... | collective-permute-start | bytes 3145736 | tf_op jit(solution)/shard_map/ppermute | solution.py:446
  69.4 26.5 %collective-permute-start.18 = (bf16[128,1024]{1,0:T(8,128)(2,1)S(1)}, bf16[128,1024]{1,0:T(8,128)(2,1)S(1)}, u32[]{:S(2)}, u32[]{:S(2)}) collective-permute-start(bf16[128,1024]{1,0:T(8,128)(2,1)S(1)} %get-tuple-element.36), channel_id=1, source_target_pairs={{0,1},{1,2},{2,3},{3,0},{4,5},{5,6},{6,7},{7,4},{8,9},{9,10},{10,1... | collective-permute-start | bytes 786440 | tf_op jit(solution)/shard_map/ppermute | solution.py:375
  69.5 14.3 %collective-permute-start.19 = (bf16[128,1024]{1,0:T(8,128)(2,1)S(1)}, bf16[128,1024]{1,0:T(8,128)(2,1)S(1)}, u32[]{:S(2)}, u32[]{:S(2)}) collective-permute-start(bf16[128,1024]{1,0:T(8,128)(2,1)S(1)} %get-tuple-element.38), channel_id=1, source_target_pairs={{0,3},{1,0},{2,1},{3,2},{4,7},{5,4},{6,5},{7,6},{8,11},{9,8},{10,9... | collective-permute-start | bytes 786440 | tf_op jit(solution)/shard_map/ppermute | solution.py:375
  73.9 22.1 %collective-permute-start.17 = (bf16[128,1024]{1,0:T(8,128)(2,1)S(1)}, bf16[128,1024]{1,0:T(8,128)(2,1)S(1)}, u32[]{:S(2)}, u32[]{:S(2)}) collective-permute-start(bf16[128,1024]{1,0:T(8,128)(2,1)S(1)} %sums.2), channel_id=1, source_target_pairs={{0,1},{1,2},{2,3},{3,0},{4,5},{5,6},{6,7},{7,4},{8,9},{9,10},{10,1... | collective-permute-start | bytes 786440 | tf_op jit(solution)/shard_map/ppermute | solution.py:375
  75.2 11.6 %collective-permute-start.22 = (bf16[2,8,32,256]{3,2,1,0:T(8,128)(2,1)S(1)}, bf16[2,8,32,256]{3,2,1,0:T(8,128)(2,1)S(1)}, u32[]{:S(2)}, u32[]{:S(2)}) collective-permute-start(bf16[2,8,32,256]{3,2,1,0:T(8,128)(2,1)S(1)} %fusion.3.refs_2_), channel_id=1, source_target_pairs={{0,8},{4,12},{8,0},{12,4},{16,24},{20,28},{24,16},{28,20},{1,9},{5... | collective-permute-start | bytes 786440 | tf_op jit(solution)/shard_map/ppermute | solution.py:466
  76.1 12.4 %collective-permute-start.25 = (bf16[2,8,32,256]{3,2,1,0:T(8,128)(2,1)S(1)}, bf16[2,8,32,256]{3,2,1,0:T(8,128)(2,1)S(1)}, u32[]{:S(2)}, u32[]{:S(2)}) collective-permute-start(bf16[2,8,32,256]{3,2,1,0:T(8,128)(2,1)S(1)} %fusion.2.refs_3_), channel_id=1, source_target_pairs={{0,16},{4,20},{8,24},{12,28},{16,0},{20,4},{24,8},{28,12},{1,17},{... | collective-permute-start | bytes 786440 | tf_op jit(solution)/shard_map/ppermute | solution.py:466
  84.4 13.0 %collective-permute-start.21 = (bf16[128,1024]{1,0:T(8,128)(2,1)S(1)}, bf16[128,1024]{1,0:T(8,128)(2,1)S(1)}, u32[]{:S(2)}, u32[]{:S(2)}) collective-permute-start(bf16[128,1024]{1,0:T(8,128)(2,1)S(1)} %sums.3), channel_id=1, source_target_pairs={{0,3},{1,0},{2,1},{3,2},{4,7},{5,4},{6,5},{7,6},{8,11},{9,8},{10,9... | collective-permute-start | bytes 786440 | tf_op jit(solution)/shard_map/ppermute | solution.py:375
  86.9 5.0 %collective-permute-start.23 = (bf16[8,32,256]{2,1,0:T(8,128)(2,1)S(1)}, bf16[8,32,256]{2,1,0:T(8,128)(2,1)S(1)}, u32[]{:S(2)}, u32[]{:S(2)}) collective-permute-start(bf16[8,32,256]{2,1,0:T(8,128)(2,1)S(1)} %fusion.7), channel_id=1, source_target_pairs={{0,16},{4,20},{8,24},{12,28},{16,0},{20,4},{24,8},{28,12},{1,17},{... | collective-permute-start | bytes 393224 | tf_op jit(solution)/shard_map/ppermute | solution.py:466
  88.6 5.0 %collective-permute-start.26 = (bf16[8,32,256]{2,1,0:T(8,128)(2,1)S(1)}, bf16[8,32,256]{2,1,0:T(8,128)(2,1)S(1)}, u32[]{:S(2)}, u32[]{:S(2)}) collective-permute-start(bf16[8,32,256]{2,1,0:T(8,128)(2,1)S(1)} %fusion.8), channel_id=1, source_target_pairs={{0,8},{4,12},{8,0},{12,4},{16,24},{20,28},{24,16},{28,20},{1,9},{5... | collective-permute-start | bytes 393224 | tf_op jit(solution)/shard_map/ppermute | solution.py:466
  92.0 6.9 %collective-permute-start.24 = (bf16[4,32,256]{2,1,0:T(8,128)(2,1)S(1)}, bf16[4,32,256]{2,1,0:T(8,128)(2,1)S(1)}, u32[]{:S(2)}, u32[]{:S(2)}) collective-permute-start(bf16[4,32,256]{2,1,0:T(8,128)(2,1)S(1)} %slice.127), channel_id=1, source_target_pairs={{0,1},{1,2},{2,3},{3,0},{4,5},{5,6},{6,7},{7,4},{8,9},{9,10},{10,1... | collective-permute-start | bytes 196616 | tf_op jit(solution)/shard_map/ppermute | solution.py:375
  93.7 6.0 %collective-permute-start.28 = (bf16[4,32,256]{2,1,0:T(8,128)(2,1)S(1)}, bf16[4,32,256]{2,1,0:T(8,128)(2,1)S(1)}, u32[]{:S(2)}, u32[]{:S(2)}) collective-permute-start(bf16[4,32,256]{2,1,0:T(8,128)(2,1)S(1)} %get-tuple-element.50), channel_id=1, source_target_pairs={{0,3},{1,0},{2,1},{3,2},{4,7},{5,4},{6,5},{7,6},{8,11},{9,8},{10,9... | collective-permute-start | bytes 196616 | tf_op jit(solution)/shard_map/ppermute | solution.py:375
  96.0 6.5 %collective-permute-start.27 = (bf16[4,32,256]{2,1,0:T(8,128)(2,1)S(1)}, bf16[4,32,256]{2,1,0:T(8,128)(2,1)S(1)}, u32[]{:S(2)}, u32[]{:S(2)}) collective-permute-start(bf16[4,32,256]{2,1,0:T(8,128)(2,1)S(1)} %get-tuple-element.51), channel_id=1, source_target_pairs={{0,2},{1,3},{2,0},{3,1},{4,6},{5,7},{6,4},{7,5},{8,10},{9,11},{10,... | collective-permute-start | bytes 196616 | tf_op jit(solution)/shard_map/ppermute | solution.py:375
